TPU v7x, 128 devices: a whole 4x4x4 slice. The times are simulated.
128 devices in a mesh: seq: 4 (over x), exp: 32 (over y, z, core).
Axes of the slice: x: 4, y: 4, z: 4, core: 2. Of those that a mesh axis runs over, the one named last changes fastest.
Arguments:
- tokens: bfloat16 [32, 2048, 768], P('exp', 'seq'), may hold values from -64 to 64
- halt_steps: int32 [32, 2048], P('exp', 'seq'), may hold values from 0 to 4, as said below
- phi: bfloat16 [768, 1024], P(None, 'exp')
- w_up: bfloat16 [128, 768, 3072], P(('seq', 'exp')), may hold values from -0.21875 to 0.21875
- w_down: bfloat16 [128, 3072, 768], P(('seq', 'exp')), may hold values from -0.875 to 0.875
- cotangent: bfloat16 [32, 2048, 768], P('exp', 'seq'), may hold values from -6 to 6
Outputs:
- mixed: bfloat16 [32, 2048, 768], P('exp', 'seq')
- grad_tokens: bfloat16 [32, 2048, 768], P('exp', 'seq')
- grad_phi_t: float32 [1024, 768], P(('seq', 'exp'))
- grad_up: bfloat16 [128, 768, 3072], P(('seq', 'exp'))
- grad_down: bfloat16 [128, 3072, 768], P(('seq', 'exp'))
Inputs may be any that keep to these rules, and one draw needn't show every extreme that they name: `halt_steps`: every clip has a token with 4 steps.
All inputs are finite; a program needn't handle non-finite values.
Results may differ from a plain program's by a relative error of at most 0.017.
Values may be sent and summed in bfloat16 or wider, within the bound.
No kernel may reach another device: no remote copies, remote signals or barrier semaphores. Data moves between devices by JAX's collectives and lax.ppermute only.
A program may use at most 128 MiB of HBM per device.

v0:
```python
import jax
import jax.numpy as jnp
from jax import lax
from jax.sharding import PartitionSpec as P

LAYER_POS = 1


EPS = 1e-06
LOW_LOGIT = -1e30


def rms_factor(values):
    return lax.rsqrt(jnp.mean(values * values, axis=-1, keepdims=True) + EPS)


def per_device(tokens, halt_steps, phi, w_up, w_down, cotangent):
    clip_part = tokens[0]
    is_live = halt_steps[0] > LAYER_POS
    live_rows = is_live[:, None]
    features = clip_part.shape[1]
    phi_all = lax.all_gather(phi, "exp", axis=1, tiled=True)
    logits = jnp.dot(clip_part, phi_all, preferred_element_type=jnp.float32)
    slot_count = phi_all.shape[1]
    own_slots = slot_count // lax.axis_size("seq")
    first_slot = lax.axis_index("seq") * own_slots
    local_top = jnp.max(jnp.where(live_rows, logits, LOW_LOGIT), axis=0)
    slot_top = lax.pmax(local_top, "seq")
    weights = jnp.where(live_rows, jnp.exp(logits - slot_top), 0.0).astype(jnp.bfloat16)
    slot_total = lax.psum(jnp.sum(weights.astype(jnp.float32), axis=0), "seq")
    section = weights
    summed = lax.psum_scatter(
        jnp.dot(section.T, clip_part, preferred_element_type=jnp.float32),
        "seq",
        scatter_dimension=0,
        tiled=True,
    )
    own_total = lax.dynamic_slice_in_dim(slot_total, first_slot, own_slots, 0)
    mixed_in = summed / own_total[:, None]
    factor = rms_factor(mixed_in)
    normed = mixed_in * factor
    slot_in = normed.astype(jnp.bfloat16)
    groups = lax.axis_size("exp")
    per_group = own_slots // groups
    up_matrix = w_up[0]
    down_matrix = w_down[0]
    hidden_count = up_matrix.shape[1]
    section = lax.all_to_all(
        slot_in.reshape(groups, per_group, features), "exp", split_axis=0, concat_axis=0, tiled=True
    )
    block_shape = section.shape
    flat_rows = section.reshape(-1, features)
    preact = jnp.dot(flat_rows, up_matrix, preferred_element_type=jnp.float32)
    hidden = jax.nn.gelu(preact).astype(jnp.bfloat16)
    output = jnp.dot(hidden, down_matrix, preferred_element_type=jnp.float32).astype(jnp.bfloat16)
    expert_outs = output.reshape(block_shape)
    expert_ins = section
    expert_pres = preact.reshape(block_shape[0], block_shape[1], hidden_count)
    returned = lax.all_to_all(expert_outs, "exp", split_axis=0, concat_axis=0, tiled=True).reshape(
        own_slots, features
    )
    slot_out = lax.all_gather(returned, "seq", axis=0, tiled=True)
    combine = jax.nn.softmax(logits, axis=-1)
    combine_b = combine.astype(jnp.bfloat16)
    mixed = jnp.where(
        live_rows, jnp.dot(combine_b, slot_out, preferred_element_type=jnp.float32), 0.0
    ).astype(jnp.bfloat16)
    masked_grad = jnp.where(live_rows, cotangent[0], jnp.zeros((), jnp.bfloat16))
    combine_grad = jnp.dot(masked_grad, slot_out.T, preferred_element_type=jnp.float32)
    combine_logit_grad = combine * (
        combine_grad - jnp.sum(combine * combine_grad, axis=-1, keepdims=True)
    )
    section = combine_b
    slot_grad = lax.psum_scatter(
        jnp.dot(section.T, masked_grad, preferred_element_type=jnp.float32),
        "seq",
        scatter_dimension=0,
        tiled=True,
    ).astype(jnp.bfloat16)
    arrived = lax.all_to_all(
        slot_grad.reshape(groups, per_group, features),
        "exp",
        split_axis=0,
        concat_axis=0,
        tiled=True,
    ).reshape(-1, features)
    inputs_flat = expert_ins.reshape(-1, features)
    preact = expert_pres.reshape(-1, hidden_count)
    hidden = jax.nn.gelu(preact).astype(jnp.bfloat16)
    hidden_grad = jnp.dot(arrived, down_matrix.T, preferred_element_type=jnp.float32)
    grad_down = jnp.dot(hidden.T, arrived, preferred_element_type=jnp.float32).astype(jnp.bfloat16)
    pre_grad = jax.vjp(jax.nn.gelu, preact)[1](hidden_grad)[0].astype(jnp.bfloat16)
    grad_up = jnp.dot(inputs_flat.T, pre_grad, preferred_element_type=jnp.float32).astype(
        jnp.bfloat16
    )
    normed_grad = jnp.dot(pre_grad, up_matrix.T, preferred_element_type=jnp.float32).astype(
        jnp.bfloat16
    )
    back_grad = lax.all_to_all(
        normed_grad.reshape(groups, per_group, features),
        "exp",
        split_axis=0,
        concat_axis=0,
        tiled=True,
    )
    back_grad = back_grad.reshape(own_slots, features).astype(jnp.float32)
    mixed_grad = (
        factor * (back_grad - normed * jnp.mean(back_grad * normed, axis=-1, keepdims=True))
    ).astype(jnp.bfloat16)
    all_grads = lax.all_gather(mixed_grad, "seq", axis=0, tiled=True)
    dispatch_grad = jnp.dot(clip_part, all_grads.T, preferred_element_type=jnp.float32)
    dispatch_share = weights.astype(jnp.float32) / slot_total
    column_sum = lax.psum(jnp.sum(dispatch_share * dispatch_grad, axis=0), "seq")
    logit_grad = (combine_logit_grad + dispatch_share * (dispatch_grad - column_sum)).astype(
        jnp.bfloat16
    )
    share_b = dispatch_share.astype(jnp.bfloat16)
    grad_rows = (
        jnp.dot(logit_grad, phi_all.T, preferred_element_type=jnp.float32)
        + jnp.dot(share_b, all_grads, preferred_element_type=jnp.float32)
    ).astype(jnp.bfloat16)
    section = logit_grad
    grad_phi_t = lax.psum_scatter(
        jnp.dot(section.T, clip_part, preferred_element_type=jnp.float32),
        ("seq", "exp"),
        scatter_dimension=0,
        tiled=True,
    )
    return (mixed[None], grad_rows[None], grad_phi_t, grad_up[None], grad_down[None])


def solution(mesh):
    placed = (
        P("exp", "seq", None),
        P("exp", "seq"),
        P(None, "exp"),
        P(("seq", "exp"), None, None),
        P(("seq", "exp"), None, None),
        P("exp", "seq", None),
    )
    return jax.shard_map(
        per_device,
        mesh=mesh,
        in_specs=placed,
        out_specs=(
            P("exp", "seq", None),
            P("exp", "seq", None),
            P(("seq", "exp"), None),
            P(("seq", "exp"), None, None),
            P(("seq", "exp"), None, None),
        ),
        check_vma=False,
    )
```

profile of v0, /device:TPU:1, one launch (start us, length us, event | category | flops | bytes accessed | tf_op | source)
XLA Modules:
  0.0 469.3 jit_solution(2275231928255649085)
XLA Ops:
  7.2 0.7 all-gather.4.cloned.1.call-update
  8.0 0.7 compare_reduce_fusion
  8.7 48.7 %all-gather.4.cloned.1.call-done = bf16[768,1024]{0,1:T(8,128)(2,1)} async-done(((bf16[768,32]{0,1:T(8,128)(2,1)}), bf16[768,1024]{0,1:T(8,128)(2,1)}) %all-gather.4.cloned.1.call-update) | async-done | bytes 1572880 | tf_op jit(solution)/shard_map/all_gather | solution.py:22
  57.4 2.5 fusion.64
  59.9 0.6 fusion.24
  60.5 8.4 %pmax.7 = f32[1024]{0:T(1024)S(1)} all-reduce(f32[1024]{0:T(1024)S(1)} %get-tuple-element.6), channel_id=1, replica_groups=mesh['seq'=4,'exp'=32] {'seq'}, use_global_device_ids=true, to_apply=%region_3.4 | all-reduce | flops 1024 | bytes 8192 | tf_op jit(solution)/shard_map/pmax | solution.py:28
  68.9 0.4 convert_reduce_fusion
  69.3 1.0 copy-done.1
  70.3 2.7 fusion.47
  73.0 0.0 reduce-scatter.6.cloned.1.call-start
  73.0 4.0 fusion.51
  77.1 6.0 %psum.14 = f32[1024]{0:T(1024)S(1)} all-reduce(f32[1024]{0:T(1024)S(1)} %get-tuple-element.7), channel_id=1, replica_groups=mesh['seq'=4,'exp'=32] {'seq'}, use_global_device_ids=true, to_apply=%region_6.7 | all-reduce | flops 1024 | bytes 8192 | tf_op jit(solution)/shard_map/psum | solution.py:30
  83.1 0.1 dynamic_slice.3
  83.1 27.0 %reduce-scatter.4.cloned.1.call-done = f32[256,768]{1,0:T(8,128)} async-done(((f32[1024,768]{1,0:T(8,128)}), f32[256,768]{1,0:T(8,128)}) %reduce-scatter.4.cloned.1.call-update) | async-done | bytes 786448 | tf_op jit(solution)/shard_map/reduce_scatter | solution.py:32
  110.1 1.4 multiply_reduce_fusion.1
  111.5 2.0 fusion.54
  113.5 7.6 %all-to-all-start = ((bf16[32,8,768]{2,1,0:T(8,128)(2,1)}), bf16[32,8,768]{2,1,0:T(8,128)(2,1)S(1)}, u32[]{:S(2)}, u32[]{:S(2)}) async-start(bf16[32,8,768]{2,1,0:T(8,128)(2,1)} %fusion.54), calls=%async_computation.1 | async-start | bytes 786432 | tf_op jit(solution)/shard_map/all_to_all | solution.py:48
  121.2 29.9 %reduce-scatter.6.cloned.1.call-done = f32[256,768]{1,0:T(8,128)} async-done(((f32[1024,768]{1,0:T(8,128)}), f32[256,768]{1,0:T(8,128)}) %reduce-scatter.6.cloned.1.call-update) | async-done | bytes 786448 | tf_op jit(solution)/shard_map/reduce_scatter | solution.py:74
  151.0 1.9 convert_bitcast_fusion
  152.9 7.7 %all-to-all-start.2 = ((bf16[32,8,768]{2,1,0:T(8,128)(2,1)}), bf16[32,8,768]{2,1,0:T(8,128)(2,1)}, u32[]{:S(2)}, u32[]{:S(2)}) async-start(bf16[32,8,768]{2,1,0:T(8,128)(2,1)} %convert_bitcast_fusion), calls=%async_computation.4 | async-start | bytes 786432 | tf_op jit(solution)/shard_map/all_to_all | solution.py:80
  160.7 0.0 all-gather.8.cloned.1.call-start
  160.7 5.4 %fusion.6 = f32[256,3072]{1,0:T(8,128)} fusion(bf16[1,768,3072]{2,1,0:T(8,128)(2,1)} %param.9, bf16[32,8,768]{2,1,0:T(8,128)(2,1)S(1)} %all-to-all-done), kind=kOutput, calls=%fused_computation.8 | convolution fusion | flops 1207959552 | bytes 8257536 | tf_op jit(solution)/shard_map/dot_general | solution.py:53
  166.1 4.9 %all-to-all-done.2 = bf16[32,8,768]{2,1,0:T(8,128)(2,1)} async-done(((bf16[32,8,768]{2,1,0:T(8,128)(2,1)}), bf16[32,8,768]{2,1,0:T(8,128)(2,1)}, u32[]{:S(2)}, u32[]{:S(2)}) %all-to-all-start.2) | async-done | bytes 393248 | tf_op jit(solution)/shard_map/all_to_all | solution.py:80
  171.0 6.1 %fusion.16 = bf16[256,3072]{1,0:T(8,128)(2,1)S(1)} fusion(f32[256,3072]{1,0:T(8,128)} %fusion.6, bf16[1,3072,768]{2,1,0:T(8,128)(2,1)} %param.10, bf16[32,8,768]{2,1,0:T(8,128)(2,1)} %all-to-all-done.2), kind=kOutput, calls=%fused_computation.20 | convolution fusion | flops 1223688192 | bytes 9830400 | tf_op jit(solution)/shard_map/dot_general | solution.py:90
  177.1 4.3 fusion.36
  181.5 13.6 %all_to_all.20 = bf16[32,8,768]{2,1,0:T(8,128)(2,1)S(1)} all-to-all(bf16[32,8,768]{2,1,0:T(8,128)(2,1)S(1)} %fusion.36), channel_id=1, replica_groups=mesh['seq'=4,'exp'=32] {'exp'}, dimensions={0} | all-to-all | bytes 786432 | tf_op jit(solution)/shard_map/all_to_all | solution.py:99
  195.1 0.3 fusion.40
  195.4 1.0 fusion.42
  196.5 0.2 all-gather.6.cloned.1.call-start
  196.7 5.2 %fusion.33 = bf16[32,8,768]{2,1,0:T(8,128)(2,1)S(1)} fusion(bf16[1,3072,768]{2,1,0:T(8,128)(2,1)} %param.10, f32[256,3072]{1,0:T(8,128)} %fusion.6), kind=kOutput, calls=%fused_computation.42 | convolution fusion | flops 1215234048 | bytes 8257536 | tf_op jit(solution)/shard_map/dot_general | solution.py:55
  201.9 13.7 %all_to_all.21 = bf16[32,8,768]{2,1,0:T(8,128)(2,1)} all-to-all(bf16[32,8,768]{2,1,0:T(8,128)(2,1)S(1)} %fusion.33), channel_id=1, replica_groups=mesh['seq'=4,'exp'=32] {'exp'}, dimensions={0} | all-to-all | bytes 786432 | tf_op jit(solution)/shard_map/all_to_all | solution.py:59
  215.7 0.0 reduce-scatter.8.cloned.1.call-start
  215.8 2.9 all-gather.8.cloned.1.call-done
  218.7 4.0 fusion.19
  222.7 7.0 %psum.15 = f32[1024]{0:T(1024)S(1)} all-reduce(f32[1024]{0:T(1024)S(1)} %get-tuple-element.11), channel_id=1, replica_groups=mesh['seq'=4,'exp'=32] {'seq'}, use_global_device_ids=true, to_apply=%region_12.13 | all-reduce | flops 1024 | bytes 8192 | tf_op jit(solution)/shard_map/psum | solution.py:113
  229.7 17.1 %all-gather.6.cloned.1.call-done = bf16[1024,768]{1,0:T(8,128)(2,1)} async-done(((bf16[256,768]{1,0:T(8,128)(2,1)}), bf16[1024,768]{1,0:T(8,128)(2,1)}) %all-gather.6.cloned.1.call-update) | async-done | bytes 1572880 | tf_op jit(solution)/shard_map/all_gather | solution.py:62
  246.8 2.9 multiply_reduce_fusion
  249.8 0.9 fusion.22
  250.7 1.0 copy-done.5
  251.6 2.7 fusion.43
  254.4 5.2 %fusion.8 = bf16[1,768,3072]{2,1,0:T(8,128)(2,1)} fusion(bf16[256,3072]{1,0:T(8,128)(2,1)} %copy-done.8, bf16[32,8,768]{2,1,0:T(8,128)(2,1)S(1)} %all-to-all-done), kind=kOutput, calls=%fused_computation.12 | convolution fusion | flops 1210318848 | bytes 6684672 | tf_op jit(solution)/shard_map/dot_general | solution.py:93
  259.5 5.6 %fusion.9 = bf16[1,3072,768]{2,1,0:T(8,128)(2,1)} fusion(bf16[32,8,768]{2,1,0:T(8,128)(2,1)} %all-to-all-done.2, f32[256,3072]{1,0:T(8,128)S(1)} %copy-done.12), kind=kOutput, calls=%fused_computation.13 | convolution fusion | flops 1217396736 | bytes 8257536 | tf_op jit(solution)/shard_map/dot_general | solution.py:91
  265.1 1.0 fusion.65
  266.1 0.2 copy-done.3
  266.4 0.5 copy-done.10
  266.9 1.9 fusion.25
  268.8 2.0 fusion.26
  270.7 191.7 %reduce-scatter.8.cloned.1.call-done = f32[8,768]{1,0:T(8,128)} async-done(((f32[1024,768]{1,0:T(8,128)}), f32[8,768]{1,0:T(8,128)}) %reduce-scatter.8.cloned.1.call-update) | async-done | bytes 24592 | tf_op jit(solution)/shard_map/reduce_scatter | solution.py:123
  (32 shorter events, 0.2 us)
Async XLA Ops:
  7.2 50.2 %copy-start = (bf16[1,512,768]{2,1,0:T(8,128)(2,1)S(1)}, bf16[1,512,768]{2,1,0:T(8,128)(2,1)}, u32[]{:S(2)}) copy-start(bf16[1,512,768]{2,1,0:T(8,128)(2,1)} %param.6) | copy-start | bytes 2359300
  7.2 50.2 %all-gather.4.cloned.1.call-start = ((), (), s32[]{:S(2)}) async-start(), calls=%async_computation.7 | async-start | bytes 1622016 | tf_op jit(solution)/shard_map/all_gather | solution.py:22
  7.9 102.2 %reduce-scatter.4.cloned.1.call-start = ((), (), s32[]{:S(2)}) async-start(), calls=%async_computation.8 | async-start | bytes 3932160 | tf_op jit(solution)/shard_map/reduce_scatter | solution.py:32
  69.3 1.0 copy-start.1
  73.0 78.0 %reduce-scatter.6.cloned.1.call-start = ((), (), s32[]{:S(2)}) async-start(), calls=%async_computation.10 | async-start | bytes 3932160 | tf_op jit(solution)/shard_map/reduce_scatter | solution.py:74
  113.5 39.4 %all-to-all-start = ((bf16[32,8,768]{2,1,0:T(8,128)(2,1)}), bf16[32,8,768]{2,1,0:T(8,128)(2,1)S(1)}, u32[]{:S(2)}, u32[]{:S(2)}) async-start(bf16[32,8,768]{2,1,0:T(8,128)(2,1)} %fusion.54), calls=%async_computation.1 | async-start | bytes 786432 | tf_op jit(solution)/shard_map/all_to_all | solution.py:48
  152.9 18.1 %all-to-all-start.2 = ((bf16[32,8,768]{2,1,0:T(8,128)(2,1)}), bf16[32,8,768]{2,1,0:T(8,128)(2,1)}, u32[]{:S(2)}, u32[]{:S(2)}) async-start(bf16[32,8,768]{2,1,0:T(8,128)(2,1)} %convert_bitcast_fusion), calls=%async_computation.4 | async-start | bytes 786432 | tf_op jit(solution)/shard_map/all_to_all | solution.py:80
  160.7 58.0 %all-gather.8.cloned.1.call-start = ((), (), s32[]{:S(2)}) async-start(), calls=%async_computation.11 | async-start | bytes 1966080 | tf_op jit(solution)/shard_map/all_gather | solution.py:110
  177.1 4.4 copy-start.8
  177.1 18.0 %copy-start.4 = (f32[256,768]{1,0:T(8,128)S(1)}, f32[256,768]{1,0:T(8,128)}, u32[]{:S(2)}) copy-start(f32[256,768]{1,0:T(8,128)} %reduce-scatter.4.cloned.1.call-done) | copy-start | bytes 2359300
  196.5 50.4 %all-gather.6.cloned.1.call-start = ((), (), s32[]{:S(2)}) async-start(), calls=%async_computation.9 | async-start | bytes 1966080 | tf_op jit(solution)/shard_map/all_gather | solution.py:62
  215.7 246.7 %reduce-scatter.8.cloned.1.call-start = ((), (), s32[]{:S(2)}) async-start(), calls=%async_computation.12 | async-start | bytes 3170304 | tf_op jit(solution)/shard_map/reduce_scatter | solution.py:123
  246.8 2.9 copy-start.2
  246.8 2.9 copy-start.7
  250.7 1.0 copy-start.5
  254.3 5.2 %copy-start.12 = (f32[256,3072]{1,0:T(8,128)S(1)}, f32[256,3072]{1,0:T(8,128)}, u32[]{:S(2)}) copy-start(f32[256,3072]{1,0:T(8,128)} %fusion.6) | copy-start | bytes 9437188
  259.5 5.6 %copy-start.6 = (bf16[512,1024]{1,0:T(8,128)(2,1)S(1)}, bf16[512,1024]{1,0:T(8,128)(2,1)}, u32[]{:S(2)}) copy-start(bf16[512,1024]{1,0:T(8,128)(2,1)} %copy-done.5) | copy-start | bytes 3145732
  259.5 5.6 %copy-start.9 = (bf16[768,1024]{0,1:T(8,128)(2,1)S(1)}, bf16[768,1024]{0,1:T(8,128)(2,1)}, u32[]{:S(2)}) copy-start(bf16[768,1024]{0,1:T(8,128)(2,1)} %all-gather.4.cloned.1.call-done) | copy-start | bytes 4718596
  265.1 1.2 copy-start.3
  265.1 1.7 copy-start.10
  266.9 1.9 copy-start.11
Sparse Core Ops, SparseCore 0:
  10.3 47.0 all-gather.3
  73.1 36.9 reduce-scatter.3
  113.1 37.8 reduce-scatter.5
  196.6 22.0 all-gather.7
  220.2 26.5 all-gather.5
  254.5 207.9 reduce-scatter.7
where the time goes:
time: 471 us; the launch traced here: 469 us
  waiting for transfers between devices  323 us (69%)
  matrix products  55.5 us (12%)
  blocking collectives  48.8 us (10%)
  starting transfers between devices  15.7 us (3%)
  between operations  14.3 us (3%)
  other arithmetic  9.22 us (2%)
    reduce_scatter x2, waiting for transfers between devices, per_device(): lax.psum_scatter(jnp.dot(section.T, clip_part, preferred_element_type=jnp...  219 us
    all_gather x1, waiting for transfers between devices, per_device(): phi_all = lax.all_gather(phi, 'exp', axis=1, tiled=True)  48.7 us
    reduce_scatter x1, waiting for transfers between devices, per_device(): lax.psum_scatter(jnp.dot(section.T, masked_grad, preferred_element_type=j...  29.9 us
    all_gather x1, waiting for transfers between devices, per_device(): slot_out = lax.all_gather(returned, 'seq', axis=0, tiled=True)  17.1 us
    all_to_all x1, blocking collectives, per_device(): lax.all_to_all(expert_outs, 'exp', split_axis=0, concat_axis=0, tiled=True)  13.7 us
    all_to_all x1, blocking collectives, per_device(): lax.all_to_all(normed_grad.reshape(groups, per_group, features), 'exp', s...  13.6 us
  transfers between devices with their start and end apart: 8, of which 7 were waited for; matrix products, arithmetic and copies ran while one was open for 9% of the time, Pallas kernels for 0%

commit v1 on v0

v1 whole, which is shorter than its diff:
```python
import jax
import jax.numpy as jnp
from jax import lax
from jax.sharding import Mesh, PartitionSpec as P

LAYER_POS = 1
EPS = 1e-06
LOW_LOGIT = -1e30

PLANE = ("y", "z")
GROUP = ("y", "z", "core")
CHIPS = ("x", "y", "z")
F32 = jnp.float32
BF16 = jnp.bfloat16


def matmul(a, b, contract):
    return lax.dot_general(a, b, ((contract[:1], contract[1:]), ((), ())), preferred_element_type=F32)


def swap_cores(values):
    return lax.ppermute(values, "core", [(0, 1), (1, 0)])


def along_x(values, steps):
    n = lax.axis_size("x")
    return lax.ppermute(values, "x", [(i, (i + steps) % n) for i in range(n)])


def gather_x(values):
    return [values] + [along_x(values, -k) for k in range(1, lax.axis_size("x"))]


def scatter_x(blocks):
    return [blocks[0]] + [along_x(blocks[k], k) for k in range(1, lax.axis_size("x"))]


def exchange(values, axes):
    return lax.all_to_all(values, axes, 0, 0, tiled=True)


def roll_blocks(blocks, first):
    return lax.dynamic_slice_in_dim(jnp.concatenate([blocks, blocks[:-1]]), first, blocks.shape[0], 0)


def after(values, *others):
    return lax.optimization_barrier((values,) + others)[0]


def gather_phi(phi):
    rows = phi.T
    planes = lax.axis_size("x")
    chips = lax.axis_size("y") * lax.axis_size("z")
    mine = exchange(jnp.broadcast_to(rows[None], (chips,) + rows.shape), PLANE)
    other = swap_cores(mine)
    first = lax.axis_index("core") == 0
    both = jnp.stack([jnp.where(first, mine, other), jnp.where(first, other, mine)], axis=1)
    groups = both.reshape(planes, -1, rows.shape[1])
    return roll_blocks(groups, lax.axis_index("x"))


def per_device(tokens, halt_steps, phi, w_up, w_down, cotangent):
    clip_part = tokens[0]
    features = clip_part.shape[1]
    live_rows = (halt_steps[0] > LAYER_POS)[:, None]
    planes = lax.axis_size("x")
    experts = lax.axis_size("y") * lax.axis_size("z") * lax.axis_size("core")
    here = lax.axis_index("x")

    phi_groups = gather_phi(phi)
    own_slots = phi_groups.shape[1]
    per_expert = own_slots // experts
    phi_all = phi_groups.reshape(-1, features)
    logits = matmul(clip_part, phi_all, (1, 1))

    def group(values, k):
        return values[..., k * own_slots : (k + 1) * own_slots]

    local_top = jnp.max(jnp.where(live_rows, logits, LOW_LOGIT), axis=0)
    weights = jnp.where(live_rows, jnp.exp(logits - local_top), 0.0).astype(BF16)
    local_total = jnp.sum(weights.astype(F32), axis=0)
    part_sums = matmul(weights, clip_part, (0, 0)).astype(BF16).reshape(planes, own_slots, features)
    arrived_sums = scatter_x(part_sums)
    stats = jnp.stack([local_top, local_total])
    all_stats = jnp.stack([jnp.roll(s, k * own_slots, axis=1) for k, s in enumerate(gather_x(stats))])
    slot_top = jnp.max(all_stats[:, 0], axis=0)
    scales = jnp.exp(all_stats[:, 0] - slot_top)
    slot_total = jnp.sum(all_stats[:, 1] * scales, axis=0)
    share_scale = scales[0] / slot_total
    own_scales = group(scales / slot_total, 0)
    mixed_in = sum(
        arrived_sums[k].astype(F32) * own_scales[(planes - k) % planes][:, None] for k in range(planes)
    )
    factor = lax.rsqrt(jnp.mean(mixed_in * mixed_in, axis=-1, keepdims=True) + EPS)
    normed = mixed_in * factor
    slot_in = normed.astype(BF16)
    expert_in = exchange(slot_in.reshape(experts, per_expert, features), GROUP).reshape(-1, features)

    combine = jax.nn.softmax(logits, axis=-1)
    combine_b = combine.astype(BF16)
    masked_grad = jnp.where(live_rows, cotangent[0], jnp.zeros((), BF16))
    part_grads = matmul(combine_b, masked_grad, (0, 0)).astype(BF16).reshape(planes, own_slots, features)
    part_grads = after(part_grads, *arrived_sums)
    slot_grad = sum(g.astype(F32) for g in scatter_x(part_grads)).astype(BF16)
    expert_grad = exchange(slot_grad.reshape(experts, per_expert, features), GROUP).reshape(-1, features)

    up_matrix, down_matrix = w_up[0], w_down[0]
    preact = matmul(expert_in, up_matrix, (1, 0))
    hidden = jax.nn.gelu(preact).astype(BF16)
    output = matmul(hidden, down_matrix, (1, 0)).astype(BF16)
    own_out = exchange(output.reshape(experts, per_expert, features), GROUP).reshape(own_slots, features)

    hidden_grad = matmul(expert_grad, down_matrix, (1, 1))
    pre_grad = jax.vjp(jax.nn.gelu, preact)[1](hidden_grad)[0].astype(BF16)
    normed_grad = matmul(pre_grad, up_matrix, (1, 1)).astype(BF16)
    back_grad = exchange(normed_grad.reshape(experts, per_expert, features), GROUP)
    grad_down = matmul(hidden, expert_grad, (0, 0)).astype(BF16)
    grad_up = matmul(expert_in, pre_grad, (0, 0)).astype(BF16)

    slot_outs = gather_x(own_out)
    mixed = sum(matmul(group(combine_b, k), slot_outs[k], (1, 0)) for k in range(planes))
    mixed = jnp.where(live_rows, mixed, 0.0).astype(BF16)
    combine_grads = [matmul(masked_grad, block, (1, 1)) for block in slot_outs]
    row_sum = sum(
        jnp.sum(group(combine, k) * combine_grads[k], axis=-1, keepdims=True) for k in range(planes)
    )

    back_grad = back_grad.reshape(own_slots, features).astype(F32)
    mixed_grad = (
        factor * (back_grad - normed * jnp.mean(back_grad * normed, axis=-1, keepdims=True))
    ).astype(BF16)
    own_column = jnp.sum(mixed_in * mixed_grad.astype(F32), axis=-1)
    all_grads = gather_x(mixed_grad)
    column_sums = gather_x(own_column)
    part_phi, shares, logit_grads = [], [], []
    for k in range(planes):
        dispatch_grad = matmul(clip_part, all_grads[k], (1, 1))
        dispatch_share = group(weights, k).astype(F32) * group(share_scale, k)
        logit_grad = (
            group(combine, k) * (combine_grads[k] - row_sum)
            + dispatch_share * (dispatch_grad - column_sums[k])
        ).astype(BF16)
        part_phi.append(matmul(logit_grad, clip_part, (0, 0)).astype(BF16))
        shares.append(dispatch_share.astype(BF16))
        logit_grads.append(logit_grad)

    halves = jnp.stack(part_phi).reshape(planes, -1, 2, per_expert, features)
    halves = roll_blocks(halves, lax.rem(planes - here, planes)).reshape((-1,) + halves.shape[2:])
    first = lax.axis_index("core") == 0
    keep = jnp.where(first, halves[:, 0], halves[:, 1])
    give = jnp.where(first, halves[:, 1], halves[:, 0])
    chip_sum = (keep.astype(F32) + swap_cores(give).astype(F32)).astype(BF16)
    grad_phi_t = jnp.sum(exchange(chip_sum, CHIPS).astype(F32), axis=0)

    logit_grads = after(tuple(logit_grads), chip_sum)
    grad_rows = sum(
        matmul(g, p, (1, 0)) + matmul(s, a, (1, 0))
        for g, p, s, a in zip(logit_grads, phi_groups, shares, all_grads)
    )
    return (mixed[None], grad_rows.astype(BF16)[None], grad_phi_t, grad_up[None], grad_down[None])


def solution(mesh):
    fine = Mesh(mesh.devices.reshape(4, 4, 4, 2), ("x", "y", "z", "core"))
    rows = P(GROUP, "x", None)
    blocks = P(("x",) + GROUP, None, None)
    return jax.shard_map(
        per_device,
        mesh=fine,
        in_specs=(rows, P(GROUP, "x"), P(None, GROUP), blocks, blocks, rows),
        out_specs=(rows, rows, P(("x",) + GROUP, None), blocks, blocks),
        check_vma=False,
    )
```

time: 471 us -> 201 us (0.43)
  waiting for transfers between devices: 323 us -> 40.6 us
  starting transfers between devices: 15.7 us -> 52.7 us
  blocking collectives: 48.8 us -> 21.8 us
  between operations: 14.3 us -> 1.41 us
  matrix products: 55.5 us -> 65.3 us
    reduce_scatter x3 -> x0, waiting for transfers between devices: 249 us -> none  [the longest x2 219 us: per_device(): lax.psum_scatter(jnp.dot(section.T, clip_part, preferred_element_type=jnp...]
    all_gather x3 -> x0, waiting for transfers between devices: 68.7 us -> none  [the longest x1 48.7 us: per_device(): phi_all = lax.all_gather(phi, 'exp', axis=1, tiled=True)]
    ppermute x0 -> x20, starting transfers between devices: none -> 25.6 us  [the longest x18 21.2 us: along_x(): return lax.ppermute(values, 'x', [(i, (i + steps) % n) for i in range(n)])]
    ppermute x0 -> x20, waiting for transfers between devices: none -> 18.1 us  [the longest x18 16.3 us: along_x(): return lax.ppermute(values, 'x', [(i, (i + steps) % n) for i in range(n)])]
    all_to_all x2 -> x5, waiting for transfers between devices: 4.92 us -> 22.4 us  [exchange(): return lax.all_to_all(values, axes, 0, 0, tiled=True)]
    psum x2 -> x0, blocking collectives: 13 us -> none  [the longest x1 7.01 us: per_device(): lax.psum(jnp.sum(dispatch_share * dispatch_grad, axis=0), 'seq')]
    all_to_all x2 -> x5, starting transfers between devices: 15.3 us -> 27.1 us  [exchange(): return lax.all_to_all(values, axes, 0, 0, tiled=True)]
    dot_general x15 -> x33, matrix products: 55.5 us -> 65.3 us  [matmul(): lax.dot_general(a, b, ((contract[:1], contract[1:]), ((), ())), preferred...]
  transfers between devices with their start and end apart: 8 -> 25, of which waited for: 7 -> 11; matrix products, arithmetic and copies ran while one was open for 9% -> 35% of each run, Pallas kernels for 0% -> 0%
where the time goes in v1:
time: 201 us; the launch traced here: 199 us
  matrix products  65.3 us (32%)
  starting transfers between devices  52.7 us (26%)
  waiting for transfers between devices  40.6 us (20%)
  blocking collectives  21.8 us (11%)
  other arithmetic  10.7 us (5%)
  local copies, waits for them, and re-layouts  6.83 us (3%)
    dot_general x33, matrix products, matmul(): lax.dot_general(a, b, ((contract[:1], contract[1:]), ((), ())), preferred...  65.3 us
    all_to_all x5, starting transfers between devices, exchange(): return lax.all_to_all(values, axes, 0, 0, tiled=True)  27.1 us
    all_to_all x5, waiting for transfers between devices, exchange(): return lax.all_to_all(values, axes, 0, 0, tiled=True)  22.4 us
    all_to_all x1, blocking collectives, exchange(): return lax.all_to_all(values, axes, 0, 0, tiled=True)  21.8 us
    ppermute x18, starting transfers between devices, along_x(): return lax.ppermute(values, 'x', [(i, (i + steps) % n) for i in range(n)])  21.2 us
    ppermute x18, waiting for transfers between devices, along_x(): return lax.ppermute(values, 'x', [(i, (i + steps) % n) for i in range(n)])  16.3 us
    unnamed x54, local copies, waits for them, and re-layouts  4.53 us
    ppermute x2, starting transfers between devices, swap_cores(): return lax.ppermute(values, 'core', [(0, 1), (1, 0)])  4.46 us
  transfers between devices with their start and end apart: 25, of which 11 were waited for; matrix products, arithmetic and copies ran while one was open for 35% of the time, Pallas kernels for 0%

profile of v1, /device:TPU:1, one launch (start us, length us, event | category | flops | bytes accessed | tf_op | source)
XLA Modules:
  0.0 199.2 jit_solution(12053310265773436425)
XLA Ops:
  1.6 21.8 %all_to_all.30 = bf16[16,32,768]{2,1,0:T(8,128)(2,1)S(1)} all-to-all(bf16[16,32,768]{2,1,0:T(8,128)(2,1)S(1)} %broadcast_in_dim.85), channel_id=1, replica_groups=mesh['x'=4,'y'=4,'z'=4,'core'=2] {'y','z'}, dimensions={0} | all-to-all | bytes 1572864 | tf_op jit(solution)/shard_map/all_to_all | solution.py:39
  23.4 1.7 collective-permute-start
  25.1 1.9 collective-permute-done
  30.2 1.3 collective-permute-start.3
  31.5 2.5 %collective-permute-start.2 = (f32[2,1024]{1,0:T(2,128)S(1)}, f32[2,1024]{1,0:T(2,128)S(1)}, u32[]{:S(2)}, u32[]{:S(2)}) collective-permute-start(f32[2,1024]{1,0:T(2,128)S(1)} %get-tuple-element.44), channel_id=1, source_target_pairs={{0,64},{32,96},{64,0},{96,32},{1,65},{33,97},{65,1},{97,33},{2,66}... | collective-permute-start | bytes 24584 | tf_op jit(solution)/shard_map/ppermute | solution.py:27
  34.0 1.2 collective-permute-start.1
  36.5 2.1 %fusion.128 = (bf16[512,1024]{0,1:T(8,128)(2,1)}, f32[512,1024]{0,1:T(8,128)}) fusion(f32[512]{0:T(512)S(1)} %get-tuple-element.19, f32[1024,512]{1,0:T(8,128)S(1)} %get-tuple-element.52, f32[512]{0:T(512)S(1)} %get-tuple-element.51), kind=kLoop, calls=%fused_computation.185 | loop fusion | flops 1572864 | bytes 5246976 | tf_op jit(solution)/shard_map/convert_element_type | solution.py:100
  38.6 2.5 %collective-permute-start.6 = (bf16[256,768]{1,0:T(8,128)(2,1)S(1)}, bf16[256,768]{1,0:T(8,128)(2,1)S(1)}, u32[]{:S(2)}, u32[]{:S(2)}) collective-permute-start(bf16[256,768]{1,0:T(8,128)(2,1)S(1)} %get-tuple-element.35), channel_id=1, source_target_pairs={{0,96},{32,0},{64,32},{96,64},{1,97},{33,1},{65,33},{97,65},{2,98}... | collective-permute-start | bytes 1179656 | tf_op jit(solution)/shard_map/ppermute | solution.py:27
  41.4 12.5 %collective-permute-done.6 = bf16[256,768]{1,0:T(8,128)(2,1)S(1)} collective-permute-done((bf16[256,768]{1,0:T(8,128)(2,1)S(1)}, bf16[256,768]{1,0:T(8,128)(2,1)S(1)}, u32[]{:S(2)}, u32[]{:S(2)}) %collective-permute-start.6) | collective-permute-done | bytes 393248 | tf_op jit(solution)/shard_map/ppermute | solution.py:27
  53.9 3.3 %collective-permute-done.4 = bf16[256,768]{1,0:T(8,128)(2,1)S(1)} collective-permute-done((bf16[256,768]{1,0:T(8,128)(2,1)S(1)}, bf16[256,768]{1,0:T(8,128)(2,1)S(1)}, u32[]{:S(2)}, u32[]{:S(2)}) %collective-permute-start.4) | collective-permute-done | bytes 393248 | tf_op jit(solution)/shard_map/ppermute | solution.py:27
  58.7 4.2 %all-to-all-start.1 = ((bf16[32,8,768]{2,1,0:T(8,128)(2,1)}), bf16[32,8,768]{2,1,0:T(8,128)(2,1)S(1)}, u32[]{:S(2)}, u32[]{:S(2)}) async-start(bf16[32,8,768]{2,1,0:T(8,128)(2,1)} %fusion.74), calls=%async_computation.1 | async-start | bytes 786432 | tf_op jit(solution)/shard_map/all_to_all | solution.py:39
  62.9 2.5 %convolution_convert_fusion.2 = bf16[1024,768]{1,0:T(8,128)(2,1)S(1)} fusion(bf16[512,1024]{0,1:T(8,128)(2,1)} %get-tuple-element.23, bf16[1,512,768]{2,1,0:T(8,128)(2,1)} %param.11, pred[512]{0:T(512)(128)(4,1)S(1)} %compare_reduce_fusion), kind=kOutput, calls=%fused_computation.33 | convolution fusion | flops 806486016 | bytes 3408384 | tf_op jit(solution)/shard_map/dot_general | solution.py:18
  66.9 1.8 collective-permute-start.11
  68.7 4.5 %all-to-all-done.1 = bf16[32,8,768]{2,1,0:T(8,128)(2,1)S(1)} async-done(((bf16[32,8,768]{2,1,0:T(8,128)(2,1)}), bf16[32,8,768]{2,1,0:T(8,128)(2,1)S(1)}, u32[]{:S(2)}, u32[]{:S(2)}) %all-to-all-start.1) | async-done | bytes 393248 | tf_op jit(solution)/shard_map/all_to_all | solution.py:39
  73.2 3.7 %fusion.6 = f32[256,3072]{1,0:T(8,128)S(1)} fusion(bf16[1,768,3072]{2,1,0:T(8,128)(2,1)} %param.9, bf16[32,8,768]{2,1,0:T(8,128)(2,1)S(1)} %all-to-all-done.1), kind=kOutput, calls=%fused_computation.8 | convolution fusion | flops 1207959552 | bytes 8257536 | tf_op jit(solution)/shard_map/dot_general | solution.py:18
  76.9 1.7 copy-done.22
  78.6 5.1 %fusion.38 = bf16[32,8,768]{2,1,0:T(8,128)(2,1)} fusion(bf16[1,3072,768]{2,1,0:T(8,128)(2,1)} %param.10, f32[256,3072]{1,0:T(8,128)S(1)} %fusion.6), kind=kOutput, calls=%fused_computation.62 | convolution fusion | flops 1215234048 | bytes 8257536 | tf_op jit(solution)/shard_map/dot_general | solution.py:18
  83.7 4.4 %all-to-all-start.2 = ((bf16[32,8,768]{2,1,0:T(8,128)(2,1)}), bf16[32,8,768]{2,1,0:T(8,128)(2,1)}, u32[]{:S(2)}, u32[]{:S(2)}) async-start(bf16[32,8,768]{2,1,0:T(8,128)(2,1)} %fusion.38), calls=%async_computation.2 | async-start | bytes 786432 | tf_op jit(solution)/shard_map/all_to_all | solution.py:39
  88.2 2.3 %fusion.75 = bf16[32,8,768]{2,1,0:T(8,128)(2,1)} fusion(bf16[256,768]{1,0:T(8,128)(2,1)} %collective-permute-done.12, bf16[256,768]{1,0:T(8,128)(2,1)} %collective-permute-done.11, bf16[256,768]{1,0:T(8,128)(2,1)} %collective-permute-done.10, bf16[4,256,768]{2,1,0:T(8,128)(2,1)} %bitcast.259), kind=kLoop, calls=%fused_computation.117 | loop fusion | flops 1572864 | bytes 1966080 | tf_op jit(solution)/shard_map/reshape | solution.py:105
  90.4 7.7 %all-to-all-done.2 = bf16[32,8,768]{2,1,0:T(8,128)(2,1)} async-done(((bf16[32,8,768]{2,1,0:T(8,128)(2,1)}), bf16[32,8,768]{2,1,0:T(8,128)(2,1)}, u32[]{:S(2)}, u32[]{:S(2)}) %all-to-all-start.2) | async-done | bytes 393248 | tf_op jit(solution)/shard_map/all_to_all | solution.py:39
  98.2 3.7 %all-to-all-start.3 = ((bf16[32,8,768]{2,1,0:T(8,128)(2,1)}), bf16[32,8,768]{2,1,0:T(8,128)(2,1)S(1)}, u32[]{:S(2)}, u32[]{:S(2)}) async-start(bf16[32,8,768]{2,1,0:T(8,128)(2,1)} %fusion.75), calls=%async_computation.3 | async-start | bytes 786432 | tf_op jit(solution)/shard_map/all_to_all | solution.py:39
  101.9 2.6 %collective-permute-start.8 = (bf16[256,768]{1,0:T(8,128)(2,1)}, bf16[256,768]{1,0:T(8,128)(2,1)}, u32[]{:S(2)}, u32[]{:S(2)}) collective-permute-start(bf16[256,768]{1,0:T(8,128)(2,1)} %bitcast.26), channel_id=1, source_target_pairs={{0,64},{32,96},{64,0},{96,32},{1,65},{33,97},{65,1},{97,33},{2,66}... | collective-permute-start | bytes 1179656 | tf_op jit(solution)/shard_map/ppermute | solution.py:27
  105.9 2.5 %fusion.55 = f32[512,256]{0,1:T(8,128)} fusion(bf16[1,512,768]{2,1,0:T(8,128)(2,1)} %param.11, pred[512]{0:T(512)(128)(4,1)S(1)} %compare_reduce_fusion, bf16[32,8,768]{2,1,0:T(8,128)(2,1)} %all-to-all-done.2), kind=kOutput, calls=%fused_computation.80 | convolution fusion | flops 201719808 | bytes 1704448 | tf_op jit(solution)/shard_map/dot_general | solution.py:18
  108.4 2.7 %fusion.101 = f32[512,768]{1,0:T(8,128)} fusion(bf16[512,1024]{0,1:T(8,128)(2,1)} %get-tuple-element.23, bf16[32,8,768]{2,1,0:T(8,128)(2,1)} %all-to-all-done.2), kind=kOutput, calls=%fused_computation.144 | convolution fusion | flops 201326592 | bytes 2228224 | tf_op jit(solution)/shard_map/dot_general | solution.py:18
  112.0 6.7 %fusion.16 = bf16[256,3072]{1,0:T(8,128)(2,1)S(1)} fusion(f32[256,3072]{1,0:T(8,128)} %copy-done.22, bf16[1,3072,768]{2,1,0:T(8,128)(2,1)} %param.10, bf16[32,8,768]{2,1,0:T(8,128)(2,1)S(1)} %all-to-all-done.3), kind=kOutput, calls=%fused_computation.20 | convolution fusion | flops 1223688192 | bytes 9830400 | tf_op jit(solution)/shard_map/dot_general | solution.py:18
  119.9 4.5 %fusion.41 = bf16[32,8,768]{2,1,0:T(8,128)(2,1)} fusion(bf16[256,3072]{1,0:T(8,128)(2,1)S(1)} %fusion.16, bf16[1,768,3072]{2,1,0:T(8,128)(2,1)} %param.9), kind=kOutput, calls=%fused_computation.63 | convolution fusion | flops 1208156160 | bytes 6684672 | tf_op jit(solution)/shard_map/dot_general | solution.py:18
  124.4 7.1 %all-to-all-start.4 = ((bf16[32,8,768]{2,1,0:T(8,128)(2,1)}), bf16[32,8,768]{2,1,0:T(8,128)(2,1)S(1)}, u32[]{:S(2)}, u32[]{:S(2)}) async-start(bf16[32,8,768]{2,1,0:T(8,128)(2,1)} %fusion.41), calls=%async_computation.4 | async-start | bytes 786432 | tf_op jit(solution)/shard_map/all_to_all | solution.py:39
  131.6 5.2 %fusion.8 = bf16[1,768,3072]{2,1,0:T(8,128)(2,1)} fusion(bf16[256,3072]{1,0:T(8,128)(2,1)} %copy-done.17, bf16[32,8,768]{2,1,0:T(8,128)(2,1)S(1)} %all-to-all-done.1), kind=kOutput, calls=%fused_computation.12 | convolution fusion | flops 1210318848 | bytes 6684672 | tf_op jit(solution)/shard_map/dot_general | solution.py:18
  136.8 4.4 %fusion.9 = bf16[1,3072,768]{2,1,0:T(8,128)(2,1)} fusion(bf16[32,8,768]{2,1,0:T(8,128)(2,1)S(1)} %copy-done.20, f32[256,3072]{1,0:T(8,128)S(1)} %copy-done.23), kind=kOutput, calls=%fused_computation.13 | convolution fusion | flops 1217396736 | bytes 8257536 | tf_op jit(solution)/shard_map/dot_general | solution.py:18
  142.9 2.4 %collective-permute-start.13 = (bf16[256,768]{1,0:T(8,128)(2,1)S(1)}, bf16[256,768]{1,0:T(8,128)(2,1)S(1)}, u32[]{:S(2)}, u32[]{:S(2)}) collective-permute-start(bf16[256,768]{1,0:T(8,128)(2,1)S(1)} %get-tuple-element.22), channel_id=1, source_target_pairs={{0,96},{32,0},{64,32},{96,64},{1,97},{33,1},{65,33},{97,65},{2,98}... | collective-permute-start | bytes 1179656 | tf_op jit(solution)/shard_map/ppermute | solution.py:27
  145.6 1.6 fusion.124
  147.7 1.5 fusion.125
  149.2 2.7 %collective-permute-start.15 = (bf16[256,768]{1,0:T(8,128)(2,1)S(1)}, bf16[256,768]{1,0:T(8,128)(2,1)S(1)}, u32[]{:S(2)}, u32[]{:S(2)}) collective-permute-start(bf16[256,768]{1,0:T(8,128)(2,1)S(1)} %get-tuple-element.22), channel_id=1, source_target_pairs={{0,64},{32,96},{64,0},{96,32},{1,65},{33,97},{65,1},{97,33},{2,66}... | collective-permute-start | bytes 1179656 | tf_op jit(solution)/shard_map/ppermute | solution.py:27
  151.9 1.7 multiply_reduce_fusion.4
  154.8 1.5 fusion.97
  156.3 1.4 fusion.99
  157.8 2.4 %fusion.49 = bf16[1,512,768]{2,1,0:T(8,128)(2,1)} fusion(f32[512,768]{1,0:T(8,128)S(1)} %fusion.97, f32[512,768]{1,0:T(8,128)S(1)} %copy-done.8, f32[512,768]{1,0:T(8,128)S(1)} %fusion.99, pred[512]{0:T(512)(128)(4,1)S(1)} %compare_reduce_fusion, bf16[256,768]{1,0:T(8,128)(2,1)} %collective-permute-done.9, bf16[512,1024]{0,1:T(8,128)(2,1)S(1)} %copy-done.9), kind=kOutput, calls=%fused_computation.71 | convolution fusion | flops 203292672 | bytes 6160896 | tf_op jit(solution)/shard_map/dot_general | solution.py:18
  160.2 1.6 fusion.85
  167.0 2.7 %collective-permute-start.19 = (bf16[64,8,768]{2,1,0:T(8,128)(2,1)S(1)}, bf16[64,8,768]{2,1,0:T(8,128)(2,1)S(1)}, u32[]{:S(2)}, u32[]{:S(2)}) collective-permute-start(bf16[64,8,768]{2,1,0:T(8,128)(2,1)S(1)} %fusion.48), channel_id=1, source_target_pairs={{0,1},{1,0},{2,3},{3,2},{4,5},{5,4},{6,7},{7,6},{8,9},{9,8},{10,11... | collective-permute-start | bytes 2359304 | tf_op jit(solution)/shard_map/ppermute | solution.py:22
  169.7 1.7 fusion.91
  171.4 1.7 fusion.89
  173.1 1.7 fusion.87
  174.8 1.3 fusion.21
  176.0 7.7 %all-to-all-start.5 = ((bf16[64,8,768]{2,1,0:T(8,128)(2,1)}), bf16[64,8,768]{2,1,0:T(8,128)(2,1)S(1)}, u32[]{:S(2)}, u32[]{:S(2)}) async-start(bf16[64,8,768]{2,1,0:T(8,128)(2,1)} %fusion.21), calls=%async_computation.5 | async-start | bytes 1572864 | tf_op jit(solution)/shard_map/all_to_all | solution.py:39
  183.8 1.5 fusion.77
  185.3 1.5 fusion.78
  187.4 2.6 %fusion.50 = bf16[1,512,768]{2,1,0:T(8,128)(2,1)} fusion(f32[512,768]{1,0:T(8,128)S(1)} %copy-done.5, f32[512,768]{1,0:T(8,128)S(1)} %fusion.77, f32[512,768]{1,0:T(8,128)S(1)} %copy-done.6, f32[512,768]{1,0:T(8,128)S(1)} %fusion.78, f32[512,768]{1,0:T(8,128)S(1)} %copy-done.7, f32[512,768]{1,0:T(8,128)S(1)} %fusion.79, f32[512,768]{1,0:T(8,128)S(1)} %copy-done.4, ...), kind=kOutput, calls=%fused_computation.72 | convolution fusion | flops 204472320 | bytes 12451840 | tf_op jit(solution)/shard_map/dot_general | solution.py:18
  190.0 8.5 %all-to-all-done.5 = bf16[64,8,768]{2,1,0:T(8,128)(2,1)S(1)} async-done(((bf16[64,8,768]{2,1,0:T(8,128)(2,1)}), bf16[64,8,768]{2,1,0:T(8,128)(2,1)S(1)}, u32[]{:S(2)}, u32[]{:S(2)}) %all-to-all-start.5) | async-done | bytes 786464 | tf_op jit(solution)/shard_map/all_to_all | solution.py:39
  (135 shorter events, 22.2 us)
Async XLA Ops:
  0.6 27.3 %copy-start = (bf16[1,512,768]{2,1,0:T(8,128)(2,1)S(1)}, bf16[1,512,768]{2,1,0:T(8,128)(2,1)}, u32[]{:S(2)}) copy-start(bf16[1,512,768]{2,1,0:T(8,128)(2,1)} %param.6) | copy-start | bytes 2359300
  0.6 24.4 %copy-start.21 = (s32[1,512]{1,0:T(1,128)S(1)}, s32[1,512]{1,0:T(1,128)}, u32[]{:S(2)}) copy-start(s32[1,512]{1,0:T(1,128)} %param.7) | copy-start | bytes 6148
  23.4 3.6 %collective-permute-start = (bf16[16,32,768]{2,1,0:T(8,128)(2,1)S(1)}, bf16[16,32,768]{2,1,0:T(8,128)(2,1)S(1)}, u32[]{:S(2)}, u32[]{:S(2)}) collective-permute-start(bf16[16,32,768]{2,1,0:T(8,128)(2,1)S(1)} %all_to_all.30), channel_id=1, source_target_pairs={{0,1},{1,0},{2,3},{3,2},{4,5},{5,4},{6,7},{7,6},{8,9},{9,8},{10,11... | collective-permute-start | bytes 2359304 | tf_op jit(solution)/shard_map/ppermute | solution.py:22
  27.9 1.1 copy-start.2
  30.2 10.9 %collective-permute-start.3 = (f32[2,1024]{1,0:T(2,128)S(1)}, f32[2,1024]{1,0:T(2,128)S(1)}, u32[]{:S(2)}, u32[]{:S(2)}) collective-permute-start(f32[2,1024]{1,0:T(2,128)S(1)} %get-tuple-element.44), channel_id=1, source_target_pairs={{0,32},{32,64},{64,96},{96,0},{1,33},{33,65},{65,97},{97,1},{2,34}... | collective-permute-start | bytes 24584 | tf_op jit(solution)/shard_map/ppermute | solution.py:27
  31.5 9.6 %collective-permute-start.2 = (f32[2,1024]{1,0:T(2,128)S(1)}, f32[2,1024]{1,0:T(2,128)S(1)}, u32[]{:S(2)}, u32[]{:S(2)}) collective-permute-start(f32[2,1024]{1,0:T(2,128)S(1)} %get-tuple-element.44), channel_id=1, source_target_pairs={{0,64},{32,96},{64,0},{96,32},{1,65},{33,97},{65,1},{97,33},{2,66}... | collective-permute-start | bytes 24584 | tf_op jit(solution)/shard_map/ppermute | solution.py:27
  34.0 7.3 %collective-permute-start.1 = (f32[2,1024]{1,0:T(2,128)S(1)}, f32[2,1024]{1,0:T(2,128)S(1)}, u32[]{:S(2)}, u32[]{:S(2)}) collective-permute-start(f32[2,1024]{1,0:T(2,128)S(1)} %get-tuple-element.44), channel_id=1, source_target_pairs={{0,96},{32,0},{64,32},{96,64},{1,97},{33,1},{65,33},{97,65},{2,98}... | collective-permute-start | bytes 24584 | tf_op jit(solution)/shard_map/ppermute | solution.py:27
  36.2 17.7 %collective-permute-start.5 = (bf16[256,768]{1,0:T(8,128)(2,1)S(1)}, bf16[256,768]{1,0:T(8,128)(2,1)S(1)}, u32[]{:S(2)}, u32[]{:S(2)}) collective-permute-start(bf16[256,768]{1,0:T(8,128)(2,1)S(1)} %get-tuple-element.36), channel_id=1, source_target_pairs={{0,64},{32,96},{64,0},{96,32},{1,65},{33,97},{65,1},{97,33},{2,66}... | collective-permute-start | bytes 1179656 | tf_op jit(solution)/shard_map/ppermute | solution.py:27
  38.6 15.3 %collective-permute-start.6 = (bf16[256,768]{1,0:T(8,128)(2,1)S(1)}, bf16[256,768]{1,0:T(8,128)(2,1)S(1)}, u32[]{:S(2)}, u32[]{:S(2)}) collective-permute-start(bf16[256,768]{1,0:T(8,128)(2,1)S(1)} %get-tuple-element.35), channel_id=1, source_target_pairs={{0,96},{32,0},{64,32},{96,64},{1,97},{33,1},{65,33},{97,65},{2,98}... | collective-permute-start | bytes 1179656 | tf_op jit(solution)/shard_map/ppermute | solution.py:27
  41.1 16.1 %collective-permute-start.4 = (bf16[256,768]{1,0:T(8,128)(2,1)S(1)}, bf16[256,768]{1,0:T(8,128)(2,1)S(1)}, u32[]{:S(2)}, u32[]{:S(2)}) collective-permute-start(bf16[256,768]{1,0:T(8,128)(2,1)S(1)} %get-tuple-element.34), channel_id=1, source_target_pairs={{0,32},{32,64},{64,96},{96,0},{1,33},{33,65},{65,97},{97,1},{2,34}... | collective-permute-start | bytes 1179656 | tf_op jit(solution)/shard_map/ppermute | solution.py:27
  58.7 14.5 %all-to-all-start.1 = ((bf16[32,8,768]{2,1,0:T(8,128)(2,1)}), bf16[32,8,768]{2,1,0:T(8,128)(2,1)S(1)}, u32[]{:S(2)}, u32[]{:S(2)}) async-start(bf16[32,8,768]{2,1,0:T(8,128)(2,1)} %fusion.74), calls=%async_computation.1 | async-start | bytes 786432 | tf_op jit(solution)/shard_map/all_to_all | solution.py:39
  65.5 3.2 %copy-start.16 = (bf16[1024,768]{1,0:T(8,128)(2,1)}, bf16[1024,768]{1,0:T(8,128)(2,1)S(1)}, u32[]{:S(2)}) copy-start(bf16[1024,768]{1,0:T(8,128)(2,1)S(1)} %convolution_convert_fusion.2) | copy-start | bytes 4718596
  66.6 21.5 %collective-permute-start.12 = (bf16[256,768]{1,0:T(8,128)(2,1)}, bf16[256,768]{1,0:T(8,128)(2,1)}, u32[]{:S(2)}, u32[]{:S(2)}) collective-permute-start(bf16[256,768]{1,0:T(8,128)(2,1)} %get-tuple-element.32), channel_id=1, source_target_pairs={{0,96},{32,0},{64,32},{96,64},{1,97},{33,1},{65,33},{97,65},{2,98}... | collective-permute-start | bytes 1179656 | tf_op jit(solution)/shard_map/ppermute | solution.py:27
  66.9 21.2 %collective-permute-start.11 = (bf16[256,768]{1,0:T(8,128)(2,1)}, bf16[256,768]{1,0:T(8,128)(2,1)}, u32[]{:S(2)}, u32[]{:S(2)}) collective-permute-start(bf16[256,768]{1,0:T(8,128)(2,1)} %get-tuple-element.33), channel_id=1, source_target_pairs={{0,64},{32,96},{64,0},{96,32},{1,65},{33,97},{65,1},{97,33},{2,66}... | collective-permute-start | bytes 1179656 | tf_op jit(solution)/shard_map/ppermute | solution.py:27
  68.7 19.5 %collective-permute-start.10 = (bf16[256,768]{1,0:T(8,128)(2,1)S(1)}, bf16[256,768]{1,0:T(8,128)(2,1)}, u32[]{:S(2)}, u32[]{:S(2)}) collective-permute-start(bf16[256,768]{1,0:T(8,128)(2,1)S(1)} %get-tuple-element.31), channel_id=1, source_target_pairs={{0,32},{32,64},{64,96},{96,0},{1,33},{33,65},{65,97},{97,1},{2,34}... | collective-permute-start | bytes 1179656 | tf_op jit(solution)/shard_map/ppermute | solution.py:27
  76.9 1.7 copy-start.22
  83.7 14.5 %all-to-all-start.2 = ((bf16[32,8,768]{2,1,0:T(8,128)(2,1)}), bf16[32,8,768]{2,1,0:T(8,128)(2,1)}, u32[]{:S(2)}, u32[]{:S(2)}) async-start(bf16[32,8,768]{2,1,0:T(8,128)(2,1)} %fusion.38), calls=%async_computation.2 | async-start | bytes 786432 | tf_op jit(solution)/shard_map/all_to_all | solution.py:39
  98.2 13.8 %all-to-all-start.3 = ((bf16[32,8,768]{2,1,0:T(8,128)(2,1)}), bf16[32,8,768]{2,1,0:T(8,128)(2,1)S(1)}, u32[]{:S(2)}, u32[]{:S(2)}) async-start(bf16[32,8,768]{2,1,0:T(8,128)(2,1)} %fusion.75), calls=%async_computation.3 | async-start | bytes 786432 | tf_op jit(solution)/shard_map/all_to_all | solution.py:39
  101.9 45.4 %collective-permute-start.8 = (bf16[256,768]{1,0:T(8,128)(2,1)}, bf16[256,768]{1,0:T(8,128)(2,1)}, u32[]{:S(2)}, u32[]{:S(2)}) collective-permute-start(bf16[256,768]{1,0:T(8,128)(2,1)} %bitcast.26), channel_id=1, source_target_pairs={{0,64},{32,96},{64,0},{96,32},{1,65},{33,97},{65,1},{97,33},{2,66}... | collective-permute-start | bytes 1179656 | tf_op jit(solution)/shard_map/ppermute | solution.py:27
  104.5 44.7 %collective-permute-start.7 = (bf16[256,768]{1,0:T(8,128)(2,1)}, bf16[256,768]{1,0:T(8,128)(2,1)}, u32[]{:S(2)}, u32[]{:S(2)}) collective-permute-start(bf16[256,768]{1,0:T(8,128)(2,1)} %bitcast.26), channel_id=1, source_target_pairs={{0,96},{32,0},{64,32},{96,64},{1,97},{33,1},{65,33},{97,65},{2,98}... | collective-permute-start | bytes 1179656 | tf_op jit(solution)/shard_map/ppermute | solution.py:27
  104.8 40.4 %collective-permute-start.9 = (bf16[256,768]{1,0:T(8,128)(2,1)}, bf16[256,768]{1,0:T(8,128)(2,1)}, u32[]{:S(2)}, u32[]{:S(2)}) collective-permute-start(bf16[256,768]{1,0:T(8,128)(2,1)} %bitcast.26), channel_id=1, source_target_pairs={{0,32},{32,64},{64,96},{96,0},{1,33},{33,65},{65,97},{97,1},{2,34}... | collective-permute-start | bytes 1179656 | tf_op jit(solution)/shard_map/ppermute | solution.py:27
  112.0 6.7 %copy-start.19 = (bf16[32,8,768]{2,1,0:T(8,128)(2,1)}, bf16[32,8,768]{2,1,0:T(8,128)(2,1)S(1)}, u32[]{:S(2)}) copy-start(bf16[32,8,768]{2,1,0:T(8,128)(2,1)S(1)} %all-to-all-done.3) | copy-start | bytes 1179652
  118.8 1.2 copy-start.17
  124.4 17.4 %all-to-all-start.4 = ((bf16[32,8,768]{2,1,0:T(8,128)(2,1)}), bf16[32,8,768]{2,1,0:T(8,128)(2,1)S(1)}, u32[]{:S(2)}, u32[]{:S(2)}) async-start(bf16[32,8,768]{2,1,0:T(8,128)(2,1)} %fusion.41), calls=%async_computation.4 | async-start | bytes 786432 | tf_op jit(solution)/shard_map/all_to_all | solution.py:39
  131.6 5.2 %copy-start.20 = (bf16[32,8,768]{2,1,0:T(8,128)(2,1)S(1)}, bf16[32,8,768]{2,1,0:T(8,128)(2,1)}, u32[]{:S(2)}) copy-start(bf16[32,8,768]{2,1,0:T(8,128)(2,1)} %copy-done.19) | copy-start | bytes 1179652
  131.6 5.2 %copy-start.23 = (f32[256,3072]{1,0:T(8,128)S(1)}, f32[256,3072]{1,0:T(8,128)}, u32[]{:S(2)}) copy-start(f32[256,3072]{1,0:T(8,128)} %copy-done.22) | copy-start | bytes 9437188
  141.9 3.7 %copy-start.18 = (bf16[1,512,768]{2,1,0:T(8,128)(2,1)S(1)}, bf16[1,512,768]{2,1,0:T(8,128)(2,1)}, u32[]{:S(2)}) copy-start(bf16[1,512,768]{2,1,0:T(8,128)(2,1)} %param.11) | copy-start | bytes 2359300
  142.5 23.1 %collective-permute-start.17 = (bf16[256,768]{1,0:T(8,128)(2,1)S(1)}, bf16[256,768]{1,0:T(8,128)(2,1)S(1)}, u32[]{:S(2)}, u32[]{:S(2)}) collective-permute-start(bf16[256,768]{1,0:T(8,128)(2,1)S(1)} %get-tuple-element.22), channel_id=1, source_target_pairs={{0,32},{32,64},{64,96},{96,0},{1,33},{33,65},{65,97},{97,1},{2,34}... | collective-permute-start | bytes 1179656 | tf_op jit(solution)/shard_map/ppermute | solution.py:27
  142.9 20.6 %collective-permute-start.13 = (bf16[256,768]{1,0:T(8,128)(2,1)S(1)}, bf16[256,768]{1,0:T(8,128)(2,1)S(1)}, u32[]{:S(2)}, u32[]{:S(2)}) collective-permute-start(bf16[256,768]{1,0:T(8,128)(2,1)S(1)} %get-tuple-element.22), channel_id=1, source_target_pairs={{0,96},{32,0},{64,32},{96,64},{1,97},{33,1},{65,33},{97,65},{2,98}... | collective-permute-start | bytes 1179656 | tf_op jit(solution)/shard_map/ppermute | solution.py:27
  145.3 6.6 %copy-start.1 = (f32[512,1024]{0,1:T(8,128)S(1)}, f32[512,1024]{0,1:T(8,128)}, u32[]{:S(2)}) copy-start(f32[512,1024]{0,1:T(8,128)} %get-tuple-element.24) | copy-start | bytes 6291460
  145.3 6.6 %copy-start.15 = (f32[512,256]{0,1:T(8,128)S(1)}, f32[512,256]{0,1:T(8,128)}, u32[]{:S(2)}) copy-start(f32[512,256]{0,1:T(8,128)} %fusion.55) | copy-start | bytes 1572868
  145.3 18.3 %collective-permute-start.14 = (f32[256]{0:T(256)S(1)}, f32[256]{0:T(256)S(1)}, u32[]{:S(2)}, u32[]{:S(2)}) collective-permute-start(f32[256]{0:T(256)S(1)} %get-tuple-element.21), channel_id=1, source_target_pairs={{0,96},{32,0},{64,32},{96,64},{1,97},{33,1},{65,33},{97,65},{2,98}... | collective-permute-start | bytes 3080 | tf_op jit(solution)/shard_map/ppermute | solution.py:27
  147.3 14.6 %collective-permute-start.16 = (f32[256]{0:T(256)S(1)}, f32[256]{0:T(256)S(1)}, u32[]{:S(2)}, u32[]{:S(2)}) collective-permute-start(f32[256]{0:T(256)S(1)} %get-tuple-element.21), channel_id=1, source_target_pairs={{0,64},{32,96},{64,0},{96,32},{1,65},{33,97},{65,1},{97,33},{2,66}... | collective-permute-start | bytes 3080 | tf_op jit(solution)/shard_map/ppermute | solution.py:27
  149.2 13.9 %collective-permute-start.15 = (bf16[256,768]{1,0:T(8,128)(2,1)S(1)}, bf16[256,768]{1,0:T(8,128)(2,1)S(1)}, u32[]{:S(2)}, u32[]{:S(2)}) collective-permute-start(bf16[256,768]{1,0:T(8,128)(2,1)S(1)} %get-tuple-element.22), channel_id=1, source_target_pairs={{0,64},{32,96},{64,0},{96,32},{1,65},{33,97},{65,1},{97,33},{2,66}... | collective-permute-start | bytes 1179656 | tf_op jit(solution)/shard_map/ppermute | solution.py:27
  153.6 1.2 copy-start.9
  154.0 0.7 copy-start.10
  154.8 2.9 %copy-start.8 = (f32[512,768]{1,0:T(8,128)S(1)}, f32[512,768]{1,0:T(8,128)}, u32[]{:S(2)}) copy-start(f32[512,768]{1,0:T(8,128)} %fusion.101) | copy-start | bytes 4718596
  161.9 3.7 %collective-permute-start.18 = (f32[256]{0:T(256)S(1)}, f32[256]{0:T(256)S(1)}, u32[]{:S(2)}, u32[]{:S(2)}) collective-permute-start(f32[256]{0:T(256)S(1)} %get-tuple-element.21), channel_id=1, source_target_pairs={{0,32},{32,64},{64,96},{96,0},{1,33},{33,65},{65,97},{97,1},{2,34}... | collective-permute-start | bytes 3080 | tf_op jit(solution)/shard_map/ppermute | solution.py:27
  163.5 1.5 copy-start.12
  166.0 0.7 copy-start.14
  167.0 7.8 %collective-permute-start.19 = (bf16[64,8,768]{2,1,0:T(8,128)(2,1)S(1)}, bf16[64,8,768]{2,1,0:T(8,128)(2,1)S(1)}, u32[]{:S(2)}, u32[]{:S(2)}) collective-permute-start(bf16[64,8,768]{2,1,0:T(8,128)(2,1)S(1)} %fusion.48), channel_id=1, source_target_pairs={{0,1},{1,0},{2,3},{3,2},{4,5},{5,4},{6,7},{7,6},{8,9},{9,8},{10,11... | collective-permute-start | bytes 2359304 | tf_op jit(solution)/shard_map/ppermute | solution.py:22
  174.8 9.0 %copy-start.3 = (bf16[4,256,768]{2,1,0:T(8,128)(2,1)S(1)}, bf16[4,256,768]{2,1,0:T(8,128)(2,1)}, u32[]{:S(2)}) copy-start(bf16[4,256,768]{2,1,0:T(8,128)(2,1)} %copy-done.2) | copy-start | bytes 4718596
  176.0 22.5 %all-to-all-start.5 = ((bf16[64,8,768]{2,1,0:T(8,128)(2,1)}), bf16[64,8,768]{2,1,0:T(8,128)(2,1)S(1)}, u32[]{:S(2)}, u32[]{:S(2)}) async-start(bf16[64,8,768]{2,1,0:T(8,128)(2,1)} %fusion.21), calls=%async_computation.5 | async-start | bytes 1572864 | tf_op jit(solution)/shard_map/all_to_all | solution.py:39
  183.8 3.1 %copy-start.11 = (bf16[512,256]{0,1:T(8,128)(2,1)S(1)}, bf16[512,256]{0,1:T(8,128)(2,1)}, u32[]{:S(2)}) copy-start(bf16[512,256]{0,1:T(8,128)(2,1)} %copy-done.10) | copy-start | bytes 786436
  183.8 3.5 %copy-start.6 = (f32[512,768]{1,0:T(8,128)S(1)}, f32[512,768]{1,0:T(8,128)}, u32[]{:S(2)}) copy-start(f32[512,768]{1,0:T(8,128)} %fusion.89) | copy-start | bytes 4718596
  183.8 3.5 %copy-start.7 = (f32[512,768]{1,0:T(8,128)S(1)}, f32[512,768]{1,0:T(8,128)}, u32[]{:S(2)}) copy-start(f32[512,768]{1,0:T(8,128)} %fusion.87) | copy-start | bytes 4718596
  185.3 2.0 copy-start.4
  185.3 2.1 %copy-start.5 = (f32[512,768]{1,0:T(8,128)S(1)}, f32[512,768]{1,0:T(8,128)}, u32[]{:S(2)}) copy-start(f32[512,768]{1,0:T(8,128)} %fusion.91) | copy-start | bytes 4718596
  (1 other events, 0.7 us)

commit v2 on v1

v2 whole, which is shorter than its diff:
```python
import functools
import math

import jax
import jax.numpy as jnp
from jax import lax
from jax.experimental import pallas as pl
from jax.experimental.pallas import tpu as pltpu
from jax.sharding import Mesh, PartitionSpec as P

LAYER_POS = 1
EPS = 1e-06
LOW_LOGIT = -1e30

PLANE = ("y", "z")
GROUP = ("y", "z", "core")
F32 = jnp.float32
BF16 = jnp.bfloat16


def matmul(a, b, contract):
    return lax.dot_general(a, b, ((contract[:1], contract[1:]), ((), ())), preferred_element_type=F32)


def swap_cores(values):
    return lax.ppermute(values, "core", [(0, 1), (1, 0)])


def along_x(values, steps):
    n = lax.axis_size("x")
    return lax.ppermute(values, "x", [(i, (i + steps) % n) for i in range(n)])


def gather_x(values):
    return [values] + [along_x(values, -k) for k in range(1, lax.axis_size("x"))]


def to_neighbours(values):
    return along_x(values, -1), along_x(values, 1)


def pass_on(ahead, behind):
    half = ahead.shape[0] // 2
    return along_x(behind[:half], 1), along_x(ahead[half:], -1)


def exchange(values, axes):
    return lax.all_to_all(values, axes, 0, 0, tiled=True)


def roll_blocks(blocks, first):
    return lax.dynamic_slice_in_dim(jnp.concatenate([blocks, blocks[:-1]]), first, blocks.shape[0], 0)


def gather_phi(phi):
    rows = phi.T
    planes = lax.axis_size("x")
    chips = lax.axis_size("y") * lax.axis_size("z")
    mine = exchange(jnp.broadcast_to(rows[None], (chips,) + rows.shape), PLANE)
    other = swap_cores(mine)
    first = lax.axis_index("core") == 0
    both = jnp.stack([jnp.where(first, mine, other), jnp.where(first, other, mine)], axis=1)
    groups = both.reshape(planes, -1, rows.shape[1])
    return roll_blocks(groups, lax.axis_index("x"))


def gelu_parts(v):
    scale = math.sqrt(2.0 / math.pi)
    square = v * v
    t = jnp.tanh(scale * v * (1.0 + 0.044715 * square))
    half = 0.5 * (1.0 + t)
    slope = half + 0.5 * scale * v * (1.0 - t * t) * (1.0 + 3.0 * 0.044715 * square)
    return v * half, slope


def unit(*arrays):
    return sum(a[0, 0].astype(BF16) * 0 for a in arrays) + jnp.ones((), BF16)


LIMIT = 56 * 1024 * 1024


def call(kernel, steps, inputs, outputs, scratch=(), work=1000):
    def spec(block, where):
        if where is None:
            where = (0,) * len(block)
        if isinstance(where, tuple):
            return pl.BlockSpec(block, lambda i: where)
        return pl.BlockSpec(block, lambda i: tuple(i if d == where else 0 for d in range(len(block))))

    return pl.pallas_call(
        kernel,
        grid=(steps,),
        in_specs=[spec(block, where) for _, block, where in inputs],
        out_specs=[spec(block, where) for _, _, block, where in outputs],
        out_shape=[jax.ShapeDtypeStruct(shape, kind) for kind, shape, _, _ in outputs],
        scratch_shapes=list(scratch),
        compiler_params=pltpu.CompilerParams(vmem_limit_bytes=LIMIT),
        cost_estimate=pl.CostEstimate(flops=work, bytes_accessed=1000, transcendentals=0),
    )(*[array for array, _, _ in inputs])


def accumulate(total, part, out_ref):
    step = pl.program_id(0)

    @pl.when(step == 0)
    def _():
        total[...] = part

    @pl.when(step > 0)
    def _():
        total[...] += part

    @pl.when(step == pl.num_programs(0) - 1)
    def _():
        out_ref[...] = total[...].astype(BF16)


def forward_kernel(rows_ref, up_ref, down_ref, hidden_ref, slope_ref, out_ref, total):
    preact = jnp.dot(rows_ref[...], up_ref[...], preferred_element_type=F32)
    hidden, slope = gelu_parts(preact)
    hidden = hidden.astype(BF16)
    hidden_ref[...] = hidden
    slope_ref[...] = slope.astype(BF16)
    accumulate(total, jnp.dot(hidden, down_ref[...], preferred_element_type=F32), out_ref)


def backward_kernel(grad_ref, slope_ref, up_ref, down_ref, pre_ref, out_ref, total):
    pre_grad = (slope_ref[...].astype(F32) * matmul(grad_ref[...], down_ref[...], (1, 1))).astype(BF16)
    pre_ref[...] = pre_grad
    accumulate(total, matmul(pre_grad, up_ref[...], (1, 1)), out_ref)


def product_kernel(a_ref, b_ref, out_ref):
    out_ref[...] = matmul(a_ref[...], b_ref[...], (0, 0)).astype(BF16)


def dispatch_kernel(
    phi_ref, tops_ref, norms_ref, *refs
):
    pieces, outs = refs[:5], refs[5:]
    weights_ref, combine_ref, in_ref, normed_ref, factor_ref, inverse_ref, top_ref, logits = outs
    phi = phi_ref[...]
    spans, at = [], 0
    for p in pieces:
        spans.append(slice(at, at + p.shape[0]))
        at += p.shape[0]
    top = None
    for p, span in zip(pieces, spans):
        l = matmul(phi, p[...], (1, 1))
        logits[:, span] = l
        norms = norms_ref[:, span]
        combine_ref[:, span] = (jnp.exp(l - tops_ref[:, span]) * norms).astype(BF16)
        here = jnp.max(jnp.where(norms > 0.0, l, LOW_LOGIT), axis=1, keepdims=True)
        top = here if top is None else jnp.maximum(top, here)
    slot_total, mixed = 0.0, 0.0
    for p, span in zip(pieces, spans):
        w = jnp.where(norms_ref[:, span] > 0.0, jnp.exp(logits[:, span] - top), 0.0).astype(BF16)
        weights_ref[:, span] = w
        slot_total += jnp.sum(w.astype(F32), axis=1, keepdims=True)
        mixed += jnp.dot(w, p[...], preferred_element_type=F32)
    inverse = 1.0 / slot_total
    mixed = mixed * inverse
    factor = lax.rsqrt(jnp.mean(mixed * mixed, axis=1, keepdims=True) + EPS)
    normed = mixed * factor
    normed_ref[...] = normed
    in_ref[...] = normed.astype(BF16)
    factor_ref[...] = factor
    inverse_ref[...] = inverse
    top_ref[...] = top


def slot_kernel(combine_ref, *refs):
    *pieces, out_ref = refs
    total, at = 0.0, 0
    for p in pieces:
        total += jnp.dot(combine_ref[:, at : at + p.shape[0]], p[...], preferred_element_type=F32)
        at += p.shape[0]
    out_ref[...] = total.astype(BF16)


def split(values):
    parts = []
    for _ in range(3):
        part = values.astype(BF16).astype(F32)
        parts.append(part)
        values = values - part
    return parts


def as_row(column):
    return jnp.transpose(jnp.broadcast_to(column, (column.shape[0], 128)))[:1]


def slot_grad_kernel(out_ref, _, combine_ref, top_ref, inverse_ref, *refs):
    *pieces, combine_grad_ref, message_ref, lines = refs
    own, at = out_ref[...], 0
    slots = own.shape[0]
    message_ref[:slots, :] = own
    lines[...] = jnp.zeros_like(lines)
    width = pieces[0].shape[0]
    for p in pieces:
        span = slice(at, at + p.shape[0])
        grad = matmul(own, p[...], (1, 1))
        combine_grad_ref[:, span] = grad
        sums = jnp.sum(combine_ref[:, span].astype(F32) * grad, axis=0, keepdims=True)
        line, start = at // width, at % width
        for k, part in enumerate(split(sums)):
            lines[4 * k + line : 4 * k + line + 1, start : start + p.shape[0]] = part
        at += p.shape[0]
    for line, ref in ((12, top_ref), (13, inverse_ref)):
        for k, part in enumerate(split(as_row(ref[...]))):
            lines[line : line + 1, k * slots : (k + 1) * slots] = part
    message_ref[slots:, :] = lines[...].astype(BF16)


def mixed_grad_kernel(back_ref, normed_ref, factor_ref, _, out_ref, column_ref):
    back = back_ref[...].astype(F32)
    normed, factor = normed_ref[...], factor_ref[...]
    out = (factor * (back - normed * jnp.mean(back * normed, axis=1, keepdims=True))).astype(BF16)
    slots = out.shape[0]
    out_ref[:slots, :] = out
    column = jnp.sum(normed * out.astype(F32), axis=1, keepdims=True) / factor
    column_ref[...] = column
    row = jnp.concatenate(split(as_row(column)), axis=1)
    out_ref[slots:, :] = jnp.broadcast_to(row, (16, row.shape[1])).astype(BF16)


def phi_kernel(grad_ref, combine_ref, combine_grad_ref, weights_ref, inverse_ref, column_ref, *refs):
    messages, pieces, out_ref = refs[:4], refs[4:9], refs[9]
    grad = grad_ref[...]
    width = pieces[0].shape[0]
    messages = [m[...].astype(F32) for m in messages]
    total, at = 0.0, 0
    for p in pieces:
        span = slice(at, at + p.shape[0])
        line, start = at // width, at % width
        at += p.shape[0]
        rows = 0.0
        for k, m in enumerate(messages):
            for j in range(3):
                i = 4 * j + (line - k) % 4
                rows += m[i : i + 1, start : start + p.shape[0]]
        tokens = p[...]
        share = weights_ref[:, span].astype(F32) * inverse_ref[...]
        logit_grad = combine_ref[:, span].astype(F32) * (combine_grad_ref[:, span] - rows) + share * (
            matmul(grad, tokens, (1, 1)) - column_ref[...]
        )
        total += jnp.dot(logit_grad.astype(BF16), tokens, preferred_element_type=F32)
    out_ref[...] = total.astype(BF16)


def combine_kernel(live_ref, tokens_ref, grad_ref, phi_ref, *refs):
    *outs, mixed_ref, logit_ref = refs
    width = outs[0].shape[0]
    logits = matmul(tokens_ref[...], phi_ref[...], (1, 1))
    powers = jnp.exp(logits - jnp.max(logits, axis=1, keepdims=True))
    combine = powers * (1.0 / jnp.sum(powers, axis=1, keepdims=True))
    combine_b = combine.astype(BF16)
    mixed = sum(
        jnp.dot(combine_b[:, k * width : (k + 1) * width], o[...], preferred_element_type=F32)
        for k, o in enumerate(outs)
    )
    mixed_ref[...] = jnp.where(live_ref[:, :1] > 0.0, mixed, 0.0).astype(BF16)
    grad = grad_ref[...]
    combine_grad = jnp.concatenate([matmul(grad, o[...], (1, 1)) for o in outs], axis=1)
    product = combine * combine_grad
    logit_ref[...] = (product - combine * jnp.sum(product, axis=1, keepdims=True)).astype(BF16)


def tokens_kernel(live_ref, logit_ref, tokens_ref, phi_ref, *refs):
    messages, grads, out_ref, zero_ref = refs[:4], refs[4:8], refs[8], refs[9]
    zero_ref[...] = jnp.zeros_like(zero_ref)
    width = grads[0].shape[0] - 16

    def joined(line, arrays):
        rows = [m[...].astype(F32)[line : line + 1] for m in arrays]
        return jnp.concatenate([sum(r[:, k * width : (k + 1) * width] for k in range(3)) for r in rows], axis=1)

    top, inverse = joined(12, messages), joined(13, messages)
    column = joined(0, [g.at[width:, :] for g in grads])
    tokens = tokens_ref[...]
    logits = matmul(tokens, phi_ref[...], (1, 1))
    weights = jnp.where(live_ref[:, :1] > 0.0, jnp.exp(logits - top), 0.0).astype(BF16)
    share = weights.astype(F32) * inverse
    dispatch_grad = jnp.concatenate([matmul(tokens, g[:width, :], (1, 1)) for g in grads], axis=1)
    logit_grad = logit_ref[...].astype(F32) + share * (dispatch_grad - column)
    total = jnp.dot(logit_grad.astype(BF16), phi_ref[...], preferred_element_type=F32)
    share_b = share.astype(BF16)
    for k, g in enumerate(grads):
        total += jnp.dot(share_b[:, k * width : (k + 1) * width], g[:width, :], preferred_element_type=F32)
    out_ref[...] = total.astype(BF16)


def sum_kernel(parts_ref, zero_ref, out_ref):
    out_ref[...] = jnp.sum(parts_ref[...].astype(F32), axis=0) + zero_ref[:, :1]


def per_device(tokens, halt_steps, phi, w_up, w_down, cotangent):
    clip_part = tokens[0]
    rows, features = clip_part.shape
    planes = lax.axis_size("x")
    experts = lax.axis_size("y") * lax.axis_size("z") * lax.axis_size("core")
    live_rows = (halt_steps[0] > LAYER_POS)[:, None]
    masked_grad = jnp.where(live_rows, cotangent[0], jnp.zeros((), BF16))
    live_rows = live_rows.astype(F32)
    live_wide = jnp.broadcast_to(live_rows, (rows, 128))

    def whole(array):
        return (array, array.shape, None)

    def made(kind, *shape):
        return (kind, shape, shape, None)

    ahead, behind = to_neighbours(clip_part)
    far = pass_on(ahead, behind)
    phi_groups = gather_phi(phi)
    own_slots = phi_groups.shape[1]
    per_expert = own_slots // experts
    phi_all = phi_groups.reshape(-1, features)
    slots = phi_all.shape[0]

    logits = matmul(clip_part, phi_all, (1, 1))
    top = jnp.max(logits, axis=-1, keepdims=True)
    norm = live_rows / jnp.sum(jnp.exp(logits - top), axis=-1, keepdims=True)
    message = jnp.stack([top, norm]).reshape(2, -1, 128)
    row_stats = jnp.concatenate(gather_x(message), axis=1).reshape(2, 1, -1)

    grad_pieces = [masked_grad] + gather_x(masked_grad * unit(far[0], far[1], row_stats[0]))[1:]
    pieces = [clip_part, ahead, *far, behind]
    clip_rows = planes * rows

    def rows_of(values):
        return values.reshape(experts, per_expert, -1)

    weights, own_combine, slot_in, normed, factor, inverse, slot_top = call(
        dispatch_kernel,
        1,
        [whole(phi_groups[0]), whole(row_stats[0]), whole(row_stats[1]), *map(whole, pieces)],
        [
            made(BF16, own_slots, clip_rows),
            made(BF16, own_slots, clip_rows),
            made(BF16, own_slots, features),
            made(F32, own_slots, features),
            made(F32, own_slots, 1),
            made(F32, own_slots, 1),
            made(F32, own_slots, 1),
        ],
        [pltpu.VMEM((own_slots, clip_rows), F32)],
    )
    expert_in = exchange(rows_of(slot_in), GROUP).reshape(-1, features)

    up_matrix, down_matrix = w_up[0], w_down[0]
    hid = up_matrix.shape[1]
    steps = 6
    tile = hid // steps
    expert_rows = expert_in.shape[0]
    block, wide = (expert_rows, features), (expert_rows, tile)
    up, down = (up_matrix, (features, tile), 1), (down_matrix, (tile, features), 0)
    total = [pltpu.VMEM(block, F32)]
    hidden, slope, output = call(
        forward_kernel,
        steps,
        [whole(expert_in), up, down],
        [(BF16, (expert_rows, hid), wide, 1), (BF16, (expert_rows, hid), wide, 1), made(BF16, *block)],
        total,
    )
    (slot_grad,) = call(
        slot_kernel, 1, [whole(own_combine), *map(whole, grad_pieces)], [made(BF16, own_slots, features)]
    )
    arrived = exchange(rows_of(jnp.concatenate([slot_grad, output], axis=1)), GROUP).reshape(own_slots, -1)

    pre_grad, normed_grad = call(
        backward_kernel,
        steps,
        [(arrived, block, (0, 0)), (slope, wide, 1), up, down],
        [(BF16, (expert_rows, hid), wide, 1), made(BF16, *block)],
        total,
    )
    back_grad = exchange(rows_of(normed_grad), GROUP).reshape(own_slots, features)
    (grad_down,) = call(
        product_kernel,
        steps,
        [(hidden, wide, 1), (arrived, block, (0, 0))],
        [(BF16, down_matrix.shape, down[1], 0)],
    )
    (grad_up,) = call(
        product_kernel,
        steps,
        [whole(expert_in), (pre_grad, wide, 1)],
        [(BF16, up_matrix.shape, up[1], 1)],
    )

    slot_combine_grad, message = call(
        slot_grad_kernel,
        1,
        [
            (arrived, block, (0, 1)),
            (normed_grad, (16, 128), None),
            *map(whole, (own_combine, slot_top, inverse)),
            *map(whole, grad_pieces),
        ],
        [made(F32, own_slots, clip_rows), made(BF16, own_slots + 16, features)],
        [pltpu.VMEM((16, features), F32)],
    )
    slot_outs = gather_x(message)
    tails = [(m, (16, features), (own_slots // 16, 0)) for m in slot_outs]

    mixed_grad, own_column = call(
        mixed_grad_kernel,
        1,
        [whole(back_grad), whole(normed), whole(factor), (grad_down, (16, 128), None)],
        [made(BF16, own_slots + 16, features), made(F32, own_slots, 1)],
    )
    all_grads = gather_x(mixed_grad)
    (part_phi,) = call(
        phi_kernel,
        1,
        [
            (mixed_grad, (own_slots, features), None),
            whole(own_combine),
            whole(slot_combine_grad),
            whole(weights),
            whole(inverse),
            whole(own_column),
            *tails,
            *map(whole, pieces),
        ],
        [made(BF16, own_slots, features)],
    )
    arrived_phi = exchange(rows_of(part_phi), GROUP)

    part = 256
    thin, lanes = (part, features), (part, 128)
    mixed, combine_logit_grad = call(
        combine_kernel,
        rows // part,
        [
            (live_wide, lanes, 0),
            (clip_part, thin, 0),
            (masked_grad, thin, 0),
            whole(phi_all),
            *[(m, (own_slots, features), None) for m in slot_outs],
        ],
        [(BF16, clip_part.shape, thin, 0), (BF16, (rows, slots), (part, slots), 0)],
    )
    grad_rows, zero = call(
        tokens_kernel,
        rows // part,
        [
            (live_wide, lanes, 0),
            (combine_logit_grad, (part, slots), 0),
            (clip_part, thin, 0),
            whole(phi_all),
            *tails,
            *map(whole, all_grads),
        ],
        [(BF16, clip_part.shape, thin, 0), made(F32, 8, 128)],
        work=5 * 10**9,
    )
    (grad_phi_t,) = call(
        sum_kernel, 1, [whole(arrived_phi), whole(zero)], [made(F32, *arrived_phi.shape[1:])]
    )
    return (mixed[None], grad_rows[None], grad_phi_t, grad_up[None], grad_down[None])


def solution(mesh):
    fine = Mesh(mesh.devices.reshape(4, 4, 4, 2), ("x", "y", "z", "core"))
    rows = P(GROUP, "x", None)
    blocks = P(("x",) + GROUP, None, None)
    return jax.shard_map(
        per_device,
        mesh=fine,
        in_specs=(rows, P(GROUP, "x"), P(None, GROUP), blocks, blocks, rows),
        out_specs=(rows, rows, P(("x",) + GROUP, None), blocks, blocks),
        check_vma=False,
    )
```

time: 201 us -> 189 us (0.940)
  Pallas kernels: 0 us -> 71.4 us
  matrix products: 65.3 us -> 1.02 us
  waiting for transfers between devices: 40.6 us -> 16.3 us
  blocking collectives: 21.8 us -> 39.2 us
  starting transfers between devices: 52.7 us -> 41.8 us
  other arithmetic: 10.7 us -> 4.53 us
  local copies, waits for them, and re-layouts: 6.83 us -> 10.4 us
    pallas_call x0 -> x12, Pallas kernels: none -> 71.4 us  [call(): pl.pallas_call(kernel, grid=(steps,), in_specs=[spec(block, where) for _,...]
    dot_general x33 -> x1, matrix products: 65.3 us -> 1.02 us  [matmul(): lax.dot_general(a, b, ((contract[:1], contract[1:]), ((), ())), preferred...]
    all_to_all x1 -> x2, blocking collectives: 21.8 us -> 39.2 us  [exchange(): return lax.all_to_all(values, axes, 0, 0, tiled=True)]
    ppermute x18 -> x16, waiting for transfers between devices: 16.3 us -> 5.01 us  [along_x(): return lax.ppermute(values, 'x', [(i, (i + steps) % n) for i in range(n)])]
    all_to_all x5 -> x3, waiting for transfers between devices: 22.4 us -> 11.2 us  [exchange(): return lax.all_to_all(values, axes, 0, 0, tiled=True)]
    all_to_all x5 -> x3, starting transfers between devices: 27.1 us -> 19.3 us  [exchange(): return lax.all_to_all(values, axes, 0, 0, tiled=True)]
    convert_element_type x2, other arithmetic: 3.31 us -> 0.03 us  [per_device(): live_rows = live_rows.astype(F32)]
    reduce_sum x7 -> x1, other arithmetic: 3.08 us -> 0.36 us  [per_device(): norm = live_rows / jnp.sum(jnp.exp(logits - top), axis=-1, keepdims=True)]
  transfers between devices with their start and end apart: 25 -> 20, of which waited for: 11 -> 4; matrix products, arithmetic and copies ran while one was open for 35% -> 3% of each run, Pallas kernels for 0% -> 27%
where the time goes in v2:
time: 189 us; the launch traced here: 188 us
  Pallas kernels  71.4 us (38%)
  starting transfers between devices  41.8 us (22%)
  blocking collectives  39.2 us (21%)
  waiting for transfers between devices  16.3 us (9%)
  local copies, waits for them, and re-layouts  10.4 us (6%)
  other arithmetic  4.53 us (2%)
  between operations  2.97 us (2%)
    pallas_call x12, Pallas kernels, call(): pl.pallas_call(kernel, grid=(steps,), in_specs=[spec(block, where) for _,...  71.4 us
    all_to_all x2, blocking collectives, exchange(): return lax.all_to_all(values, axes, 0, 0, tiled=True)  39.2 us
    ppermute x16, starting transfers between devices, along_x(): return lax.ppermute(values, 'x', [(i, (i + steps) % n) for i in range(n)])  19.9 us
    all_to_all x3, starting transfers between devices, exchange(): return lax.all_to_all(values, axes, 0, 0, tiled=True)  19.3 us
    all_to_all x3, waiting for transfers between devices, exchange(): return lax.all_to_all(values, axes, 0, 0, tiled=True)  11.2 us
    ppermute x16, waiting for transfers between devices, along_x(): return lax.ppermute(values, 'x', [(i, (i + steps) % n) for i in range(n)])  5.01 us
    unnamed x42, local copies, waits for them, and re-layouts  4.74 us
  transfers between devices with their start and end apart: 20, of which 4 were waited for; matrix products, arithmetic and copies ran while one was open for 3% of the time, Pallas kernels for 27%

profile of v2, /device:TPU:1, one launch (start us, length us, event | category | flops | bytes accessed | tf_op | source)
XLA Modules:
  0.0 187.5 jit_solution(1089879855445049875)
XLA Ops:
  0.7 1.8 broadcast_in_dim.41
  2.5 8.6 %all-to-all-start = ((bf16[16,32,768]{2,1,0:T(8,128)(2,1)}), bf16[16,32,768]{2,1,0:T(8,128)(2,1)S(1)}, u32[]{:S(2)}, u32[]{:S(2)}) async-start(bf16[16,32,768]{2,1,0:T(8,128)(2,1)} %broadcast_in_dim.41), calls=%async_computation | async-start | bytes 1572864 | tf_op jit(solution)/shard_map/all_to_all | solution.py:48
  11.1 1.3 collective-permute-start.5
  12.4 1.5 collective-permute-start.4
  13.8 10.0 %all-to-all-done = bf16[16,32,768]{2,1,0:T(8,128)(2,1)S(1)} async-done(((bf16[16,32,768]{2,1,0:T(8,128)(2,1)}), bf16[16,32,768]{2,1,0:T(8,128)(2,1)S(1)}, u32[]{:S(2)}, u32[]{:S(2)}) %all-to-all-start) | async-done | bytes 786464 | tf_op jit(solution)/shard_map/all_to_all | solution.py:48
  23.9 2.5 %collective-permute-start = (bf16[16,32,768]{2,1,0:T(8,128)(2,1)S(1)}, bf16[16,32,768]{2,1,0:T(8,128)(2,1)}, u32[]{:S(2)}, u32[]{:S(2)}) collective-permute-start(bf16[16,32,768]{2,1,0:T(8,128)(2,1)S(1)} %all-to-all-done), channel_id=1, source_target_pairs={{0,1},{1,0},{2,3},{3,2},{4,5},{5,4},{6,7},{7,6},{8,9},{9,8},{10,11... | collective-permute-start | bytes 2359304 | tf_op jit(solution)/shard_map/ppermute | solution.py:26
  26.4 4.0 %collective-permute-done.5.refs_4_.refs_8_ = bf16[512,768]{1,0:T(8,128)(2,1)S(1)} collective-permute-done((bf16[512,768]{1,0:T(8,128)(2,1)S(1)}, bf16[512,768]{1,0:T(8,128)(2,1)S(1)}, u32[]{:S(2)}, u32[]{:S(2)}) %collective-permute-start.5) | collective-permute-done | bytes 786464 | tf_op jit(solution)/shard_map/ppermute | solution.py:31
  30.6 2.7 %collective-permute-start.7 = (bf16[256,768]{1,0:T(8,128)(2,1)S(1)}, bf16[256,768]{1,0:T(8,128)(2,1)S(1)}, u32[]{:S(2)}, u32[]{:S(2)}) collective-permute-start(bf16[256,768]{1,0:T(8,128)(2,1)S(1)} %slice.50), channel_id=1, source_target_pairs={{0,96},{32,0},{64,32},{96,64},{1,97},{33,1},{65,33},{97,65},{2,98}... | collective-permute-start | bytes 1179656 | tf_op jit(solution)/shard_map/ppermute | solution.py:31
  33.4 1.2 select_bitcast_fusion.1
  34.9 0.5 fusion
  35.4 1.0 fusion.5
  36.9 1.4 collective-permute-start.2
  38.3 1.3 collective-permute-start.1
  39.6 0.9 collective-permute-done.6.refs_2_.refs_6_
  40.5 0.5 slice.51
  41.1 0.5 slice.52
  43.0 0.6 fusion.4
  44.8 1.1 broadcast_multiply_fusion
  45.9 3.1 %collective-permute-start.9 = (bf16[512,768]{1,0:T(8,128)(2,1)S(1)}, bf16[512,768]{1,0:T(8,128)(2,1)S(1)}, u32[]{:S(2)}, u32[]{:S(2)}) collective-permute-start(bf16[512,768]{1,0:T(8,128)(2,1)S(1)} %get-tuple-element.45), channel_id=1, source_target_pairs={{0,64},{32,96},{64,0},{96,32},{1,65},{33,97},{65,1},{97,33},{2,66}... | collective-permute-start | bytes 2359304 | tf_op jit(solution)/shard_map/ppermute | solution.py:31
  49.3 0.8 slice_bitcast_fusion.phi_ref
  50.1 6.0 %shard_map.101 = (bf16[256,2048]{1,0:T(8,128)(2,1)}, bf16[256,2048]{1,0:T(8,128)(2,1)}, bf16[256,768]{1,0:T(8,128)(2,1)}, f32[256,768]{1,0:T(8,128)}, f32[256,1]...) custom-call(bf16[256,768]{1,0:T(8,128)(2,1)} %slice_bitcast_fusion.phi_ref, f32[1,2048]{1,0:T(1,128)} %bitcast.70, ...), custom_call_target="tpu_custom_call" | custom-call | flops 1000 | bytes 1000 | tf_op jit(solution)/shard_map/pallas_call | solution.py:91
  56.1 21.5 %all_to_all.25 = bf16[32,8,768]{2,1,0:T(8,128)(2,1)} all-to-all(bf16[32,8,768]{2,1,0:T(8,128)(2,1)} %bitcast.66), channel_id=1, replica_groups=mesh['x'=4,'y'=4,'z'=4,'core'=2] {'y','z','core'}, dimensions={0} | all-to-all | bytes 786432 | tf_op jit(solution)/shard_map/all_to_all | solution.py:48
  77.6 9.5 %shard_map.103 = (bf16[256,3072]{1,0:T(8,128)(2,1)}, bf16[256,3072]{1,0:T(8,128)(2,1)}, bf16[256,768]{1,0:T(8,128)(2,1)}) custom-call(bf16[256,768]{1,0:T(8,128)(2,1)} %bitcast.62, bf16[768,3072]{1,0:T(8,128)(2,1)} %bitcast.43, bf16[3072,768]{1,0:T(8,128)(2,1)} %bitcast.45), custom_call_target="tpu_custom_call" | custom-call | flops 1000 | bytes 1000 | tf_op jit(solution)/shard_map/pallas_call | solution.py:91
  87.1 0.8 copy-done.4
  88.5 3.9 %shard_map.102 = bf16[256,768]{1,0:T(8,128)(2,1)} custom-call(bf16[256,2048]{1,0:T(8,128)(2,1)} %get-tuple-element.25.combine_ref, bf16[512,768]{1,0:T(8,128)(2,1)} %get-tuple-element.46.refs_0_.grad_ref, bf16[512,768]{1,0:T(8,128)(2,1)} %copy-done.6, bf16[512,768]{1,0:T(8,128)(2,1)} %copy-done.5, bf16[512,768]{1,0:T(8,128)(2,1)} %copy-done.4), custom_call_target="tpu_custom_call" | custom-call | flops 1000 | bytes 1000 | tf_op jit(solution)/shard_map/pallas_call | solution.py:91
  92.4 1.0 maximum_bitcast_fusion
  93.5 17.7 %all_to_all.26 = bf16[32,8,1536]{2,1,0:T(8,128)(2,1)} all-to-all(bf16[32,8,1536]{2,1,0:T(8,128)(2,1)S(1)} %maximum_bitcast_fusion), channel_id=1, replica_groups=mesh['x'=4,'y'=4,'z'=4,'core'=2] {'y','z','core'}, dimensions={0} | all-to-all | bytes 1572864 | tf_op jit(solution)/shard_map/all_to_all | solution.py:48
  111.1 9.4 %shard_map.104 = (bf16[256,3072]{1,0:T(8,128)(2,1)}, bf16[256,768]{1,0:T(8,128)(2,1)}) custom-call(bf16[256,1536]{1,0:T(8,128)(2,1)} %bitcast.47, bf16[256,3072]{1,0:T(8,128)(2,1)} %get-tuple-element.28.slope_ref, bf16[768,3072]{1,0:T(8,128)(2,1)} %bitcast.44, bf16[3072,768]{1,0:T(8,128)(2,1)} %bitcast.46), custom_call_target="tpu_custom_call" | custom-call | flops 1000 | bytes 1000 | tf_op jit(solution)/shard_map/pallas_call | solution.py:91
  120.5 4.9 %shard_map.105 = (f32[256,2048]{1,0:T(8,128)}, bf16[272,768]{1,0:T(8,128)(2,1)}) custom-call(bf16[256,1536]{1,0:T(8,128)(2,1)} %bitcast.48, bf16[256,768]{1,0:T(8,128)(2,1)} %get-tuple-element.29._, bf16[256,2048]{1,0:T(8,128)(2,1)} %get-tuple-element.25.combine_ref, f32[256,1]{1,0:T(8,128)} %get-tuple-element.30.top_ref, ...), custom_call_target="tpu_custom_call" | custom-call | flops 1000 | bytes 1000 | tf_op jit(solution)/shard_map/pallas_call | solution.py:91
  125.4 0.8 collective-permute-start.13
  126.2 4.1 %all-to-all-start.3 = ((bf16[32,8,768]{2,1,0:T(8,128)(2,1)}), bf16[32,8,768]{2,1,0:T(8,128)(2,1)S(1)}, u32[]{:S(2)}, u32[]{:S(2)}) async-start(bf16[32,8,768]{2,1,0:T(8,128)(2,1)} %bitcast.23), calls=%async_computation.3 | async-start | bytes 786432 | tf_op jit(solution)/shard_map/all_to_all | solution.py:48
  130.4 2.5 %collective-permute-start.12 = (bf16[272,768]{1,0:T(8,128)(2,1)}, bf16[272,768]{1,0:T(8,128)(2,1)S(1)}, u32[]{:S(2)}, u32[]{:S(2)}) collective-permute-start(bf16[272,768]{1,0:T(8,128)(2,1)} %get-tuple-element.32.refs_0_), channel_id=1, source_target_pairs={{0,64},{32,96},{64,0},{96,32},{1,65},{33,97},{65,1},{97,33},{2,66}... | collective-permute-start | bytes 1253384 | tf_op jit(solution)/shard_map/ppermute | solution.py:31
  133.2 6.3 %shard_map.107._ = bf16[3072,768]{1,0:T(8,128)(2,1)} custom-call(bf16[256,3072]{1,0:T(8,128)(2,1)} %get-tuple-element.37.a_ref, bf16[256,1536]{1,0:T(8,128)(2,1)} %bitcast.49), custom_call_target="tpu_custom_call" | custom-call | flops 1000 | bytes 1000 | tf_op jit(solution)/shard_map/pallas_call | solution.py:91
  139.4 1.2 all-to-all-done.3
  140.7 0.7 copy-done.13
  141.4 2.6 %shard_map.108 = (bf16[272,768]{1,0:T(8,128)(2,1)}, f32[256,1]{1,0:T(8,128)}) custom-call(bf16[256,768]{1,0:T(8,128)(2,1)} %bitcast.65, f32[256,768]{1,0:T(8,128)} %get-tuple-element.35.normed_ref, f32[256,1]{1,0:T(8,128)} %get-tuple-element.36.factor_ref, bf16[3072,768]{1,0:T(8,128)(2,1)} %shard_map.107._), custom_call_target="tpu_custom_call" | custom-call | flops 1000 | bytes 1000 | tf_op jit(solution)/shard_map/pallas_call | solution.py:91
  144.3 2.7 %collective-permute-start.15 = (bf16[272,768]{1,0:T(8,128)(2,1)}, bf16[272,768]{1,0:T(8,128)(2,1)S(1)}, u32[]{:S(2)}, u32[]{:S(2)}) collective-permute-start(bf16[272,768]{1,0:T(8,128)(2,1)} %get-tuple-element.38.refs_4_.grad_ref), channel_id=1, source_target_pairs={{0,64},{32,96},{64,0},{96,32},{1,65},{33,97},{65,1},{97,33},{2,66}... | collective-permute-start | bytes 1253384 | tf_op jit(solution)/shard_map/ppermute | solution.py:31
  147.0 1.5 collective-permute-start.14
  148.5 6.2 %shard_map.112 = bf16[768,3072]{1,0:T(8,128)(2,1)} custom-call(bf16[256,768]{1,0:T(8,128)(2,1)} %bitcast.63, bf16[256,3072]{1,0:T(8,128)(2,1)} %get-tuple-element.44.b_ref), custom_call_target="tpu_custom_call" | custom-call | flops 1000 | bytes 1000 | tf_op jit(solution)/shard_map/pallas_call | solution.py:91
  154.8 0.8 copy-done.8
  155.7 6.4 %shard_map.110 = bf16[256,768]{1,0:T(8,128)(2,1)} custom-call(bf16[272,768]{1,0:T(8,128)(2,1)} %get-tuple-element.38.refs_4_.grad_ref, bf16[256,2048]{1,0:T(8,128)(2,1)} %get-tuple-element.25.combine_ref, f32[256,2048]{1,0:T(8,128)} %get-tuple-element.40.combine_grad_ref, bf16[256,2048]{1,0:T(8,128)(2,1)} %get-tuple-element.41.weights_ref, ...), custom_call_target="tpu_custom_call" | custom-call | flops 1000 | bytes 1000 | tf_op jit(solution)/shard_map/pallas_call | solution.py:91
  162.1 6.6 %all-to-all-start.4 = ((bf16[32,8,768]{2,1,0:T(8,128)(2,1)}), bf16[32,8,768]{2,1,0:T(8,128)(2,1)S(1)}, u32[]{:S(2)}, u32[]{:S(2)}) async-start(bf16[32,8,768]{2,1,0:T(8,128)(2,1)} %bitcast.64), calls=%async_computation.4 | async-start | bytes 786432 | tf_op jit(solution)/shard_map/all_to_all | solution.py:48
  168.7 0.8 broadcast_in_dim.38.live_ref
  169.5 7.1 %shard_map.106 = (bf16[512,768]{1,0:T(8,128)(2,1)}, bf16[512,1024]{1,0:T(8,128)(2,1)}) custom-call(f32[512,128]{1,0:T(8,128)} %broadcast_in_dim.38.live_ref, bf16[512,768]{1,0:T(8,128)(2,1)} %bitcast.55, bf16[512,768]{1,0:T(8,128)(2,1)} %get-tuple-element.46.refs_0_.grad_ref, bf16[1024,768]{1,0:T(8,128)(2,1)} %bitcast.51, ...), custom_call_target="tpu_custom_call" | custom-call | flops 1000 | bytes 1000 | tf_op jit(solution)/shard_map/pallas_call | solution.py:91
  176.7 0.7 copy-done.18
  177.7 7.4 %shard_map.109 = (bf16[512,768]{1,0:T(8,128)(2,1)}, f32[8,128]{1,0:T(8,128)}) custom-call(f32[512,128]{1,0:T(8,128)} %broadcast_in_dim.38.live_ref, bf16[512,1024]{1,0:T(8,128)(2,1)} %get-tuple-element.34.logit_ref, bf16[512,768]{1,0:T(8,128)(2,1)} %bitcast.56, bf16[1024,768]{1,0:T(8,128)(2,1)} %bitcast.52, bf16[272,768]{1,0:T(8,128)(2,1)} %get-tuple-element.32.refs_0_, ...), custom_call_target="tpu_custom_call" | custom-call | flops 5000000000 | bytes 1000 | tf_op jit(solution)/shard_map/pallas_call | solution.py:91
  185.1 0.7 copy-done.12
  185.8 1.7 shard_map.111
  (70 shorter events, 3.5 us)
Async XLA Ops:
  0.6 10.5 %copy-start.1 = (bf16[1,512,768]{2,1,0:T(8,128)(2,1)S(1)}, bf16[1,512,768]{2,1,0:T(8,128)(2,1)}, u32[]{:S(2)}) copy-start(bf16[1,512,768]{2,1,0:T(8,128)(2,1)} %param.6) | copy-start | bytes 2359300
  0.6 25.8 %copy-start.17 = (s32[1,512]{1,0:T(1,128)S(1)}, s32[1,512]{1,0:T(1,128)}, u32[]{:S(2)}) copy-start(s32[1,512]{1,0:T(1,128)} %param.7) | copy-start | bytes 6148
  2.5 21.4 %all-to-all-start = ((bf16[16,32,768]{2,1,0:T(8,128)(2,1)}), bf16[16,32,768]{2,1,0:T(8,128)(2,1)S(1)}, u32[]{:S(2)}, u32[]{:S(2)}) async-start(bf16[16,32,768]{2,1,0:T(8,128)(2,1)} %broadcast_in_dim.41), calls=%async_computation | async-start | bytes 1572864 | tf_op jit(solution)/shard_map/all_to_all | solution.py:48
  11.1 19.4 %collective-permute-start.5 = (bf16[512,768]{1,0:T(8,128)(2,1)S(1)}, bf16[512,768]{1,0:T(8,128)(2,1)S(1)}, u32[]{:S(2)}, u32[]{:S(2)}) collective-permute-start(bf16[512,768]{1,0:T(8,128)(2,1)S(1)} %bitcast.57), channel_id=1, source_target_pairs={{0,32},{32,64},{64,96},{96,0},{1,33},{33,65},{65,97},{97,1},{2,34}... | collective-permute-start | bytes 2359304 | tf_op jit(solution)/shard_map/ppermute | solution.py:31
  12.4 18.2 %collective-permute-start.4 = (bf16[512,768]{1,0:T(8,128)(2,1)S(1)}, bf16[512,768]{1,0:T(8,128)(2,1)S(1)}, u32[]{:S(2)}, u32[]{:S(2)}) collective-permute-start(bf16[512,768]{1,0:T(8,128)(2,1)S(1)} %bitcast.58), channel_id=1, source_target_pairs={{0,96},{32,0},{64,32},{96,64},{1,97},{33,1},{65,33},{97,65},{2,98}... | collective-permute-start | bytes 2359304 | tf_op jit(solution)/shard_map/ppermute | solution.py:31
  23.9 9.5 %collective-permute-start = (bf16[16,32,768]{2,1,0:T(8,128)(2,1)S(1)}, bf16[16,32,768]{2,1,0:T(8,128)(2,1)}, u32[]{:S(2)}, u32[]{:S(2)}) collective-permute-start(bf16[16,32,768]{2,1,0:T(8,128)(2,1)S(1)} %all-to-all-done), channel_id=1, source_target_pairs={{0,1},{1,0},{2,3},{3,2},{4,5},{5,4},{6,7},{7,6},{8,9},{9,8},{10,11... | collective-permute-start | bytes 2359304 | tf_op jit(solution)/shard_map/ppermute | solution.py:26
  30.5 4.1 %copy-start.2 = (bf16[512,768]{1,0:T(8,128)(2,1)}, bf16[512,768]{1,0:T(8,128)(2,1)S(1)}, u32[]{:S(2)}) copy-start(bf16[512,768]{1,0:T(8,128)(2,1)S(1)} %collective-permute-done.5.refs_4_.refs_8_) | copy-start | bytes 2359300
  30.5 10.0 %collective-permute-start.6 = (bf16[256,768]{1,0:T(8,128)(2,1)S(1)}, bf16[256,768]{1,0:T(8,128)(2,1)S(1)}, u32[]{:S(2)}, u32[]{:S(2)}) collective-permute-start(bf16[256,768]{1,0:T(8,128)(2,1)S(1)} %slice.49), channel_id=1, source_target_pairs={{0,32},{32,64},{64,96},{96,0},{1,33},{33,65},{65,97},{97,1},{2,34}... | collective-permute-start | bytes 1179656 | tf_op jit(solution)/shard_map/ppermute | solution.py:31
  30.6 4.0 %copy-start.3 = (bf16[512,768]{1,0:T(8,128)(2,1)}, bf16[512,768]{1,0:T(8,128)(2,1)S(1)}, u32[]{:S(2)}) copy-start(bf16[512,768]{1,0:T(8,128)(2,1)S(1)} %collective-permute-done.4.refs_1_.refs_5_) | copy-start | bytes 2359300
  30.6 10.4 %collective-permute-start.7 = (bf16[256,768]{1,0:T(8,128)(2,1)S(1)}, bf16[256,768]{1,0:T(8,128)(2,1)S(1)}, u32[]{:S(2)}, u32[]{:S(2)}) collective-permute-start(bf16[256,768]{1,0:T(8,128)(2,1)S(1)} %slice.50), channel_id=1, source_target_pairs={{0,96},{32,0},{64,32},{96,64},{1,97},{33,1},{65,33},{97,65},{2,98}... | collective-permute-start | bytes 1179656 | tf_op jit(solution)/shard_map/ppermute | solution.py:31
  35.4 13.9 %copy-start = (bf16[4,256,768]{2,1,0:T(8,128)(2,1)}, bf16[4,256,768]{2,1,0:T(8,128)(2,1)S(1)}, u32[]{:S(2)}) copy-start(bf16[4,256,768]{2,1,0:T(8,128)(2,1)S(1)} %fusion) | copy-start | bytes 4718596
  36.5 8.3 %copy-start.14 = (bf16[1,512,768]{2,1,0:T(8,128)(2,1)S(1)}, bf16[1,512,768]{2,1,0:T(8,128)(2,1)}, u32[]{:S(2)}) copy-start(bf16[1,512,768]{2,1,0:T(8,128)(2,1)} %param.11) | copy-start | bytes 2359300
  36.8 6.1 %collective-permute-start.3 = (f32[2,4,128]{2,1,0:T(4,128)S(1)}, f32[2,4,128]{2,1,0:T(4,128)S(1)}, u32[]{:S(2)}, u32[]{:S(2)}) collective-permute-start(f32[2,4,128]{2,1,0:T(4,128)S(1)} %pad_maximum_fusion.2), channel_id=1, source_target_pairs={{0,32},{32,64},{64,96},{96,0},{1,33},{33,65},{65,97},{97,1},{2,34}... | collective-permute-start | bytes 12296 | tf_op jit(solution)/shard_map/ppermute | solution.py:31
  36.9 6.0 %collective-permute-start.2 = (f32[2,4,128]{2,1,0:T(4,128)S(1)}, f32[2,4,128]{2,1,0:T(4,128)S(1)}, u32[]{:S(2)}, u32[]{:S(2)}) collective-permute-start(f32[2,4,128]{2,1,0:T(4,128)S(1)} %pad_maximum_fusion.2), channel_id=1, source_target_pairs={{0,64},{32,96},{64,0},{96,32},{1,65},{33,97},{65,1},{97,33},{2,66}... | collective-permute-start | bytes 12296 | tf_op jit(solution)/shard_map/ppermute | solution.py:31
  38.3 4.7 %collective-permute-start.1 = (f32[2,4,128]{2,1,0:T(4,128)S(1)}, f32[2,4,128]{2,1,0:T(4,128)S(1)}, u32[]{:S(2)}, u32[]{:S(2)}) collective-permute-start(f32[2,4,128]{2,1,0:T(4,128)S(1)} %pad_maximum_fusion.2), channel_id=1, source_target_pairs={{0,96},{32,0},{64,32},{96,64},{1,97},{33,1},{65,33},{97,65},{2,98}... | collective-permute-start | bytes 12296 | tf_op jit(solution)/shard_map/ppermute | solution.py:31
  40.5 9.6 %copy-start.10 = (bf16[256,768]{1,0:T(8,128)(2,1)}, bf16[256,768]{1,0:T(8,128)(2,1)S(1)}, u32[]{:S(2)}) copy-start(bf16[256,768]{1,0:T(8,128)(2,1)S(1)} %collective-permute-done.6.refs_2_.refs_6_) | copy-start | bytes 1179652
  41.1 9.0 %copy-start.11 = (bf16[256,768]{1,0:T(8,128)(2,1)}, bf16[256,768]{1,0:T(8,128)(2,1)S(1)}, u32[]{:S(2)}) copy-start(bf16[256,768]{1,0:T(8,128)(2,1)S(1)} %collective-permute-done.7.refs_3_.refs_7_) | copy-start | bytes 1179652
  43.6 6.5 %copy-start.16 = (f32[1,16,128]{2,1,0:T(8,128)}, f32[1,16,128]{2,1,0:T(8,128)S(1)}, u32[]{:S(2)}) copy-start(f32[1,16,128]{2,1,0:T(8,128)S(1)} %get-tuple-element.50) | copy-start | bytes 24580
  45.8 41.2 %collective-permute-start.10 = (bf16[512,768]{1,0:T(8,128)(2,1)S(1)}, bf16[512,768]{1,0:T(8,128)(2,1)S(1)}, u32[]{:S(2)}, u32[]{:S(2)}) collective-permute-start(bf16[512,768]{1,0:T(8,128)(2,1)S(1)} %get-tuple-element.45), channel_id=1, source_target_pairs={{0,32},{32,64},{64,96},{96,0},{1,33},{33,65},{65,97},{97,1},{2,34}... | collective-permute-start | bytes 2359304 | tf_op jit(solution)/shard_map/ppermute | solution.py:31
  45.9 41.2 %collective-permute-start.9 = (bf16[512,768]{1,0:T(8,128)(2,1)S(1)}, bf16[512,768]{1,0:T(8,128)(2,1)S(1)}, u32[]{:S(2)}, u32[]{:S(2)}) collective-permute-start(bf16[512,768]{1,0:T(8,128)(2,1)S(1)} %get-tuple-element.45), channel_id=1, source_target_pairs={{0,64},{32,96},{64,0},{96,32},{1,65},{33,97},{65,1},{97,33},{2,66}... | collective-permute-start | bytes 2359304 | tf_op jit(solution)/shard_map/ppermute | solution.py:31
  49.0 38.1 %collective-permute-start.8 = (bf16[512,768]{1,0:T(8,128)(2,1)S(1)}, bf16[512,768]{1,0:T(8,128)(2,1)S(1)}, u32[]{:S(2)}, u32[]{:S(2)}) collective-permute-start(bf16[512,768]{1,0:T(8,128)(2,1)S(1)} %get-tuple-element.45), channel_id=1, source_target_pairs={{0,96},{32,0},{64,32},{96,64},{1,97},{33,1},{65,33},{97,65},{2,98}... | collective-permute-start | bytes 2359304 | tf_op jit(solution)/shard_map/ppermute | solution.py:31
  87.1 0.9 copy-start.4
  87.1 1.1 copy-start.5
  87.1 1.4 copy-start.6
  88.5 4.0 %copy-start.15 = (bf16[256,768]{1,0:T(8,128)(2,1)S(1)}, bf16[256,768]{1,0:T(8,128)(2,1)}, u32[]{:S(2)}) copy-start(bf16[256,768]{1,0:T(8,128)(2,1)} %get-tuple-element.27) | copy-start | bytes 1179652
  125.4 21.6 %collective-permute-start.13 = (bf16[272,768]{1,0:T(8,128)(2,1)}, bf16[272,768]{1,0:T(8,128)(2,1)S(1)}, u32[]{:S(2)}, u32[]{:S(2)}) collective-permute-start(bf16[272,768]{1,0:T(8,128)(2,1)} %get-tuple-element.32.refs_0_), channel_id=1, source_target_pairs={{0,32},{32,64},{64,96},{96,0},{1,33},{33,65},{65,97},{97,1},{2,34}... | collective-permute-start | bytes 1253384 | tf_op jit(solution)/shard_map/ppermute | solution.py:31
  126.2 14.4 %all-to-all-start.3 = ((bf16[32,8,768]{2,1,0:T(8,128)(2,1)}), bf16[32,8,768]{2,1,0:T(8,128)(2,1)S(1)}, u32[]{:S(2)}, u32[]{:S(2)}) async-start(bf16[32,8,768]{2,1,0:T(8,128)(2,1)} %bitcast.23), calls=%async_computation.3 | async-start | bytes 786432 | tf_op jit(solution)/shard_map/all_to_all | solution.py:48
  130.4 24.4 %collective-permute-start.12 = (bf16[272,768]{1,0:T(8,128)(2,1)}, bf16[272,768]{1,0:T(8,128)(2,1)S(1)}, u32[]{:S(2)}, u32[]{:S(2)}) collective-permute-start(bf16[272,768]{1,0:T(8,128)(2,1)} %get-tuple-element.32.refs_0_), channel_id=1, source_target_pairs={{0,64},{32,96},{64,0},{96,32},{1,65},{33,97},{65,1},{97,33},{2,66}... | collective-permute-start | bytes 1253384 | tf_op jit(solution)/shard_map/ppermute | solution.py:31
  132.9 21.9 %collective-permute-start.11 = (bf16[272,768]{1,0:T(8,128)(2,1)}, bf16[272,768]{1,0:T(8,128)(2,1)S(1)}, u32[]{:S(2)}, u32[]{:S(2)}) collective-permute-start(bf16[272,768]{1,0:T(8,128)(2,1)} %get-tuple-element.32.refs_0_), channel_id=1, source_target_pairs={{0,96},{32,0},{64,32},{96,64},{1,97},{33,1},{65,33},{97,65},{2,98}... | collective-permute-start | bytes 1253384 | tf_op jit(solution)/shard_map/ppermute | solution.py:31
  140.7 0.7 copy-start.13
  144.0 32.6 %collective-permute-start.16 = (bf16[272,768]{1,0:T(8,128)(2,1)}, bf16[272,768]{1,0:T(8,128)(2,1)S(1)}, u32[]{:S(2)}, u32[]{:S(2)}) collective-permute-start(bf16[272,768]{1,0:T(8,128)(2,1)} %get-tuple-element.38.refs_4_.grad_ref), channel_id=1, source_target_pairs={{0,32},{32,64},{64,96},{96,0},{1,33},{33,65},{65,97},{97,1},{2,34}... | collective-permute-start | bytes 1253384 | tf_op jit(solution)/shard_map/ppermute | solution.py:31
  144.3 32.3 %collective-permute-start.15 = (bf16[272,768]{1,0:T(8,128)(2,1)}, bf16[272,768]{1,0:T(8,128)(2,1)S(1)}, u32[]{:S(2)}, u32[]{:S(2)}) collective-permute-start(bf16[272,768]{1,0:T(8,128)(2,1)} %get-tuple-element.38.refs_4_.grad_ref), channel_id=1, source_target_pairs={{0,64},{32,96},{64,0},{96,32},{1,65},{33,97},{65,1},{97,33},{2,66}... | collective-permute-start | bytes 1253384 | tf_op jit(solution)/shard_map/ppermute | solution.py:31
  147.0 7.8 %copy-start.7 = (bf16[272,768]{1,0:T(8,128)(2,1)}, bf16[272,768]{1,0:T(8,128)(2,1)S(1)}, u32[]{:S(2)}) copy-start(bf16[272,768]{1,0:T(8,128)(2,1)S(1)} %collective-permute-done.13.refs_3_) | copy-start | bytes 1253380
  147.0 29.7 %collective-permute-start.14 = (bf16[272,768]{1,0:T(8,128)(2,1)}, bf16[272,768]{1,0:T(8,128)(2,1)S(1)}, u32[]{:S(2)}, u32[]{:S(2)}) collective-permute-start(bf16[272,768]{1,0:T(8,128)(2,1)} %get-tuple-element.38.refs_4_.grad_ref), channel_id=1, source_target_pairs={{0,96},{32,0},{64,32},{96,64},{1,97},{33,1},{65,33},{97,65},{2,98}... | collective-permute-start | bytes 1253384 | tf_op jit(solution)/shard_map/ppermute | solution.py:31
  154.8 0.8 copy-start.8
  154.8 0.9 copy-start.9
  162.1 23.0 %all-to-all-start.4 = ((bf16[32,8,768]{2,1,0:T(8,128)(2,1)}), bf16[32,8,768]{2,1,0:T(8,128)(2,1)S(1)}, u32[]{:S(2)}, u32[]{:S(2)}) async-start(bf16[32,8,768]{2,1,0:T(8,128)(2,1)} %bitcast.64), calls=%async_computation.4 | async-start | bytes 786432 | tf_op jit(solution)/shard_map/all_to_all | solution.py:48
  176.6 0.7 copy-start.18
  176.7 0.9 copy-start.19
  176.7 1.0 copy-start.20
  185.1 0.7 copy-start.12

commit v3 on v2

--- a/solution.py
+++ b/solution.py
@@ -39,11 +39,6 @@
     return along_x(values, -1), along_x(values, 1)
 
 
-def pass_on(ahead, behind):
-    half = ahead.shape[0] // 2
-    return along_x(behind[:half], 1), along_x(ahead[half:], -1)
-
-
 def exchange(values, axes):
     return lax.all_to_all(values, axes, 0, 0, tiled=True)
 
@@ -52,11 +47,11 @@
     return lax.dynamic_slice_in_dim(jnp.concatenate([blocks, blocks[:-1]]), first, blocks.shape[0], 0)
 
 
-def gather_phi(phi):
+def gather_phi(phi, one):
     rows = phi.T
     planes = lax.axis_size("x")
     chips = lax.axis_size("y") * lax.axis_size("z")
-    mine = exchange(jnp.broadcast_to(rows[None], (chips,) + rows.shape), PLANE)
+    mine = exchange(jnp.broadcast_to(rows[None], (chips,) + rows.shape), PLANE) * one
     other = swap_cores(mine)
     first = lax.axis_index("core") == 0
     both = jnp.stack([jnp.where(first, mine, other), jnp.where(first, other, mine)], axis=1)
@@ -125,14 +120,15 @@
     accumulate(total, jnp.dot(hidden, down_ref[...], preferred_element_type=F32), out_ref)
 
 
-def backward_kernel(grad_ref, slope_ref, up_ref, down_ref, pre_ref, out_ref, total):
+def backward_kernel(grad_ref, slope_ref, up_ref, down_ref, _, pre_ref, out_ref, total):
     pre_grad = (slope_ref[...].astype(F32) * matmul(grad_ref[...], down_ref[...], (1, 1))).astype(BF16)
     pre_ref[...] = pre_grad
     accumulate(total, matmul(pre_grad, up_ref[...], (1, 1)), out_ref)
 
 
-def product_kernel(a_ref, b_ref, out_ref):
-    out_ref[...] = matmul(a_ref[...], b_ref[...], (0, 0)).astype(BF16)
+def weights_kernel(rows_ref, grad_ref, hidden_ref, pre_ref, up_ref, down_ref):
+    up_ref[...] = matmul(rows_ref[...], pre_ref[...], (0, 0)).astype(BF16)
+    down_ref[...] = matmul(hidden_ref[...], grad_ref[...], (0, 0)).astype(BF16)
 
 
 def dispatch_kernel(
@@ -170,13 +166,44 @@
     top_ref[...] = top
 
 
-def slot_kernel(combine_ref, *refs):
+def slot_kernel(combine_ref, output_ref, *refs):
     *pieces, out_ref = refs
     total, at = 0.0, 0
     for p in pieces:
         total += jnp.dot(combine_ref[:, at : at + p.shape[0]], p[...], preferred_element_type=F32)
         at += p.shape[0]
-    out_ref[...] = total.astype(BF16)
+    width = total.shape[1]
+    out_ref[:, :width] = total.astype(BF16)
+    out_ref[:, width:] = output_ref[...]
+
+
+def halves_kernel(ahead_ref, behind_ref, ahead_out_ref, behind_out_ref):
+    ahead_out_ref[...] = ahead_ref[...]
+    behind_out_ref[...] = behind_ref[...]
+
+
+def mask_kernel(live_ref, grad_ref, *refs):
+    refs[-1][...] = jnp.where(live_ref[:, :1] > 0.0, grad_ref[...].astype(F32), 0.0).astype(BF16)
+
+
+def softmax_kernel(live_ref, tokens_ref, phi_ref, _, out_ref):
+    logits = matmul(tokens_ref[...], phi_ref[...], (1, 1))
+    powers = jnp.exp(logits - jnp.max(logits, axis=1, keepdims=True))
+    scale = live_ref[:, :1] / jnp.sum(powers, axis=1, keepdims=True)
+    out_ref[...] = (powers * scale).astype(BF16)
+
+
+def row_sum_kernel(*refs):
+    *messages, out_ref = refs
+    width = out_ref.shape[1] // len(messages)
+    messages = [m[...].astype(F32) for m in messages]
+    for line in range(len(messages)):
+        rows = 0.0
+        for k, m in enumerate(messages):
+            for j in range(3):
+                i = 4 * j + (line - k) % 4
+                rows += m[i : i + 1, :width]
+        out_ref[:, line * width : (line + 1) * width] = rows
 
 
 def split(values):
@@ -214,7 +241,7 @@
     message_ref[slots:, :] = lines[...].astype(BF16)
 
 
-def mixed_grad_kernel(back_ref, normed_ref, factor_ref, _, out_ref, column_ref):
+def mixed_grad_kernel(back_ref, normed_ref, factor_ref, _down, _up, out_ref, column_ref):
     back = back_ref[...].astype(F32)
     normed, factor = normed_ref[...], factor_ref[...]
     out = (factor * (back - normed * jnp.mean(back * normed, axis=1, keepdims=True))).astype(BF16)
@@ -226,21 +253,14 @@
     out_ref[slots:, :] = jnp.broadcast_to(row, (16, row.shape[1])).astype(BF16)
 
 
-def phi_kernel(grad_ref, combine_ref, combine_grad_ref, weights_ref, inverse_ref, column_ref, *refs):
-    messages, pieces, out_ref = refs[:4], refs[4:9], refs[9]
+def phi_kernel(grad_ref, combine_ref, combine_grad_ref, row_ref, weights_ref, inverse_ref, column_ref, *refs):
+    *pieces, out_ref = refs
     grad = grad_ref[...]
-    width = pieces[0].shape[0]
-    messages = [m[...].astype(F32) for m in messages]
     total, at = 0.0, 0
     for p in pieces:
         span = slice(at, at + p.shape[0])
-        line, start = at // width, at % width
         at += p.shape[0]
-        rows = 0.0
-        for k, m in enumerate(messages):
-            for j in range(3):
-                i = 4 * j + (line - k) % 4
-                rows += m[i : i + 1, start : start + p.shape[0]]
+        rows = row_ref[:, span]
         tokens = p[...]
         share = weights_ref[:, span].astype(F32) * inverse_ref[...]
         logit_grad = combine_ref[:, span].astype(F32) * (combine_grad_ref[:, span] - rows) + share * (
@@ -250,20 +270,18 @@
     out_ref[...] = total.astype(BF16)
 
 
-def combine_kernel(live_ref, tokens_ref, grad_ref, phi_ref, *refs):
+def combine_kernel(combine_ref, grad_ref, *refs):
     *outs, mixed_ref, logit_ref = refs
     width = outs[0].shape[0]
-    logits = matmul(tokens_ref[...], phi_ref[...], (1, 1))
-    powers = jnp.exp(logits - jnp.max(logits, axis=1, keepdims=True))
-    combine = powers * (1.0 / jnp.sum(powers, axis=1, keepdims=True))
-    combine_b = combine.astype(BF16)
+    combine_b = combine_ref[...]
     mixed = sum(
         jnp.dot(combine_b[:, k * width : (k + 1) * width], o[...], preferred_element_type=F32)
         for k, o in enumerate(outs)
     )
-    mixed_ref[...] = jnp.where(live_ref[:, :1] > 0.0, mixed, 0.0).astype(BF16)
+    mixed_ref[...] = mixed.astype(BF16)
     grad = grad_ref[...]
     combine_grad = jnp.concatenate([matmul(grad, o[...], (1, 1)) for o in outs], axis=1)
+    combine = combine_b.astype(F32)
     product = combine * combine_grad
     logit_ref[...] = (product - combine * jnp.sum(product, axis=1, keepdims=True)).astype(BF16)
 
@@ -296,25 +314,29 @@
     out_ref[...] = jnp.sum(parts_ref[...].astype(F32), axis=0) + zero_ref[:, :1]
 
 
+def whole(array):
+    return (array, array.shape, None)
+
+
+def made(kind, *shape):
+    return (kind, shape, shape, None)
+
+
 def per_device(tokens, halt_steps, phi, w_up, w_down, cotangent):
     clip_part = tokens[0]
     rows, features = clip_part.shape
     planes = lax.axis_size("x")
     experts = lax.axis_size("y") * lax.axis_size("z") * lax.axis_size("core")
-    live_rows = (halt_steps[0] > LAYER_POS)[:, None]
-    masked_grad = jnp.where(live_rows, cotangent[0], jnp.zeros((), BF16))
-    live_rows = live_rows.astype(F32)
+    live_rows = (halt_steps[0] > LAYER_POS)[:, None].astype(F32)
     live_wide = jnp.broadcast_to(live_rows, (rows, 128))
 
-    def whole(array):
-        return (array, array.shape, None)
-
-    def made(kind, *shape):
-        return (kind, shape, shape, None)
-
     ahead, behind = to_neighbours(clip_part)
-    far = pass_on(ahead, behind)
-    phi_groups = gather_phi(phi)
+    half = (rows // 2, features)
+    ahead_half, behind_half = call(
+        halves_kernel, 1, [(ahead, half, (1, 0)), (behind, half, (0, 0))], [made(BF16, *half)] * 2, work=10**10
+    )
+    far = along_x(behind_half, 1), along_x(ahead_half, -1)
+    phi_groups = gather_phi(phi, unit(ahead_half))
     own_slots = phi_groups.shape[1]
     per_expert = own_slots // experts
     phi_all = phi_groups.reshape(-1, features)
@@ -326,7 +348,15 @@
     message = jnp.stack([top, norm]).reshape(2, -1, 128)
     row_stats = jnp.concatenate(gather_x(message), axis=1).reshape(2, 1, -1)
 
-    grad_pieces = [masked_grad] + gather_x(masked_grad * unit(far[0], far[1], row_stats[0]))[1:]
+    (masked_grad,) = call(
+        mask_kernel,
+        1,
+        [whole(live_wide), whole(cotangent[0])]
+        + [(f, (16, 128), None) for f in far]
+        + [(message, (2, 4, 128), None)],
+        [made(BF16, rows, features)],
+    )
+    grad_pieces = gather_x(masked_grad)
     pieces = [clip_part, ahead, *far, behind]
     clip_rows = planes * rows
 
@@ -352,7 +382,7 @@
 
     up_matrix, down_matrix = w_up[0], w_down[0]
     hid = up_matrix.shape[1]
-    steps = 6
+    steps = 4
     tile = hid // steps
     expert_rows = expert_in.shape[0]
     block, wide = (expert_rows, features), (expert_rows, tile)
@@ -365,51 +395,70 @@
         [(BF16, (expert_rows, hid), wide, 1), (BF16, (expert_rows, hid), wide, 1), made(BF16, *block)],
         total,
     )
-    (slot_grad,) = call(
-        slot_kernel, 1, [whole(own_combine), *map(whole, grad_pieces)], [made(BF16, own_slots, features)]
-    )
-    arrived = exchange(rows_of(jnp.concatenate([slot_grad, output], axis=1)), GROUP).reshape(own_slots, -1)
+    (message,) = call(
+        slot_kernel,
+        1,
+        [whole(own_combine), whole(output), *map(whole, grad_pieces)],
+        [made(BF16, own_slots, 2 * features)],
+    )
+    arrived = exchange(rows_of(message), GROUP).reshape(own_slots, -1)
+    part = 256
+    thin, lanes = (part, features), (part, 128)
+    (combine,) = call(
+        softmax_kernel,
+        rows // part,
+        [(live_wide, lanes, 0), (clip_part, thin, 0), whole(phi_all), (output, (16, 128), None)],
+        [(BF16, (rows, slots), (part, slots), 0)],
+    )
+
+    slot_combine_grad, message = call(
+        slot_grad_kernel,
+        1,
+        [
+            (arrived, block, (0, 1)),
+            (combine, (16, 128), None),
+            *map(whole, (own_combine, slot_top, inverse)),
+            *map(whole, grad_pieces),
+        ],
+        [made(F32, own_slots, clip_rows), made(BF16, own_slots + 16, features)],
+        [pltpu.VMEM((16, features), F32)],
+    )
+    slot_outs = gather_x(message)
+    tails = [(m, (16, features), (own_slots // 16, 0)) for m in slot_outs]
 
     pre_grad, normed_grad = call(
         backward_kernel,
         steps,
-        [(arrived, block, (0, 0)), (slope, wide, 1), up, down],
+        [
+            (arrived, block, (0, 0)),
+            (slope, wide, 1),
+            up,
+            down,
+            (message, (16, 128), None),
+        ],
         [(BF16, (expert_rows, hid), wide, 1), made(BF16, *block)],
         total,
     )
     back_grad = exchange(rows_of(normed_grad), GROUP).reshape(own_slots, features)
-    (grad_down,) = call(
-        product_kernel,
+    grad_up, grad_down = call(
+        weights_kernel,
         steps,
-        [(hidden, wide, 1), (arrived, block, (0, 0))],
-        [(BF16, down_matrix.shape, down[1], 0)],
-    )
-    (grad_up,) = call(
-        product_kernel,
-        steps,
-        [whole(expert_in), (pre_grad, wide, 1)],
-        [(BF16, up_matrix.shape, up[1], 1)],
-    )
-
-    slot_combine_grad, message = call(
-        slot_grad_kernel,
-        1,
-        [
-            (arrived, block, (0, 1)),
-            (normed_grad, (16, 128), None),
-            *map(whole, (own_combine, slot_top, inverse)),
-            *map(whole, grad_pieces),
-        ],
-        [made(F32, own_slots, clip_rows), made(BF16, own_slots + 16, features)],
-        [pltpu.VMEM((16, features), F32)],
-    )
-    slot_outs = gather_x(message)
-    tails = [(m, (16, features), (own_slots // 16, 0)) for m in slot_outs]
+        [whole(expert_in), (arrived, block, (0, 0)), (hidden, wide, 1), (pre_grad, wide, 1)],
+        [(BF16, up_matrix.shape, up[1], 1), (BF16, down_matrix.shape, down[1], 0)],
+    )
+
+    (row_sums,) = call(row_sum_kernel, 1, tails, [made(F32, 1, clip_rows)], work=2 * 10**10)
 
     mixed_grad, own_column = call(
         mixed_grad_kernel,
         1,
-        [whole(back_grad), whole(normed), whole(factor), (grad_down, (16, 128), None)],
+        [
+            whole(back_grad),
+            whole(normed),
+            whole(factor),
+            (grad_down, (16, 128), None),
+            (grad_up, (16, 128), None),
+        ],
         [made(BF16, own_slots + 16, features), made(F32, own_slots, 1)],
     )
     all_grads = gather_x(mixed_grad)
@@ -420,26 +469,22 @@
             (mixed_grad, (own_slots, features), None),
             whole(own_combine),
             whole(slot_combine_grad),
+            whole(row_sums),
             whole(weights),
             whole(inverse),
             whole(own_column),
-            *tails,
             *map(whole, pieces),
         ],
         [made(BF16, own_slots, features)],
     )
     arrived_phi = exchange(rows_of(part_phi), GROUP)
 
-    part = 256
-    thin, lanes = (part, features), (part, 128)
     mixed, combine_logit_grad = call(
         combine_kernel,
         rows // part,
         [
-            (live_wide, lanes, 0),
-            (clip_part, thin, 0),
+            (combine, (part, slots), 0),
             (masked_grad, thin, 0),
-            whole(phi_all),
             *[(m, (own_slots, features), None) for m in slot_outs],
         ],
         [(BF16, clip_part.shape, thin, 0), (BF16, (rows, slots), (part, slots), 0)],

time: 189 us -> 183 us (0.968)
  blocking collectives: 39.2 us -> 19.9 us
  waiting for transfers between devices: 16.3 us -> 30.2 us
  other arithmetic: 4.53 us -> 1.34 us
  local copies, waits for them, and re-layouts: 10.4 us -> 12.5 us
    all_to_all x2 -> x1, blocking collectives: 39.2 us -> 19.9 us  [exchange(): return lax.all_to_all(values, axes, 0, 0, tiled=True)]
    ppermute x16, waiting for transfers between devices: 5.01 us -> 16.8 us  [along_x(): return lax.ppermute(values, 'x', [(i, (i + steps) % n) for i in range(n)])]
    all_to_all x3 -> x4, starting transfers between devices: 19.3 us -> 25.6 us  [exchange(): return lax.all_to_all(values, axes, 0, 0, tiled=True)]
    ppermute x16, starting transfers between devices: 19.9 us -> 15.6 us  [along_x(): return lax.ppermute(values, 'x', [(i, (i + steps) % n) for i in range(n)])]
    unnamed x42 -> x44, local copies, waits for them, and re-layouts: 4.74 us -> 7.09 us
    all_to_all x3 -> x4, waiting for transfers between devices: 11.2 us -> 13.1 us  [exchange(): return lax.all_to_all(values, axes, 0, 0, tiled=True)]
    pallas_call x12 -> x15, Pallas kernels: 71.4 us -> 71.9 us  [call(): pl.pallas_call(kernel, grid=(steps,), in_specs=[spec(block, where) for _,...]
  transfers between devices with their start and end apart: 20 -> 21, of which waited for: 4 -> 8; matrix products, arithmetic and copies ran while one was open for 3% -> 4% of each run, Pallas kernels for 27% -> 34%
where the time goes in v3:
time: 183 us; the launch traced here: 182 us
  Pallas kernels  71.9 us (39%)
  starting transfers between devices  43.2 us (24%)
  waiting for transfers between devices  30.2 us (17%)
  blocking collectives  19.9 us (11%)
  local copies, waits for them, and re-layouts  12.5 us (7%)
    pallas_call x15, Pallas kernels, call(): pl.pallas_call(kernel, grid=(steps,), in_specs=[spec(block, where) for _,...  71.9 us
    all_to_all x4, starting transfers between devices, exchange(): return lax.all_to_all(values, axes, 0, 0, tiled=True)  25.6 us
    all_to_all x1, blocking collectives, exchange(): return lax.all_to_all(values, axes, 0, 0, tiled=True)  19.9 us
    ppermute x16, waiting for transfers between devices, along_x(): return lax.ppermute(values, 'x', [(i, (i + steps) % n) for i in range(n)])  16.8 us
    ppermute x16, starting transfers between devices, along_x(): return lax.ppermute(values, 'x', [(i, (i + steps) % n) for i in range(n)])  15.6 us
    all_to_all x4, waiting for transfers between devices, exchange(): return lax.all_to_all(values, axes, 0, 0, tiled=True)  13.1 us
    unnamed x44, local copies, waits for them, and re-layouts  7.09 us
  transfers between devices with their start and end apart: 21, of which 8 were waited for; matrix products, arithmetic and copies ran while one was open for 4% of the time, Pallas kernels for 34%

profile of v3, /device:TPU:1, one launch (start us, length us, event | category | flops | bytes accessed | tf_op | source)
XLA Modules:
  0.0 181.6 jit_solution(11001475743240408800)
XLA Ops:
  0.6 3.4 %collective-permute-start = (bf16[512,768]{1,0:T(8,128)(2,1)}, bf16[512,768]{1,0:T(8,128)(2,1)S(1)}, u32[]{:S(2)}, u32[]{:S(2)}) collective-permute-start(bf16[512,768]{1,0:T(8,128)(2,1)} %bitcast.50), channel_id=1, source_target_pairs={{0,96},{32,0},{64,32},{96,64},{1,97},{33,1},{65,33},{97,65},{2,98}... | collective-permute-start | bytes 2359304 | tf_op jit(solution)/shard_map/ppermute | solution.py:31
  4.0 1.8 broadcast_in_dim.13
  5.8 7.8 %all-to-all-start = ((bf16[16,32,768]{2,1,0:T(8,128)(2,1)}), bf16[16,32,768]{2,1,0:T(8,128)(2,1)S(1)}, u32[]{:S(2)}, u32[]{:S(2)}) async-start(bf16[16,32,768]{2,1,0:T(8,128)(2,1)} %broadcast_in_dim.13), calls=%async_computation | async-start | bytes 1572864 | tf_op jit(solution)/shard_map/all_to_all | solution.py:43
  13.5 7.0 %collective-permute-done.ahead_ref.refs_1_ = bf16[512,768]{1,0:T(8,128)(2,1)S(1)} collective-permute-done((bf16[512,768]{1,0:T(8,128)(2,1)}, bf16[512,768]{1,0:T(8,128)(2,1)S(1)}, u32[]{:S(2)}, u32[]{:S(2)}) %collective-permute-start) | collective-permute-done | bytes 786464 | tf_op jit(solution)/shard_map/ppermute | solution.py:31
  20.5 3.0 %collective-permute-done.1.behind_ref.refs_4_ = bf16[512,768]{1,0:T(8,128)(2,1)S(1)} collective-permute-done((bf16[512,768]{1,0:T(8,128)(2,1)}, bf16[512,768]{1,0:T(8,128)(2,1)S(1)}, u32[]{:S(2)}, u32[]{:S(2)}) %collective-permute-start.1) | collective-permute-done | bytes 786464 | tf_op jit(solution)/shard_map/ppermute | solution.py:31
  23.5 0.9 copy-done.6
  24.4 2.0 %shard_map.101 = (bf16[256,768]{1,0:T(8,128)(2,1)}, bf16[256,768]{1,0:T(8,128)(2,1)}) custom-call(bf16[512,768]{1,0:T(8,128)(2,1)} %copy-done.5, bf16[512,768]{1,0:T(8,128)(2,1)} %copy-done.6), custom_call_target="tpu_custom_call" | custom-call | flops 10000000000 | bytes 1000 | tf_op jit(solution)/shard_map/pallas_call | solution.py:86
  26.4 1.3 slice.20
  28.4 1.9 %collective-permute-start.2 = (bf16[16,32,768]{2,1,0:T(8,128)(2,1)S(1)}, bf16[16,32,768]{2,1,0:T(8,128)(2,1)S(1)}, u32[]{:S(2)}, u32[]{:S(2)}) collective-permute-start(bf16[16,32,768]{2,1,0:T(8,128)(2,1)S(1)} %broadcast_multiply_fusion), channel_id=1, source_target_pairs={{0,1},{1,0},{2,3},{3,2},{4,5},{5,4},{6,7},{7,6},{8,9},{9,8},{10,11... | collective-permute-start | bytes 2359304 | tf_op jit(solution)/shard_map/ppermute | solution.py:26
  30.4 1.3 collective-permute-start.7
  33.2 0.6 copy-done.2
  33.8 1.0 fusion.5
  35.3 3.3 %collective-permute-start.4 = (f32[2,4,128]{2,1,0:T(4,128)S(1)}, f32[2,4,128]{2,1,0:T(4,128)S(1)}, u32[]{:S(2)}, u32[]{:S(2)}) collective-permute-start(f32[2,4,128]{2,1,0:T(4,128)S(1)} %pad_maximum_fusion.2.refs_2_), channel_id=1, source_target_pairs={{0,64},{32,96},{64,0},{96,32},{1,65},{33,97},{65,1},{97,33},{2,66}... | collective-permute-start | bytes 12296 | tf_op jit(solution)/shard_map/ppermute | solution.py:31
  38.6 4.8 %collective-permute-done.6.refs_2_.refs_0_ = bf16[256,768]{1,0:T(8,128)(2,1)S(1)} collective-permute-done((bf16[256,768]{1,0:T(8,128)(2,1)S(1)}, bf16[256,768]{1,0:T(8,128)(2,1)S(1)}, u32[]{:S(2)}, u32[]{:S(2)}) %collective-permute-start.6) | collective-permute-done | bytes 393248 | tf_op jit(solution)/shard_map/ppermute | solution.py:31
  43.4 1.0 broadcast_in_dim.12.live_ref
  44.4 2.3 %shard_map.105.refs_0_.grad_ref = bf16[512,768]{1,0:T(8,128)(2,1)} custom-call(f32[512,128]{1,0:T(8,128)} %broadcast_in_dim.12.live_ref, bf16[512,768]{1,0:T(8,128)(2,1)} %bitcast.65, bf16[256,768]{1,0:T(8,128)(2,1)} %copy-done.4, bf16[256,768]{1,0:T(8,128)(2,1)} %copy-done.3, f32[2,4,128]{2,1,0:T(4,128)} %copy-done.15), custom_call_target="tpu_custom_call" | custom-call | flops 1000 | bytes 1000 | tf_op jit(solution)/shard_map/pallas_call | solution.py:86
  47.4 0.8 collective-permute-start.10
  48.1 0.8 slice_bitcast_fusion.phi_ref
  48.9 0.6 fusion.4
  49.5 6.0 %shard_map.102 = (bf16[256,2048]{1,0:T(8,128)(2,1)}, bf16[256,2048]{1,0:T(8,128)(2,1)}, bf16[256,768]{1,0:T(8,128)(2,1)}, f32[256,768]{1,0:T(8,128)}, f32[256,1]...) custom-call(bf16[256,768]{1,0:T(8,128)(2,1)} %slice_bitcast_fusion.phi_ref, f32[1,2048]{1,0:T(1,128)} %bitcast.70, ...), custom_call_target="tpu_custom_call" | custom-call | flops 1000 | bytes 1000 | tf_op jit(solution)/shard_map/pallas_call | solution.py:86
  55.5 19.9 %all_to_all.25 = bf16[32,8,768]{2,1,0:T(8,128)(2,1)} all-to-all(bf16[32,8,768]{2,1,0:T(8,128)(2,1)} %bitcast.67), channel_id=1, replica_groups=mesh['x'=4,'y'=4,'z'=4,'core'=2] {'y','z','core'}, dimensions={0} | all-to-all | bytes 786432 | tf_op jit(solution)/shard_map/all_to_all | solution.py:43
  75.4 8.6 %shard_map.103 = (bf16[256,3072]{1,0:T(8,128)(2,1)}, bf16[256,3072]{1,0:T(8,128)(2,1)}, bf16[256,768]{1,0:T(8,128)(2,1)}) custom-call(bf16[256,768]{1,0:T(8,128)(2,1)} %bitcast.60, bf16[768,3072]{1,0:T(8,128)(2,1)} %bitcast.40, bf16[3072,768]{1,0:T(8,128)(2,1)} %bitcast.42), custom_call_target="tpu_custom_call" | custom-call | flops 1000 | bytes 1000 | tf_op jit(solution)/shard_map/pallas_call | solution.py:86
  84.1 0.8 collective-permute-done.10.refs_3_
  85.7 4.2 %shard_map.106 = bf16[256,1536]{1,0:T(8,128)(2,1)} custom-call(bf16[256,2048]{1,0:T(8,128)(2,1)} %get-tuple-element.33.combine_ref, bf16[256,768]{1,0:T(8,128)(2,1)} %get-tuple-element.32._.output_ref, bf16[512,768]{1,0:T(8,128)(2,1)} %shard_map.105.refs_0_.grad_ref, bf16[512,768]{1,0:T(8,128)(2,1)} %copy-done.7, bf16[512,768]{1,0:T(8,128)(2,1)} %copy-done.8, ...), custom_call_target="tpu_custom_call" | custom-call | flops 1000 | bytes 1000 | tf_op jit(solution)/shard_map/pallas_call | solution.py:86
  89.9 8.2 %all-to-all-start.2 = ((bf16[32,8,1536]{2,1,0:T(8,128)(2,1)}), bf16[32,8,1536]{2,1,0:T(8,128)(2,1)S(1)}, u32[]{:S(2)}, u32[]{:S(2)}) async-start(bf16[32,8,1536]{2,1,0:T(8,128)(2,1)} %bitcast.62), calls=%async_computation.2 | async-start | bytes 1572864 | tf_op jit(solution)/shard_map/all_to_all | solution.py:43
  98.1 4.4 %shard_map.104._.combine_ref = bf16[512,1024]{1,0:T(8,128)(2,1)} custom-call(f32[512,128]{1,0:T(8,128)} %broadcast_in_dim.12.live_ref, bf16[512,768]{1,0:T(8,128)(2,1)} %bitcast.53, bf16[1024,768]{1,0:T(8,128)(2,1)} %bitcast.48, bf16[256,768]{1,0:T(8,128)(2,1)} %get-tuple-element.32._.output_ref), custom_call_target="tpu_custom_call" | custom-call | flops 1000 | bytes 1000 | tf_op jit(solution)/shard_map/pallas_call | solution.py:86
  102.4 9.9 %all-to-all-done.2 = bf16[32,8,1536]{2,1,0:T(8,128)(2,1)S(1)} async-done(((bf16[32,8,1536]{2,1,0:T(8,128)(2,1)}), bf16[32,8,1536]{2,1,0:T(8,128)(2,1)S(1)}, u32[]{:S(2)}, u32[]{:S(2)}) %all-to-all-start.2) | async-done | bytes 786464 | tf_op jit(solution)/shard_map/all_to_all | solution.py:43
  112.3 0.9 copy-done
  113.2 4.9 %shard_map.107 = (f32[256,2048]{1,0:T(8,128)}, bf16[272,768]{1,0:T(8,128)(2,1)}) custom-call(bf16[256,1536]{1,0:T(8,128)(2,1)} %bitcast.44, bf16[512,1024]{1,0:T(8,128)(2,1)} %shard_map.104._.combine_ref, bf16[256,2048]{1,0:T(8,128)(2,1)} %get-tuple-element.33.combine_ref, f32[256,1]{1,0:T(8,128)} %get-tuple-element.34.top_ref, ...), custom_call_target="tpu_custom_call" | custom-call | flops 1000 | bytes 1000 | tf_op jit(solution)/shard_map/pallas_call | solution.py:86
  118.1 1.1 collective-permute-start.11
  120.0 8.3 %shard_map.109 = (bf16[256,3072]{1,0:T(8,128)(2,1)}, bf16[256,768]{1,0:T(8,128)(2,1)}) custom-call(bf16[256,1536]{1,0:T(8,128)(2,1)} %bitcast.45, bf16[256,3072]{1,0:T(8,128)(2,1)} %get-tuple-element.39.slope_ref, bf16[768,3072]{1,0:T(8,128)(2,1)} %bitcast.41, bf16[3072,768]{1,0:T(8,128)(2,1)} %bitcast.43, bf16[272,768]{1,0:T(8,128)(2,1)} %get-tuple-element.36.refs_0_._), custom_call_target="tpu_custom_call" | custom-call | flops 1000 | bytes 1000 | tf_op jit(solution)/shard_map/pallas_call | solution.py:86
  128.3 4.7 %all-to-all-start.3 = ((bf16[32,8,768]{2,1,0:T(8,128)(2,1)}), bf16[32,8,768]{2,1,0:T(8,128)(2,1)S(1)}, u32[]{:S(2)}, u32[]{:S(2)}) async-start(bf16[32,8,768]{2,1,0:T(8,128)(2,1)} %bitcast.66), calls=%async_computation.3 | async-start | bytes 786432 | tf_op jit(solution)/shard_map/all_to_all | solution.py:43
  133.0 7.1 %shard_map.110 = (bf16[768,3072]{1,0:T(8,128)(2,1)}, bf16[3072,768]{1,0:T(8,128)(2,1)}) custom-call(bf16[256,768]{1,0:T(8,128)(2,1)} %bitcast.61, bf16[256,1536]{1,0:T(8,128)(2,1)} %bitcast.46, bf16[256,3072]{1,0:T(8,128)(2,1)} %get-tuple-element.43.hidden_ref, bf16[256,3072]{1,0:T(8,128)(2,1)} %get-tuple-element.44.pre_ref), custom_call_target="tpu_custom_call" | custom-call | flops 1000 | bytes 1000 | tf_op jit(solution)/shard_map/pallas_call | solution.py:86
  140.1 3.2 %all-to-all-done.3 = bf16[32,8,768]{2,1,0:T(8,128)(2,1)S(1)} async-done(((bf16[32,8,768]{2,1,0:T(8,128)(2,1)}), bf16[32,8,768]{2,1,0:T(8,128)(2,1)S(1)}, u32[]{:S(2)}, u32[]{:S(2)}) %all-to-all-start.3) | async-done | bytes 393248 | tf_op jit(solution)/shard_map/all_to_all | solution.py:43
  143.3 0.7 copy-done.11
  144.0 2.6 %shard_map.111 = (bf16[272,768]{1,0:T(8,128)(2,1)}, f32[256,1]{1,0:T(8,128)}) custom-call(bf16[256,768]{1,0:T(8,128)(2,1)} %bitcast.64, f32[256,768]{1,0:T(8,128)} %get-tuple-element.41.normed_ref, f32[256,1]{1,0:T(8,128)} %get-tuple-element.42.factor_ref, bf16[3072,768]{1,0:T(8,128)(2,1)} %get-tuple-element.45._down, bf16[768,3072]{1,0:T(8,128)(2,1)} %get-tuple-element.46._up), custom_call_target="tpu_custom_call" | custom-call | flops 1000 | bytes 1000 | tf_op jit(solution)/shard_map/pallas_call | solution.py:86
  146.6 2.1 %collective-permute-start.14 = (bf16[272,768]{1,0:T(8,128)(2,1)}, bf16[272,768]{1,0:T(8,128)(2,1)S(1)}, u32[]{:S(2)}, u32[]{:S(2)}) collective-permute-start(bf16[272,768]{1,0:T(8,128)(2,1)} %get-tuple-element.47.refs_4_.grad_ref), channel_id=1, source_target_pairs={{0,96},{32,0},{64,32},{96,64},{1,97},{33,1},{65,33},{97,65},{2,98}... | collective-permute-start | bytes 1253384 | tf_op jit(solution)/shard_map/ppermute | solution.py:31
  148.7 1.6 collective-permute-start.15
  151.4 0.8 copy-done.14
  152.2 1.4 shard_map.113.row_ref
  153.6 6.4 %shard_map.114 = bf16[256,768]{1,0:T(8,128)(2,1)} custom-call(bf16[272,768]{1,0:T(8,128)(2,1)} %get-tuple-element.47.refs_4_.grad_ref, bf16[256,2048]{1,0:T(8,128)(2,1)} %get-tuple-element.33.combine_ref, f32[256,2048]{1,0:T(8,128)} %get-tuple-element.49.combine_grad_ref, f32[1,2048]{1,0:T(1,128)} %shard_map.113.row_ref, ...), custom_call_target="tpu_custom_call" | custom-call | flops 1000 | bytes 1000 | tf_op jit(solution)/shard_map/pallas_call | solution.py:86
  160.0 5.0 %all-to-all-start.4 = ((bf16[32,8,768]{2,1,0:T(8,128)(2,1)}), bf16[32,8,768]{2,1,0:T(8,128)(2,1)S(1)}, u32[]{:S(2)}, u32[]{:S(2)}) async-start(bf16[32,8,768]{2,1,0:T(8,128)(2,1)} %bitcast.63), calls=%async_computation.4 | async-start | bytes 786432 | tf_op jit(solution)/shard_map/all_to_all | solution.py:43
  165.0 4.7 %shard_map.108 = (bf16[512,768]{1,0:T(8,128)(2,1)}, bf16[512,1024]{1,0:T(8,128)(2,1)}) custom-call(bf16[512,1024]{1,0:T(8,128)(2,1)} %shard_map.104._.combine_ref, bf16[512,768]{1,0:T(8,128)(2,1)} %shard_map.105.refs_0_.grad_ref, bf16[272,768]{1,0:T(8,128)(2,1)} %get-tuple-element.36.refs_0_._, bf16[272,768]{1,0:T(8,128)(2,1)} %copy-done.12, ...), custom_call_target="tpu_custom_call" | custom-call | flops 1000 | bytes 1000 | tf_op jit(solution)/shard_map/pallas_call | solution.py:86
  169.8 1.2 collective-permute-done.16.refs_7_
  171.0 0.8 copy-done.19
  171.8 7.4 %shard_map.112 = (bf16[512,768]{1,0:T(8,128)(2,1)}, f32[8,128]{1,0:T(8,128)}) custom-call(f32[512,128]{1,0:T(8,128)} %broadcast_in_dim.12.live_ref, bf16[512,1024]{1,0:T(8,128)(2,1)} %get-tuple-element.38.logit_ref, bf16[512,768]{1,0:T(8,128)(2,1)} %bitcast.55, bf16[1024,768]{1,0:T(8,128)(2,1)} %bitcast.49, bf16[272,768]{1,0:T(8,128)(2,1)} %get-tuple-element.36.refs_0_._, ...), custom_call_target="tpu_custom_call" | custom-call | flops 5000000000 | bytes 1000 | tf_op jit(solution)/shard_map/pallas_call | solution.py:86
  179.2 0.7 copy-done.10
  179.9 1.7 shard_map.115
  (70 shorter events, 5.6 us)
Async XLA Ops:
  0.6 19.9 %collective-permute-start = (bf16[512,768]{1,0:T(8,128)(2,1)}, bf16[512,768]{1,0:T(8,128)(2,1)S(1)}, u32[]{:S(2)}, u32[]{:S(2)}) collective-permute-start(bf16[512,768]{1,0:T(8,128)(2,1)} %bitcast.50), channel_id=1, source_target_pairs={{0,96},{32,0},{64,32},{96,64},{1,97},{33,1},{65,33},{97,65},{2,98}... | collective-permute-start | bytes 2359304 | tf_op jit(solution)/shard_map/ppermute | solution.py:31
  4.0 19.5 %collective-permute-start.1 = (bf16[512,768]{1,0:T(8,128)(2,1)}, bf16[512,768]{1,0:T(8,128)(2,1)S(1)}, u32[]{:S(2)}, u32[]{:S(2)}) collective-permute-start(bf16[512,768]{1,0:T(8,128)(2,1)} %bitcast.51), channel_id=1, source_target_pairs={{0,32},{32,64},{64,96},{96,0},{1,33},{33,65},{65,97},{97,1},{2,34}... | collective-permute-start | bytes 2359304 | tf_op jit(solution)/shard_map/ppermute | solution.py:31
  5.8 22.6 %all-to-all-start = ((bf16[16,32,768]{2,1,0:T(8,128)(2,1)}), bf16[16,32,768]{2,1,0:T(8,128)(2,1)S(1)}, u32[]{:S(2)}, u32[]{:S(2)}) async-start(bf16[16,32,768]{2,1,0:T(8,128)(2,1)} %broadcast_in_dim.13), calls=%async_computation | async-start | bytes 1572864 | tf_op jit(solution)/shard_map/all_to_all | solution.py:43
  20.5 3.0 %copy-start.5 = (bf16[512,768]{1,0:T(8,128)(2,1)}, bf16[512,768]{1,0:T(8,128)(2,1)S(1)}, u32[]{:S(2)}) copy-start(bf16[512,768]{1,0:T(8,128)(2,1)S(1)} %collective-permute-done.ahead_ref.refs_1_) | copy-start | bytes 2359300
  23.5 0.9 copy-start.6
  26.4 4.0 %copy-start.16 = (s32[1,512]{1,0:T(1,128)S(1)}, s32[1,512]{1,0:T(1,128)}, u32[]{:S(2)}) copy-start(s32[1,512]{1,0:T(1,128)} %param.7) | copy-start | bytes 6148
  26.4 4.0 %copy-start.20 = (bf16[256,768]{1,0:T(8,128)(2,1)S(1)}, bf16[256,768]{1,0:T(8,128)(2,1)}, u32[]{:S(2)}) copy-start(bf16[256,768]{1,0:T(8,128)(2,1)} %get-tuple-element.29) | copy-start | bytes 1179652
  26.4 5.3 %copy-start.21 = (bf16[256,768]{1,0:T(8,128)(2,1)S(1)}, bf16[256,768]{1,0:T(8,128)(2,1)}, u32[]{:S(2)}) copy-start(bf16[256,768]{1,0:T(8,128)(2,1)} %get-tuple-element.30) | copy-start | bytes 1179652
  28.4 3.9 %collective-permute-start.2 = (bf16[16,32,768]{2,1,0:T(8,128)(2,1)S(1)}, bf16[16,32,768]{2,1,0:T(8,128)(2,1)S(1)}, u32[]{:S(2)}, u32[]{:S(2)}) collective-permute-start(bf16[16,32,768]{2,1,0:T(8,128)(2,1)S(1)} %broadcast_multiply_fusion), channel_id=1, source_target_pairs={{0,1},{1,0},{2,3},{3,2},{4,5},{5,4},{6,7},{7,6},{8,9},{9,8},{10,11... | collective-permute-start | bytes 2359304 | tf_op jit(solution)/shard_map/ppermute | solution.py:26
  30.4 13.0 %collective-permute-start.7 = (bf16[256,768]{1,0:T(8,128)(2,1)S(1)}, bf16[256,768]{1,0:T(8,128)(2,1)S(1)}, u32[]{:S(2)}, u32[]{:S(2)}) collective-permute-start(bf16[256,768]{1,0:T(8,128)(2,1)S(1)} %copy-done.20), channel_id=1, source_target_pairs={{0,96},{32,0},{64,32},{96,64},{1,97},{33,1},{65,33},{97,65},{2,98}... | collective-permute-start | bytes 1179656 | tf_op jit(solution)/shard_map/ppermute | solution.py:31
  31.7 11.7 %collective-permute-start.6 = (bf16[256,768]{1,0:T(8,128)(2,1)S(1)}, bf16[256,768]{1,0:T(8,128)(2,1)S(1)}, u32[]{:S(2)}, u32[]{:S(2)}) collective-permute-start(bf16[256,768]{1,0:T(8,128)(2,1)S(1)} %copy-done.21), channel_id=1, source_target_pairs={{0,32},{32,64},{64,96},{96,0},{1,33},{33,65},{65,97},{97,1},{2,34}... | collective-permute-start | bytes 1179656 | tf_op jit(solution)/shard_map/ppermute | solution.py:31
  32.7 1.1 copy-start.2
  33.2 14.9 %copy-start.1 = (bf16[4,256,768]{2,1,0:T(8,128)(2,1)}, bf16[4,256,768]{2,1,0:T(8,128)(2,1)S(1)}, u32[]{:S(2)}) copy-start(bf16[4,256,768]{2,1,0:T(8,128)(2,1)S(1)} %fusion) | copy-start | bytes 4718596
  35.2 9.2 %copy-start.15 = (f32[2,4,128]{2,1,0:T(4,128)}, f32[2,4,128]{2,1,0:T(4,128)S(1)}, u32[]{:S(2)}) copy-start(f32[2,4,128]{2,1,0:T(4,128)S(1)} %pad_maximum_fusion.2.refs_2_) | copy-start | bytes 12292
  35.2 12.2 %collective-permute-start.5 = (f32[2,4,128]{2,1,0:T(4,128)S(1)}, f32[2,4,128]{2,1,0:T(4,128)S(1)}, u32[]{:S(2)}, u32[]{:S(2)}) collective-permute-start(f32[2,4,128]{2,1,0:T(4,128)S(1)} %pad_maximum_fusion.2.refs_2_), channel_id=1, source_target_pairs={{0,32},{32,64},{64,96},{96,0},{1,33},{33,65},{65,97},{97,1},{2,34}... | collective-permute-start | bytes 12296 | tf_op jit(solution)/shard_map/ppermute | solution.py:31
  35.3 13.6 %collective-permute-start.4 = (f32[2,4,128]{2,1,0:T(4,128)S(1)}, f32[2,4,128]{2,1,0:T(4,128)S(1)}, u32[]{:S(2)}, u32[]{:S(2)}) collective-permute-start(f32[2,4,128]{2,1,0:T(4,128)S(1)} %pad_maximum_fusion.2.refs_2_), channel_id=1, source_target_pairs={{0,64},{32,96},{64,0},{96,32},{1,65},{33,97},{65,1},{97,33},{2,66}... | collective-permute-start | bytes 12296 | tf_op jit(solution)/shard_map/ppermute | solution.py:31
  38.6 10.3 %collective-permute-start.3 = (f32[2,4,128]{2,1,0:T(4,128)S(1)}, f32[2,4,128]{2,1,0:T(4,128)S(1)}, u32[]{:S(2)}, u32[]{:S(2)}) collective-permute-start(f32[2,4,128]{2,1,0:T(4,128)S(1)} %pad_maximum_fusion.2.refs_2_), channel_id=1, source_target_pairs={{0,96},{32,0},{64,32},{96,64},{1,97},{33,1},{65,33},{97,65},{2,98}... | collective-permute-start | bytes 12296 | tf_op jit(solution)/shard_map/ppermute | solution.py:31
  43.4 1.0 copy-start.4
  43.4 1.0 copy-start.3
  46.7 37.4 %collective-permute-start.8 = (bf16[512,768]{1,0:T(8,128)(2,1)}, bf16[512,768]{1,0:T(8,128)(2,1)S(1)}, u32[]{:S(2)}, u32[]{:S(2)}) collective-permute-start(bf16[512,768]{1,0:T(8,128)(2,1)} %shard_map.105.refs_0_.grad_ref), channel_id=1, source_target_pairs={{0,96},{32,0},{64,32},{96,64},{1,97},{33,1},{65,33},{97,65},{2,98}... | collective-permute-start | bytes 2359304 | tf_op jit(solution)/shard_map/ppermute | solution.py:31
  46.8 37.2 %collective-permute-start.9 = (bf16[512,768]{1,0:T(8,128)(2,1)}, bf16[512,768]{1,0:T(8,128)(2,1)S(1)}, u32[]{:S(2)}, u32[]{:S(2)}) collective-permute-start(bf16[512,768]{1,0:T(8,128)(2,1)} %shard_map.105.refs_0_.grad_ref), channel_id=1, source_target_pairs={{0,64},{32,96},{64,0},{96,32},{1,65},{33,97},{65,1},{97,33},{2,66}... | collective-permute-start | bytes 2359304 | tf_op jit(solution)/shard_map/ppermute | solution.py:31
  47.4 37.5 %collective-permute-start.10 = (bf16[512,768]{1,0:T(8,128)(2,1)}, bf16[512,768]{1,0:T(8,128)(2,1)S(1)}, u32[]{:S(2)}, u32[]{:S(2)}) collective-permute-start(bf16[512,768]{1,0:T(8,128)(2,1)} %shard_map.105.refs_0_.grad_ref), channel_id=1, source_target_pairs={{0,32},{32,64},{64,96},{96,0},{1,33},{33,65},{65,97},{97,1},{2,34}... | collective-permute-start | bytes 2359304 | tf_op jit(solution)/shard_map/ppermute | solution.py:31
  84.0 0.9 copy-start.7
  84.0 1.1 copy-start.8
  84.8 0.9 copy-start.9
  89.9 22.4 %all-to-all-start.2 = ((bf16[32,8,1536]{2,1,0:T(8,128)(2,1)}), bf16[32,8,1536]{2,1,0:T(8,128)(2,1)S(1)}, u32[]{:S(2)}, u32[]{:S(2)}) async-start(bf16[32,8,1536]{2,1,0:T(8,128)(2,1)} %bitcast.62), calls=%async_computation.2 | async-start | bytes 1572864 | tf_op jit(solution)/shard_map/all_to_all | solution.py:43
  112.3 0.9 copy-start
  118.1 32.2 %collective-permute-start.11 = (bf16[272,768]{1,0:T(8,128)(2,1)}, bf16[272,768]{1,0:T(8,128)(2,1)S(1)}, u32[]{:S(2)}, u32[]{:S(2)}) collective-permute-start(bf16[272,768]{1,0:T(8,128)(2,1)} %get-tuple-element.36.refs_0_._), channel_id=1, source_target_pairs={{0,96},{32,0},{64,32},{96,64},{1,97},{33,1},{65,33},{97,65},{2,98}... | collective-permute-start | bytes 1253384 | tf_op jit(solution)/shard_map/ppermute | solution.py:31
  119.2 31.5 %collective-permute-start.12 = (bf16[272,768]{1,0:T(8,128)(2,1)}, bf16[272,768]{1,0:T(8,128)(2,1)S(1)}, u32[]{:S(2)}, u32[]{:S(2)}) collective-permute-start(bf16[272,768]{1,0:T(8,128)(2,1)} %get-tuple-element.36.refs_0_._), channel_id=1, source_target_pairs={{0,64},{32,96},{64,0},{96,32},{1,65},{33,97},{65,1},{97,33},{2,66}... | collective-permute-start | bytes 1253384 | tf_op jit(solution)/shard_map/ppermute | solution.py:31
  119.4 31.3 %collective-permute-start.13 = (bf16[272,768]{1,0:T(8,128)(2,1)}, bf16[272,768]{1,0:T(8,128)(2,1)S(1)}, u32[]{:S(2)}, u32[]{:S(2)}) collective-permute-start(bf16[272,768]{1,0:T(8,128)(2,1)} %get-tuple-element.36.refs_0_._), channel_id=1, source_target_pairs={{0,32},{32,64},{64,96},{96,0},{1,33},{33,65},{65,97},{97,1},{2,34}... | collective-permute-start | bytes 1253384 | tf_op jit(solution)/shard_map/ppermute | solution.py:31
  128.3 15.0 %all-to-all-start.3 = ((bf16[32,8,768]{2,1,0:T(8,128)(2,1)}), bf16[32,8,768]{2,1,0:T(8,128)(2,1)S(1)}, u32[]{:S(2)}, u32[]{:S(2)}) async-start(bf16[32,8,768]{2,1,0:T(8,128)(2,1)} %bitcast.66), calls=%async_computation.3 | async-start | bytes 786432 | tf_op jit(solution)/shard_map/all_to_all | solution.py:43
  143.3 0.7 copy-start.11
  146.6 23.1 %collective-permute-start.14 = (bf16[272,768]{1,0:T(8,128)(2,1)}, bf16[272,768]{1,0:T(8,128)(2,1)S(1)}, u32[]{:S(2)}, u32[]{:S(2)}) collective-permute-start(bf16[272,768]{1,0:T(8,128)(2,1)} %get-tuple-element.47.refs_4_.grad_ref), channel_id=1, source_target_pairs={{0,96},{32,0},{64,32},{96,64},{1,97},{33,1},{65,33},{97,65},{2,98}... | collective-permute-start | bytes 1253384 | tf_op jit(solution)/shard_map/ppermute | solution.py:31
  148.7 21.0 %collective-permute-start.15 = (bf16[272,768]{1,0:T(8,128)(2,1)}, bf16[272,768]{1,0:T(8,128)(2,1)S(1)}, u32[]{:S(2)}, u32[]{:S(2)}) collective-permute-start(bf16[272,768]{1,0:T(8,128)(2,1)} %get-tuple-element.47.refs_4_.grad_ref), channel_id=1, source_target_pairs={{0,64},{32,96},{64,0},{96,32},{1,65},{33,97},{65,1},{97,33},{2,66}... | collective-permute-start | bytes 1253384 | tf_op jit(solution)/shard_map/ppermute | solution.py:31
  150.3 0.8 copy-start.12
  150.3 20.7 %collective-permute-start.16 = (bf16[272,768]{1,0:T(8,128)(2,1)}, bf16[272,768]{1,0:T(8,128)(2,1)S(1)}, u32[]{:S(2)}, u32[]{:S(2)}) collective-permute-start(bf16[272,768]{1,0:T(8,128)(2,1)} %get-tuple-element.47.refs_4_.grad_ref), channel_id=1, source_target_pairs={{0,32},{32,64},{64,96},{96,0},{1,33},{33,65},{65,97},{97,1},{2,34}... | collective-permute-start | bytes 1253384 | tf_op jit(solution)/shard_map/ppermute | solution.py:31
  150.7 0.7 copy-start.13
  151.4 0.8 copy-start.14
  160.0 19.2 %all-to-all-start.4 = ((bf16[32,8,768]{2,1,0:T(8,128)(2,1)}), bf16[32,8,768]{2,1,0:T(8,128)(2,1)S(1)}, u32[]{:S(2)}, u32[]{:S(2)}) async-start(bf16[32,8,768]{2,1,0:T(8,128)(2,1)} %bitcast.63), calls=%async_computation.4 | async-start | bytes 786432 | tf_op jit(solution)/shard_map/all_to_all | solution.py:43
  169.8 1.2 copy-start.17
  169.8 1.2 copy-start.18
  171.0 0.8 copy-start.19
  179.2 0.8 copy-start.10

commit v4 on v3

--- a/solution.py
+++ b/solution.py
@@ -177,13 +177,26 @@
     out_ref[:, width:] = output_ref[...]
 
 
-def halves_kernel(ahead_ref, behind_ref, ahead_out_ref, behind_out_ref):
+def halves_kernel(ahead_ref, behind_ref, _, ahead_out_ref, behind_out_ref):
     ahead_out_ref[...] = ahead_ref[...]
     behind_out_ref[...] = behind_ref[...]
 
 
-def mask_kernel(live_ref, grad_ref, *refs):
-    refs[-1][...] = jnp.where(live_ref[:, :1] > 0.0, grad_ref[...].astype(F32), 0.0).astype(BF16)
+def nothing_kernel(*refs):
+    del refs
+
+
+def tied(values, *others):
+    where = pl.BlockSpec(memory_space=pl.ANY)
+    return pl.pallas_call(
+        nothing_kernel,
+        in_specs=[where] * (1 + len(others)),
+        out_specs=where,
+        out_shape=jax.ShapeDtypeStruct(values.shape, values.dtype),
+        input_output_aliases={0: 0},
+        compiler_params=pltpu.CompilerParams(vmem_limit_bytes=LIMIT),
+        cost_estimate=pl.CostEstimate(flops=1000, bytes_accessed=1000, transcendentals=0),
+    )(values, *others)
 
 
 def softmax_kernel(live_ref, tokens_ref, phi_ref, _, out_ref):
@@ -327,13 +340,16 @@
     rows, features = clip_part.shape
     planes = lax.axis_size("x")
     experts = lax.axis_size("y") * lax.axis_size("z") * lax.axis_size("core")
-    live_rows = (halt_steps[0] > LAYER_POS)[:, None].astype(F32)
+    live_rows = (halt_steps[0] > LAYER_POS)[:, None]
+    masked_grad = jnp.where(live_rows, cotangent[0], jnp.zeros((), BF16))
+    live_rows = live_rows.astype(F32)
     live_wide = jnp.broadcast_to(live_rows, (rows, 128))
 
     ahead, behind = to_neighbours(clip_part)
     half = (rows // 2, features)
     ahead_half, behind_half = call(
-        halves_kernel, 1, [(ahead, half, (1, 0)), (behind, half, (0, 0))], [made(BF16, *half)] * 2, work=10**10
+        halves_kernel, 1, [(ahead, half, (1, 0)), (behind, half, (0, 0)), (masked_grad, (16, 128), None)], [made(BF16, *half)] * 2,
+        work=10**10,
     )
     far = along_x(behind_half, 1), along_x(ahead_half, -1)
     phi_groups = gather_phi(phi, unit(ahead_half))
@@ -348,14 +364,7 @@
     message = jnp.stack([top, norm]).reshape(2, -1, 128)
     row_stats = jnp.concatenate(gather_x(message), axis=1).reshape(2, 1, -1)
 
-    (masked_grad,) = call(
-        mask_kernel,
-        1,
-        [whole(live_wide), whole(cotangent[0])]
-        + [(f, (16, 128), None) for f in far]
-        + [(message, (2, 4, 128), None)],
-        [made(BF16, rows, features)],
-    )
+    masked_grad = tied(masked_grad, *far, message)
     grad_pieces = gather_x(masked_grad)
     pieces = [clip_part, ahead, *far, behind]
     clip_rows = planes * rows

time: 183 us -> 181 us (0.989)
  Pallas kernels: 71.9 us -> 69.6 us
  waiting for transfers between devices: 30.2 us -> 28.2 us
    pallas_call x15 -> x14, Pallas kernels: 71.9 us -> 69.6 us  [call(): pl.pallas_call(kernel, grid=(steps,), in_specs=[spec(block, where) for _,...]
    unnamed x44 -> x46, local copies, waits for them, and re-layouts: 7.09 us -> 8.54 us
  transfers between devices with their start and end apart: 21 -> 21, of which waited for: 8 -> 8; matrix products, arithmetic and copies ran while one was open for 4% -> 5% of each run, Pallas kernels for 34% -> 33%
where the time goes in v4:
time: 181 us; the launch traced here: 180 us
  Pallas kernels  69.6 us (38%)
  starting transfers between devices  43.1 us (24%)
  waiting for transfers between devices  28.2 us (16%)
  blocking collectives  19.9 us (11%)
  local copies, waits for them, and re-layouts  13.8 us (8%)
  other arithmetic  2.4 us (1%)
    pallas_call x14, Pallas kernels, call(): pl.pallas_call(kernel, grid=(steps,), in_specs=[spec(block, where) for _,...  69.6 us
    all_to_all x4, starting transfers between devices, exchange(): return lax.all_to_all(values, axes, 0, 0, tiled=True)  25.7 us
    all_to_all x1, blocking collectives, exchange(): return lax.all_to_all(values, axes, 0, 0, tiled=True)  19.9 us
    ppermute x16, waiting for transfers between devices, along_x(): return lax.ppermute(values, 'x', [(i, (i + steps) % n) for i in range(n)])  15.5 us
    ppermute x16, starting transfers between devices, along_x(): return lax.ppermute(values, 'x', [(i, (i + steps) % n) for i in range(n)])  15.5 us
    all_to_all x4, waiting for transfers between devices, exchange(): return lax.all_to_all(values, axes, 0, 0, tiled=True)  12.2 us
    unnamed x46, local copies, waits for them, and re-layouts  8.54 us
  transfers between devices with their start and end apart: 21, of which 8 were waited for; matrix products, arithmetic and copies ran while one was open for 5% of the time, Pallas kernels for 33%

profile of v4, /device:TPU:1, one launch (start us, length us, event | category | flops | bytes accessed | tf_op | source)
XLA Modules:
  0.0 179.7 jit_solution(6656063888195663192)
XLA Ops:
  0.7 3.4 %collective-permute-start = (bf16[512,768]{1,0:T(8,128)(2,1)}, bf16[512,768]{1,0:T(8,128)(2,1)S(1)}, u32[]{:S(2)}, u32[]{:S(2)}) collective-permute-start(bf16[512,768]{1,0:T(8,128)(2,1)} %bitcast.50), channel_id=1, source_target_pairs={{0,96},{32,0},{64,32},{96,64},{1,97},{33,1},{65,33},{97,65},{2,98}... | collective-permute-start | bytes 2359304 | tf_op jit(solution)/shard_map/ppermute | solution.py:31
  4.0 1.8 broadcast_in_dim.39
  5.8 7.8 %all-to-all-start = ((bf16[16,32,768]{2,1,0:T(8,128)(2,1)}), bf16[16,32,768]{2,1,0:T(8,128)(2,1)S(1)}, u32[]{:S(2)}, u32[]{:S(2)}) async-start(bf16[16,32,768]{2,1,0:T(8,128)(2,1)} %broadcast_in_dim.39), calls=%async_computation | async-start | bytes 1572864 | tf_op jit(solution)/shard_map/all_to_all | solution.py:43
  13.6 1.0 bitcast_select_fusion._.refs_0_
  14.7 5.9 %collective-permute-done.ahead_ref.refs_1_ = bf16[512,768]{1,0:T(8,128)(2,1)S(1)} collective-permute-done((bf16[512,768]{1,0:T(8,128)(2,1)}, bf16[512,768]{1,0:T(8,128)(2,1)S(1)}, u32[]{:S(2)}, u32[]{:S(2)}) %collective-permute-start) | collective-permute-done | bytes 786464 | tf_op jit(solution)/shard_map/ppermute | solution.py:31
  20.6 3.0 %collective-permute-done.1.behind_ref.refs_4_ = bf16[512,768]{1,0:T(8,128)(2,1)S(1)} collective-permute-done((bf16[512,768]{1,0:T(8,128)(2,1)}, bf16[512,768]{1,0:T(8,128)(2,1)S(1)}, u32[]{:S(2)}, u32[]{:S(2)}) %collective-permute-start.1) | collective-permute-done | bytes 786464 | tf_op jit(solution)/shard_map/ppermute | solution.py:31
  23.5 0.9 copy-done.6
  24.4 2.0 %shard_map.101 = (bf16[256,768]{1,0:T(8,128)(2,1)}, bf16[256,768]{1,0:T(8,128)(2,1)}) custom-call(bf16[512,768]{1,0:T(8,128)(2,1)} %copy-done.5, bf16[512,768]{1,0:T(8,128)(2,1)} %copy-done.6, bf16[512,768]{1,0:T(8,128)(2,1)} %bitcast_select_fusion._.refs_0_), custom_call_target="tpu_custom_call" | custom-call | flops 10000000000 | bytes 1000 | tf_op jit(solution)/shard_map/pallas_call | solution.py:86
  26.5 1.3 slice.20
  28.5 1.9 %collective-permute-start.2 = (bf16[16,32,768]{2,1,0:T(8,128)(2,1)S(1)}, bf16[16,32,768]{2,1,0:T(8,128)(2,1)S(1)}, u32[]{:S(2)}, u32[]{:S(2)}) collective-permute-start(bf16[16,32,768]{2,1,0:T(8,128)(2,1)S(1)} %broadcast_multiply_fusion), channel_id=1, source_target_pairs={{0,1},{1,0},{2,3},{3,2},{4,5},{5,4},{6,7},{7,6},{8,9},{9,8},{10,11... | collective-permute-start | bytes 2359304 | tf_op jit(solution)/shard_map/ppermute | solution.py:26
  30.4 1.2 collective-permute-start.7
  33.8 1.0 fusion.5
  35.3 3.2 %collective-permute-start.4 = (f32[2,4,128]{2,1,0:T(4,128)S(1)}, f32[2,4,128]{2,1,0:T(4,128)S(1)}, u32[]{:S(2)}, u32[]{:S(2)}) collective-permute-start(f32[2,4,128]{2,1,0:T(4,128)S(1)} %pad_maximum_fusion.2.refs_3_), channel_id=1, source_target_pairs={{0,64},{32,96},{64,0},{96,32},{1,65},{33,97},{65,1},{97,33},{2,66}... | collective-permute-start | bytes 12296 | tf_op jit(solution)/shard_map/ppermute | solution.py:31
  38.5 4.8 %collective-permute-done.6.refs_2_.refs_1_ = bf16[256,768]{1,0:T(8,128)(2,1)S(1)} collective-permute-done((bf16[256,768]{1,0:T(8,128)(2,1)S(1)}, bf16[256,768]{1,0:T(8,128)(2,1)S(1)}, u32[]{:S(2)}, u32[]{:S(2)}) %collective-permute-start.6) | collective-permute-done | bytes 393248 | tf_op jit(solution)/shard_map/ppermute | solution.py:31
  43.3 0.7 copy-done.4
  44.0 0.8 copy-done.3
  44.8 0.7 collective-permute-start.9
  45.5 0.7 collective-permute-start.10
  46.3 0.8 slice_bitcast_fusion.phi_ref
  47.7 6.0 %shard_map.102 = (bf16[256,2048]{1,0:T(8,128)(2,1)}, bf16[256,2048]{1,0:T(8,128)(2,1)}, bf16[256,768]{1,0:T(8,128)(2,1)}, f32[256,768]{1,0:T(8,128)}, f32[256,1]...) custom-call(bf16[256,768]{1,0:T(8,128)(2,1)} %slice_bitcast_fusion.phi_ref, f32[1,2048]{1,0:T(1,128)} %bitcast.69, ...), custom_call_target="tpu_custom_call" | custom-call | flops 1000 | bytes 1000 | tf_op jit(solution)/shard_map/pallas_call | solution.py:86
  53.7 19.9 %all_to_all.25 = bf16[32,8,768]{2,1,0:T(8,128)(2,1)} all-to-all(bf16[32,8,768]{2,1,0:T(8,128)(2,1)} %bitcast.66), channel_id=1, replica_groups=mesh['x'=4,'y'=4,'z'=4,'core'=2] {'y','z','core'}, dimensions={0} | all-to-all | bytes 786432 | tf_op jit(solution)/shard_map/all_to_all | solution.py:43
  73.6 8.6 %shard_map.103 = (bf16[256,3072]{1,0:T(8,128)(2,1)}, bf16[256,3072]{1,0:T(8,128)(2,1)}, bf16[256,768]{1,0:T(8,128)(2,1)}) custom-call(bf16[256,768]{1,0:T(8,128)(2,1)} %bitcast.60, bf16[768,3072]{1,0:T(8,128)(2,1)} %bitcast.40, bf16[3072,768]{1,0:T(8,128)(2,1)} %bitcast.42), custom_call_target="tpu_custom_call" | custom-call | flops 1000 | bytes 1000 | tf_op jit(solution)/shard_map/pallas_call | solution.py:86
  83.7 4.1 %shard_map.106 = bf16[256,1536]{1,0:T(8,128)(2,1)} custom-call(bf16[256,2048]{1,0:T(8,128)(2,1)} %get-tuple-element.33.combine_ref, bf16[256,768]{1,0:T(8,128)(2,1)} %get-tuple-element.32._.output_ref, bf16[512,768]{1,0:T(8,128)(2,1)} %shard_map.105.refs_0_.grad_ref, bf16[512,768]{1,0:T(8,128)(2,1)} %copy-done.7, bf16[512,768]{1,0:T(8,128)(2,1)} %copy-done.8, ...), custom_call_target="tpu_custom_call" | custom-call | flops 1000 | bytes 1000 | tf_op jit(solution)/shard_map/pallas_call | solution.py:86
  87.9 8.3 %all-to-all-start.2 = ((bf16[32,8,1536]{2,1,0:T(8,128)(2,1)}), bf16[32,8,1536]{2,1,0:T(8,128)(2,1)S(1)}, u32[]{:S(2)}, u32[]{:S(2)}) async-start(bf16[32,8,1536]{2,1,0:T(8,128)(2,1)} %bitcast.62), calls=%async_computation.2 | async-start | bytes 1572864 | tf_op jit(solution)/shard_map/all_to_all | solution.py:43
  96.1 0.9 broadcast_in_dim.38.live_ref
  97.0 4.3 %shard_map.104._.combine_ref = bf16[512,1024]{1,0:T(8,128)(2,1)} custom-call(f32[512,128]{1,0:T(8,128)} %broadcast_in_dim.38.live_ref, bf16[512,768]{1,0:T(8,128)(2,1)} %bitcast.53, bf16[1024,768]{1,0:T(8,128)(2,1)} %bitcast.48, bf16[256,768]{1,0:T(8,128)(2,1)} %get-tuple-element.32._.output_ref), custom_call_target="tpu_custom_call" | custom-call | flops 1000 | bytes 1000 | tf_op jit(solution)/shard_map/pallas_call | solution.py:86
  101.3 9.0 %all-to-all-done.2 = bf16[32,8,1536]{2,1,0:T(8,128)(2,1)S(1)} async-done(((bf16[32,8,1536]{2,1,0:T(8,128)(2,1)}), bf16[32,8,1536]{2,1,0:T(8,128)(2,1)S(1)}, u32[]{:S(2)}, u32[]{:S(2)}) %all-to-all-start.2) | async-done | bytes 786464 | tf_op jit(solution)/shard_map/all_to_all | solution.py:43
  110.3 0.9 copy-done
  111.2 4.9 %shard_map.107 = (f32[256,2048]{1,0:T(8,128)}, bf16[272,768]{1,0:T(8,128)(2,1)}) custom-call(bf16[256,1536]{1,0:T(8,128)(2,1)} %bitcast.44, bf16[512,1024]{1,0:T(8,128)(2,1)} %shard_map.104._.combine_ref, bf16[256,2048]{1,0:T(8,128)(2,1)} %get-tuple-element.33.combine_ref, f32[256,1]{1,0:T(8,128)} %get-tuple-element.34.top_ref, ...), custom_call_target="tpu_custom_call" | custom-call | flops 1000 | bytes 1000 | tf_op jit(solution)/shard_map/pallas_call | solution.py:86
  116.1 1.2 collective-permute-start.11
  118.0 8.3 %shard_map.109 = (bf16[256,3072]{1,0:T(8,128)(2,1)}, bf16[256,768]{1,0:T(8,128)(2,1)}) custom-call(bf16[256,1536]{1,0:T(8,128)(2,1)} %bitcast.45, bf16[256,3072]{1,0:T(8,128)(2,1)} %get-tuple-element.39.slope_ref, bf16[768,3072]{1,0:T(8,128)(2,1)} %bitcast.41, bf16[3072,768]{1,0:T(8,128)(2,1)} %bitcast.43, bf16[272,768]{1,0:T(8,128)(2,1)} %get-tuple-element.36.refs_0_._), custom_call_target="tpu_custom_call" | custom-call | flops 1000 | bytes 1000 | tf_op jit(solution)/shard_map/pallas_call | solution.py:86
  126.3 4.7 %all-to-all-start.3 = ((bf16[32,8,768]{2,1,0:T(8,128)(2,1)}), bf16[32,8,768]{2,1,0:T(8,128)(2,1)S(1)}, u32[]{:S(2)}, u32[]{:S(2)}) async-start(bf16[32,8,768]{2,1,0:T(8,128)(2,1)} %bitcast.65), calls=%async_computation.3 | async-start | bytes 786432 | tf_op jit(solution)/shard_map/all_to_all | solution.py:43
  131.0 7.1 %shard_map.110 = (bf16[768,3072]{1,0:T(8,128)(2,1)}, bf16[3072,768]{1,0:T(8,128)(2,1)}) custom-call(bf16[256,768]{1,0:T(8,128)(2,1)} %bitcast.61, bf16[256,1536]{1,0:T(8,128)(2,1)} %bitcast.46, bf16[256,3072]{1,0:T(8,128)(2,1)} %get-tuple-element.43.hidden_ref, bf16[256,3072]{1,0:T(8,128)(2,1)} %get-tuple-element.44.pre_ref), custom_call_target="tpu_custom_call" | custom-call | flops 1000 | bytes 1000 | tf_op jit(solution)/shard_map/pallas_call | solution.py:86
  138.1 3.2 %all-to-all-done.3 = bf16[32,8,768]{2,1,0:T(8,128)(2,1)S(1)} async-done(((bf16[32,8,768]{2,1,0:T(8,128)(2,1)}), bf16[32,8,768]{2,1,0:T(8,128)(2,1)S(1)}, u32[]{:S(2)}, u32[]{:S(2)}) %all-to-all-start.3) | async-done | bytes 393248 | tf_op jit(solution)/shard_map/all_to_all | solution.py:43
  141.3 0.7 copy-done.11
  142.1 2.6 %shard_map.111 = (bf16[272,768]{1,0:T(8,128)(2,1)}, f32[256,1]{1,0:T(8,128)}) custom-call(bf16[256,768]{1,0:T(8,128)(2,1)} %bitcast.64, f32[256,768]{1,0:T(8,128)} %get-tuple-element.41.normed_ref, f32[256,1]{1,0:T(8,128)} %get-tuple-element.42.factor_ref, bf16[3072,768]{1,0:T(8,128)(2,1)} %get-tuple-element.45._down, bf16[768,3072]{1,0:T(8,128)(2,1)} %get-tuple-element.46._up), custom_call_target="tpu_custom_call" | custom-call | flops 1000 | bytes 1000 | tf_op jit(solution)/shard_map/pallas_call | solution.py:86
  144.7 2.1 %collective-permute-start.14 = (bf16[272,768]{1,0:T(8,128)(2,1)}, bf16[272,768]{1,0:T(8,128)(2,1)S(1)}, u32[]{:S(2)}, u32[]{:S(2)}) collective-permute-start(bf16[272,768]{1,0:T(8,128)(2,1)} %get-tuple-element.47.refs_4_.grad_ref), channel_id=1, source_target_pairs={{0,96},{32,0},{64,32},{96,64},{1,97},{33,1},{65,33},{97,65},{2,98}... | collective-permute-start | bytes 1253384 | tf_op jit(solution)/shard_map/ppermute | solution.py:31
  146.8 1.5 collective-permute-start.15
  149.4 0.8 copy-done.15
  150.2 1.4 shard_map.113.row_ref
  151.6 6.3 %shard_map.114 = bf16[256,768]{1,0:T(8,128)(2,1)} custom-call(bf16[272,768]{1,0:T(8,128)(2,1)} %get-tuple-element.47.refs_4_.grad_ref, bf16[256,2048]{1,0:T(8,128)(2,1)} %get-tuple-element.33.combine_ref, f32[256,2048]{1,0:T(8,128)} %get-tuple-element.49.combine_grad_ref, f32[1,2048]{1,0:T(1,128)} %shard_map.113.row_ref, ...), custom_call_target="tpu_custom_call" | custom-call | flops 1000 | bytes 1000 | tf_op jit(solution)/shard_map/pallas_call | solution.py:86
  157.9 5.0 %all-to-all-start.4 = ((bf16[32,8,768]{2,1,0:T(8,128)(2,1)}), bf16[32,8,768]{2,1,0:T(8,128)(2,1)S(1)}, u32[]{:S(2)}, u32[]{:S(2)}) async-start(bf16[32,8,768]{2,1,0:T(8,128)(2,1)} %bitcast.63), calls=%async_computation.4 | async-start | bytes 786432 | tf_op jit(solution)/shard_map/all_to_all | solution.py:43
  163.0 4.8 %shard_map.108 = (bf16[512,768]{1,0:T(8,128)(2,1)}, bf16[512,1024]{1,0:T(8,128)(2,1)}) custom-call(bf16[512,1024]{1,0:T(8,128)(2,1)} %shard_map.104._.combine_ref, bf16[512,768]{1,0:T(8,128)(2,1)} %shard_map.105.refs_0_.grad_ref, bf16[272,768]{1,0:T(8,128)(2,1)} %get-tuple-element.36.refs_0_._, bf16[272,768]{1,0:T(8,128)(2,1)} %copy-done.13, ...), custom_call_target="tpu_custom_call" | custom-call | flops 1000 | bytes 1000 | tf_op jit(solution)/shard_map/pallas_call | solution.py:86
  167.8 1.3 collective-permute-done.16.refs_7_
  169.1 0.8 copy-done.20
  169.8 7.4 %shard_map.112 = (bf16[512,768]{1,0:T(8,128)(2,1)}, f32[8,128]{1,0:T(8,128)}) custom-call(f32[512,128]{1,0:T(8,128)} %broadcast_in_dim.38.live_ref, bf16[512,1024]{1,0:T(8,128)(2,1)} %get-tuple-element.38.logit_ref, bf16[512,768]{1,0:T(8,128)(2,1)} %bitcast.55, bf16[1024,768]{1,0:T(8,128)(2,1)} %bitcast.49, bf16[272,768]{1,0:T(8,128)(2,1)} %get-tuple-element.36.refs_0_._, ...), custom_call_target="tpu_custom_call" | custom-call | flops 5000000000 | bytes 1000 | tf_op jit(solution)/shard_map/pallas_call | solution.py:86
  177.2 0.7 copy-done.10
  178.0 1.7 shard_map.115
  (74 shorter events, 6.6 us)
Async XLA Ops:
  0.6 12.9 %copy-start.17 = (s32[1,512]{1,0:T(1,128)S(1)}, s32[1,512]{1,0:T(1,128)}, u32[]{:S(2)}) copy-start(s32[1,512]{1,0:T(1,128)} %param.7) | copy-start | bytes 6148
  0.6 13.0 %copy-start.12 = (bf16[1,512,768]{2,1,0:T(8,128)(2,1)S(1)}, bf16[1,512,768]{2,1,0:T(8,128)(2,1)}, u32[]{:S(2)}) copy-start(bf16[1,512,768]{2,1,0:T(8,128)(2,1)} %param.11) | copy-start | bytes 2359300
  0.7 19.9 %collective-permute-start = (bf16[512,768]{1,0:T(8,128)(2,1)}, bf16[512,768]{1,0:T(8,128)(2,1)S(1)}, u32[]{:S(2)}, u32[]{:S(2)}) collective-permute-start(bf16[512,768]{1,0:T(8,128)(2,1)} %bitcast.50), channel_id=1, source_target_pairs={{0,96},{32,0},{64,32},{96,64},{1,97},{33,1},{65,33},{97,65},{2,98}... | collective-permute-start | bytes 2359304 | tf_op jit(solution)/shard_map/ppermute | solution.py:31
  4.0 19.5 %collective-permute-start.1 = (bf16[512,768]{1,0:T(8,128)(2,1)}, bf16[512,768]{1,0:T(8,128)(2,1)S(1)}, u32[]{:S(2)}, u32[]{:S(2)}) collective-permute-start(bf16[512,768]{1,0:T(8,128)(2,1)} %bitcast.51), channel_id=1, source_target_pairs={{0,32},{32,64},{64,96},{96,0},{1,33},{33,65},{65,97},{97,1},{2,34}... | collective-permute-start | bytes 2359304 | tf_op jit(solution)/shard_map/ppermute | solution.py:31
  5.8 22.6 %all-to-all-start = ((bf16[16,32,768]{2,1,0:T(8,128)(2,1)}), bf16[16,32,768]{2,1,0:T(8,128)(2,1)S(1)}, u32[]{:S(2)}, u32[]{:S(2)}) async-start(bf16[16,32,768]{2,1,0:T(8,128)(2,1)} %broadcast_in_dim.39), calls=%async_computation | async-start | bytes 1572864 | tf_op jit(solution)/shard_map/all_to_all | solution.py:43
  20.6 3.0 %copy-start.5 = (bf16[512,768]{1,0:T(8,128)(2,1)}, bf16[512,768]{1,0:T(8,128)(2,1)S(1)}, u32[]{:S(2)}) copy-start(bf16[512,768]{1,0:T(8,128)(2,1)S(1)} %collective-permute-done.ahead_ref.refs_1_) | copy-start | bytes 2359300
  23.5 0.9 copy-start.6
  26.4 4.0 %copy-start.21 = (bf16[256,768]{1,0:T(8,128)(2,1)S(1)}, bf16[256,768]{1,0:T(8,128)(2,1)}, u32[]{:S(2)}) copy-start(bf16[256,768]{1,0:T(8,128)(2,1)} %get-tuple-element.29) | copy-start | bytes 1179652
  26.4 5.2 %copy-start.22 = (bf16[256,768]{1,0:T(8,128)(2,1)S(1)}, bf16[256,768]{1,0:T(8,128)(2,1)}, u32[]{:S(2)}) copy-start(bf16[256,768]{1,0:T(8,128)(2,1)} %get-tuple-element.30) | copy-start | bytes 1179652
  28.5 3.9 %collective-permute-start.2 = (bf16[16,32,768]{2,1,0:T(8,128)(2,1)S(1)}, bf16[16,32,768]{2,1,0:T(8,128)(2,1)S(1)}, u32[]{:S(2)}, u32[]{:S(2)}) collective-permute-start(bf16[16,32,768]{2,1,0:T(8,128)(2,1)S(1)} %broadcast_multiply_fusion), channel_id=1, source_target_pairs={{0,1},{1,0},{2,3},{3,2},{4,5},{5,4},{6,7},{7,6},{8,9},{9,8},{10,11... | collective-permute-start | bytes 2359304 | tf_op jit(solution)/shard_map/ppermute | solution.py:26
  30.4 12.9 %collective-permute-start.7 = (bf16[256,768]{1,0:T(8,128)(2,1)S(1)}, bf16[256,768]{1,0:T(8,128)(2,1)S(1)}, u32[]{:S(2)}, u32[]{:S(2)}) collective-permute-start(bf16[256,768]{1,0:T(8,128)(2,1)S(1)} %copy-done.21), channel_id=1, source_target_pairs={{0,96},{32,0},{64,32},{96,64},{1,97},{33,1},{65,33},{97,65},{2,98}... | collective-permute-start | bytes 1179656 | tf_op jit(solution)/shard_map/ppermute | solution.py:31
  31.7 11.6 %collective-permute-start.6 = (bf16[256,768]{1,0:T(8,128)(2,1)S(1)}, bf16[256,768]{1,0:T(8,128)(2,1)S(1)}, u32[]{:S(2)}, u32[]{:S(2)}) collective-permute-start(bf16[256,768]{1,0:T(8,128)(2,1)S(1)} %copy-done.22), channel_id=1, source_target_pairs={{0,32},{32,64},{64,96},{96,0},{1,33},{33,65},{65,97},{97,1},{2,34}... | collective-permute-start | bytes 1179656 | tf_op jit(solution)/shard_map/ppermute | solution.py:31
  32.7 1.1 copy-start.2
  33.2 13.0 %copy-start.1 = (bf16[4,256,768]{2,1,0:T(8,128)(2,1)}, bf16[4,256,768]{2,1,0:T(8,128)(2,1)S(1)}, u32[]{:S(2)}) copy-start(bf16[4,256,768]{2,1,0:T(8,128)(2,1)S(1)} %fusion) | copy-start | bytes 4718596
  35.3 8.0 %copy-start.16 = (f32[2,4,128]{2,1,0:T(4,128)}, f32[2,4,128]{2,1,0:T(4,128)S(1)}, u32[]{:S(2)}) copy-start(f32[2,4,128]{2,1,0:T(4,128)S(1)} %pad_maximum_fusion.2.refs_3_) | copy-start | bytes 12292
  35.3 10.3 %collective-permute-start.5 = (f32[2,4,128]{2,1,0:T(4,128)S(1)}, f32[2,4,128]{2,1,0:T(4,128)S(1)}, u32[]{:S(2)}, u32[]{:S(2)}) collective-permute-start(f32[2,4,128]{2,1,0:T(4,128)S(1)} %pad_maximum_fusion.2.refs_3_), channel_id=1, source_target_pairs={{0,32},{32,64},{64,96},{96,0},{1,33},{33,65},{65,97},{97,1},{2,34}... | collective-permute-start | bytes 12296 | tf_op jit(solution)/shard_map/ppermute | solution.py:31
  35.3 11.7 %collective-permute-start.4 = (f32[2,4,128]{2,1,0:T(4,128)S(1)}, f32[2,4,128]{2,1,0:T(4,128)S(1)}, u32[]{:S(2)}, u32[]{:S(2)}) collective-permute-start(f32[2,4,128]{2,1,0:T(4,128)S(1)} %pad_maximum_fusion.2.refs_3_), channel_id=1, source_target_pairs={{0,64},{32,96},{64,0},{96,32},{1,65},{33,97},{65,1},{97,33},{2,66}... | collective-permute-start | bytes 12296 | tf_op jit(solution)/shard_map/ppermute | solution.py:31
  38.5 8.5 %collective-permute-start.3 = (f32[2,4,128]{2,1,0:T(4,128)S(1)}, f32[2,4,128]{2,1,0:T(4,128)S(1)}, u32[]{:S(2)}, u32[]{:S(2)}) collective-permute-start(f32[2,4,128]{2,1,0:T(4,128)S(1)} %pad_maximum_fusion.2.refs_3_), channel_id=1, source_target_pairs={{0,96},{32,0},{64,32},{96,64},{1,97},{33,1},{65,33},{97,65},{2,98}... | collective-permute-start | bytes 12296 | tf_op jit(solution)/shard_map/ppermute | solution.py:31
  43.3 0.7 copy-start.4
  44.0 0.8 copy-start.3
  44.8 37.5 %collective-permute-start.8 = (bf16[512,768]{1,0:T(8,128)(2,1)}, bf16[512,768]{1,0:T(8,128)(2,1)S(1)}, u32[]{:S(2)}, u32[]{:S(2)}) collective-permute-start(bf16[512,768]{1,0:T(8,128)(2,1)} %shard_map.105.refs_0_.grad_ref), channel_id=1, source_target_pairs={{0,96},{32,0},{64,32},{96,64},{1,97},{33,1},{65,33},{97,65},{2,98}... | collective-permute-start | bytes 2359304 | tf_op jit(solution)/shard_map/ppermute | solution.py:31
  44.8 37.5 %collective-permute-start.9 = (bf16[512,768]{1,0:T(8,128)(2,1)}, bf16[512,768]{1,0:T(8,128)(2,1)S(1)}, u32[]{:S(2)}, u32[]{:S(2)}) collective-permute-start(bf16[512,768]{1,0:T(8,128)(2,1)} %shard_map.105.refs_0_.grad_ref), channel_id=1, source_target_pairs={{0,64},{32,96},{64,0},{96,32},{1,65},{33,97},{65,1},{97,33},{2,66}... | collective-permute-start | bytes 2359304 | tf_op jit(solution)/shard_map/ppermute | solution.py:31
  45.5 37.3 %collective-permute-start.10 = (bf16[512,768]{1,0:T(8,128)(2,1)}, bf16[512,768]{1,0:T(8,128)(2,1)S(1)}, u32[]{:S(2)}, u32[]{:S(2)}) collective-permute-start(bf16[512,768]{1,0:T(8,128)(2,1)} %shard_map.105.refs_0_.grad_ref), channel_id=1, source_target_pairs={{0,32},{32,64},{64,96},{96,0},{1,33},{33,65},{65,97},{97,1},{2,34}... | collective-permute-start | bytes 2359304 | tf_op jit(solution)/shard_map/ppermute | solution.py:31
  82.3 0.9 copy-start.7
  82.3 1.2 copy-start.8
  82.8 0.9 copy-start.9
  87.9 22.5 %all-to-all-start.2 = ((bf16[32,8,1536]{2,1,0:T(8,128)(2,1)}), bf16[32,8,1536]{2,1,0:T(8,128)(2,1)S(1)}, u32[]{:S(2)}, u32[]{:S(2)}) async-start(bf16[32,8,1536]{2,1,0:T(8,128)(2,1)} %bitcast.62), calls=%async_computation.2 | async-start | bytes 1572864 | tf_op jit(solution)/shard_map/all_to_all | solution.py:43
  110.3 0.9 copy-start
  116.1 32.3 %collective-permute-start.11 = (bf16[272,768]{1,0:T(8,128)(2,1)}, bf16[272,768]{1,0:T(8,128)(2,1)S(1)}, u32[]{:S(2)}, u32[]{:S(2)}) collective-permute-start(bf16[272,768]{1,0:T(8,128)(2,1)} %get-tuple-element.36.refs_0_._), channel_id=1, source_target_pairs={{0,96},{32,0},{64,32},{96,64},{1,97},{33,1},{65,33},{97,65},{2,98}... | collective-permute-start | bytes 1253384 | tf_op jit(solution)/shard_map/ppermute | solution.py:31
  117.3 31.4 %collective-permute-start.12 = (bf16[272,768]{1,0:T(8,128)(2,1)}, bf16[272,768]{1,0:T(8,128)(2,1)S(1)}, u32[]{:S(2)}, u32[]{:S(2)}) collective-permute-start(bf16[272,768]{1,0:T(8,128)(2,1)} %get-tuple-element.36.refs_0_._), channel_id=1, source_target_pairs={{0,64},{32,96},{64,0},{96,32},{1,65},{33,97},{65,1},{97,33},{2,66}... | collective-permute-start | bytes 1253384 | tf_op jit(solution)/shard_map/ppermute | solution.py:31
  117.5 31.1 %collective-permute-start.13 = (bf16[272,768]{1,0:T(8,128)(2,1)}, bf16[272,768]{1,0:T(8,128)(2,1)S(1)}, u32[]{:S(2)}, u32[]{:S(2)}) collective-permute-start(bf16[272,768]{1,0:T(8,128)(2,1)} %get-tuple-element.36.refs_0_._), channel_id=1, source_target_pairs={{0,32},{32,64},{64,96},{96,0},{1,33},{33,65},{65,97},{97,1},{2,34}... | collective-permute-start | bytes 1253384 | tf_op jit(solution)/shard_map/ppermute | solution.py:31
  126.3 15.0 %all-to-all-start.3 = ((bf16[32,8,768]{2,1,0:T(8,128)(2,1)}), bf16[32,8,768]{2,1,0:T(8,128)(2,1)S(1)}, u32[]{:S(2)}, u32[]{:S(2)}) async-start(bf16[32,8,768]{2,1,0:T(8,128)(2,1)} %bitcast.65), calls=%async_computation.3 | async-start | bytes 786432 | tf_op jit(solution)/shard_map/all_to_all | solution.py:43
  141.3 0.7 copy-start.11
  144.7 23.1 %collective-permute-start.14 = (bf16[272,768]{1,0:T(8,128)(2,1)}, bf16[272,768]{1,0:T(8,128)(2,1)S(1)}, u32[]{:S(2)}, u32[]{:S(2)}) collective-permute-start(bf16[272,768]{1,0:T(8,128)(2,1)} %get-tuple-element.47.refs_4_.grad_ref), channel_id=1, source_target_pairs={{0,96},{32,0},{64,32},{96,64},{1,97},{33,1},{65,33},{97,65},{2,98}... | collective-permute-start | bytes 1253384 | tf_op jit(solution)/shard_map/ppermute | solution.py:31
  146.8 20.9 %collective-permute-start.15 = (bf16[272,768]{1,0:T(8,128)(2,1)}, bf16[272,768]{1,0:T(8,128)(2,1)S(1)}, u32[]{:S(2)}, u32[]{:S(2)}) collective-permute-start(bf16[272,768]{1,0:T(8,128)(2,1)} %get-tuple-element.47.refs_4_.grad_ref), channel_id=1, source_target_pairs={{0,64},{32,96},{64,0},{96,32},{1,65},{33,97},{65,1},{97,33},{2,66}... | collective-permute-start | bytes 1253384 | tf_op jit(solution)/shard_map/ppermute | solution.py:31
  148.4 0.8 copy-start.13
  148.4 20.7 %collective-permute-start.16 = (bf16[272,768]{1,0:T(8,128)(2,1)}, bf16[272,768]{1,0:T(8,128)(2,1)S(1)}, u32[]{:S(2)}, u32[]{:S(2)}) collective-permute-start(bf16[272,768]{1,0:T(8,128)(2,1)} %get-tuple-element.47.refs_4_.grad_ref), channel_id=1, source_target_pairs={{0,32},{32,64},{64,96},{96,0},{1,33},{33,65},{65,97},{97,1},{2,34}... | collective-permute-start | bytes 1253384 | tf_op jit(solution)/shard_map/ppermute | solution.py:31
  148.6 0.8 copy-start.14
  149.4 0.8 copy-start.15
  157.9 19.3 %all-to-all-start.4 = ((bf16[32,8,768]{2,1,0:T(8,128)(2,1)}), bf16[32,8,768]{2,1,0:T(8,128)(2,1)S(1)}, u32[]{:S(2)}, u32[]{:S(2)}) async-start(bf16[32,8,768]{2,1,0:T(8,128)(2,1)} %bitcast.63), calls=%async_computation.4 | async-start | bytes 786432 | tf_op jit(solution)/shard_map/all_to_all | solution.py:43
  167.7 1.3 copy-start.18
  167.7 1.3 copy-start.19
  169.0 0.8 copy-start.20
  177.2 0.8 copy-start.10

commit v5 on v4

--- a/solution.py
+++ b/solution.py
@@ -47,11 +47,11 @@
     return lax.dynamic_slice_in_dim(jnp.concatenate([blocks, blocks[:-1]]), first, blocks.shape[0], 0)
 
 
-def gather_phi(phi, one):
+def gather_phi(phi, ahead_half):
     rows = phi.T
     planes = lax.axis_size("x")
     chips = lax.axis_size("y") * lax.axis_size("z")
-    mine = exchange(jnp.broadcast_to(rows[None], (chips,) + rows.shape), PLANE) * one
+    mine = tied(exchange(jnp.broadcast_to(rows[None], (chips,) + rows.shape), PLANE), ahead_half)
     other = swap_cores(mine)
     first = lax.axis_index("core") == 0
     both = jnp.stack([jnp.where(first, mine, other), jnp.where(first, other, mine)], axis=1)
@@ -66,10 +66,6 @@
     half = 0.5 * (1.0 + t)
     slope = half + 0.5 * scale * v * (1.0 - t * t) * (1.0 + 3.0 * 0.044715 * square)
     return v * half, slope
-
-
-def unit(*arrays):
-    return sum(a[0, 0].astype(BF16) * 0 for a in arrays) + jnp.ones((), BF16)
 
 
 LIMIT = 56 * 1024 * 1024
@@ -352,7 +348,7 @@
         work=10**10,
     )
     far = along_x(behind_half, 1), along_x(ahead_half, -1)
-    phi_groups = gather_phi(phi, unit(ahead_half))
+    phi_groups = gather_phi(phi, ahead_half)
     own_slots = phi_groups.shape[1]
     per_expert = own_slots // experts
     phi_all = phi_groups.reshape(-1, features)

time: 181 us -> 179 us (0.989)
  blocking collectives: 19.9 us -> 17.9 us
    all_to_all x4, starting transfers between devices: 25.7 us -> 23.4 us  [exchange(): return lax.all_to_all(values, axes, 0, 0, tiled=True)]
    all_to_all x1, blocking collectives: 19.9 us -> 17.9 us  [exchange(): return lax.all_to_all(values, axes, 0, 0, tiled=True)]
    ppermute x16, starting transfers between devices: 15.5 us -> 17.3 us  [along_x(): return lax.ppermute(values, 'x', [(i, (i + steps) % n) for i in range(n)])]
    unnamed x46 -> x48, local copies, waits for them, and re-layouts: 8.54 us -> 9.39 us
  transfers between devices with their start and end apart: 21 -> 21, of which waited for: 8 -> 7; matrix products, arithmetic and copies ran while one was open for 5% -> 5% of each run, Pallas kernels for 33% -> 33%
where the time goes in v5:
time: 179 us; the launch traced here: 178 us
  Pallas kernels  69.6 us (39%)
  starting transfers between devices  43.1 us (24%)
  waiting for transfers between devices  28.5 us (16%)
  blocking collectives  17.9 us (10%)
  local copies, waits for them, and re-layouts  13.6 us (8%)
  other arithmetic  3.48 us (2%)
    pallas_call x14, Pallas kernels, call(): pl.pallas_call(kernel, grid=(steps,), in_specs=[spec(block, where) for _,...  69.6 us
    all_to_all x4, starting transfers between devices, exchange(): return lax.all_to_all(values, axes, 0, 0, tiled=True)  23.4 us
    all_to_all x1, blocking collectives, exchange(): return lax.all_to_all(values, axes, 0, 0, tiled=True)  17.9 us
    ppermute x16, starting transfers between devices, along_x(): return lax.ppermute(values, 'x', [(i, (i + steps) % n) for i in range(n)])  17.3 us
    ppermute x16, waiting for transfers between devices, along_x(): return lax.ppermute(values, 'x', [(i, (i + steps) % n) for i in range(n)])  16.3 us
    all_to_all x4, waiting for transfers between devices, exchange(): return lax.all_to_all(values, axes, 0, 0, tiled=True)  12.3 us
    unnamed x48, local copies, waits for them, and re-layouts  9.39 us
  transfers between devices with their start and end apart: 21, of which 7 were waited for; matrix products, arithmetic and copies ran while one was open for 5% of the time, Pallas kernels for 33%

profile of v5, /device:TPU:1, one launch (start us, length us, event | category | flops | bytes accessed | tf_op | source)
XLA Modules:
  0.0 178.2 jit_solution(3211258835897246643)
XLA Ops:
  0.7 3.4 %collective-permute-start = (bf16[512,768]{1,0:T(8,128)(2,1)}, bf16[512,768]{1,0:T(8,128)(2,1)S(1)}, u32[]{:S(2)}, u32[]{:S(2)}) collective-permute-start(bf16[512,768]{1,0:T(8,128)(2,1)} %bitcast.47), channel_id=1, source_target_pairs={{0,96},{32,0},{64,32},{96,64},{1,97},{33,1},{65,33},{97,65},{2,98}... | collective-permute-start | bytes 2359304 | tf_op jit(solution)/shard_map/ppermute | solution.py:31
  4.0 1.8 broadcast_in_dim.39
  5.8 7.8 %all-to-all-start = ((bf16[16,32,768]{2,1,0:T(8,128)(2,1)}), bf16[16,32,768]{2,1,0:T(8,128)(2,1)S(1)}, u32[]{:S(2)}, u32[]{:S(2)}) async-start(bf16[16,32,768]{2,1,0:T(8,128)(2,1)} %broadcast_in_dim.39), calls=%async_computation | async-start | bytes 1572864 | tf_op jit(solution)/shard_map/all_to_all | solution.py:43
  13.6 1.1 bitcast_select_fusion._.refs_0_
  14.7 5.9 %collective-permute-done.ahead_ref.refs_1_ = bf16[512,768]{1,0:T(8,128)(2,1)S(1)} collective-permute-done((bf16[512,768]{1,0:T(8,128)(2,1)}, bf16[512,768]{1,0:T(8,128)(2,1)S(1)}, u32[]{:S(2)}, u32[]{:S(2)}) %collective-permute-start) | collective-permute-done | bytes 786464 | tf_op jit(solution)/shard_map/ppermute | solution.py:31
  20.6 3.0 %collective-permute-done.1.behind_ref.refs_4_ = bf16[512,768]{1,0:T(8,128)(2,1)S(1)} collective-permute-done((bf16[512,768]{1,0:T(8,128)(2,1)}, bf16[512,768]{1,0:T(8,128)(2,1)S(1)}, u32[]{:S(2)}, u32[]{:S(2)}) %collective-permute-start.1) | collective-permute-done | bytes 786464 | tf_op jit(solution)/shard_map/ppermute | solution.py:31
  23.5 0.9 copy-done.7
  24.4 2.0 %shard_map.101 = (bf16[256,768]{1,0:T(8,128)(2,1)}, bf16[256,768]{1,0:T(8,128)(2,1)}) custom-call(bf16[512,768]{1,0:T(8,128)(2,1)} %copy-done.6, bf16[512,768]{1,0:T(8,128)(2,1)} %copy-done.7, bf16[512,768]{1,0:T(8,128)(2,1)} %bitcast_select_fusion._.refs_0_), custom_call_target="tpu_custom_call" | custom-call | flops 10000000000 | bytes 1000 | tf_op jit(solution)/shard_map/pallas_call | solution.py:82
  26.5 0.9 copy-done.3
  27.3 2.4 %collective-permute-start.2 = (bf16[16,32,768]{2,1,0:T(8,128)(2,1)}, bf16[16,32,768]{2,1,0:T(8,128)(2,1)S(1)}, u32[]{:S(2)}, u32[]{:S(2)}) collective-permute-start(bf16[16,32,768]{2,1,0:T(8,128)(2,1)} %shard_map.102), channel_id=1, source_target_pairs={{0,1},{1,0},{2,3},{3,2},{4,5},{5,4},{6,7},{7,6},{8,9},{9,8},{10,11... | collective-permute-start | bytes 2359304 | tf_op jit(solution)/shard_map/ppermute | solution.py:26
  29.7 2.7 %collective-permute-start.7 = (bf16[256,768]{1,0:T(8,128)(2,1)S(1)}, bf16[256,768]{1,0:T(8,128)(2,1)S(1)}, u32[]{:S(2)}, u32[]{:S(2)}) collective-permute-start(bf16[256,768]{1,0:T(8,128)(2,1)S(1)} %copy-done.17), channel_id=1, source_target_pairs={{0,96},{32,0},{64,32},{96,64},{1,97},{33,1},{65,33},{97,65},{2,98}... | collective-permute-start | bytes 1179656 | tf_op jit(solution)/shard_map/ppermute | solution.py:31
  32.4 1.2 select_bitcast_fusion.1
  35.3 1.0 fusion.5
  36.8 3.8 %collective-permute-start.4 = (f32[2,4,128]{2,1,0:T(4,128)S(1)}, f32[2,4,128]{2,1,0:T(4,128)S(1)}, u32[]{:S(2)}, u32[]{:S(2)}) collective-permute-start(f32[2,4,128]{2,1,0:T(4,128)S(1)} %pad_maximum_fusion.2.refs_3_), channel_id=1, source_target_pairs={{0,64},{32,96},{64,0},{96,32},{1,65},{33,97},{65,1},{97,33},{2,66}... | collective-permute-start | bytes 12296 | tf_op jit(solution)/shard_map/ppermute | solution.py:31
  40.6 3.5 %collective-permute-done.6.refs_2_.refs_1_ = bf16[256,768]{1,0:T(8,128)(2,1)S(1)} collective-permute-done((bf16[256,768]{1,0:T(8,128)(2,1)S(1)}, bf16[256,768]{1,0:T(8,128)(2,1)S(1)}, u32[]{:S(2)}, u32[]{:S(2)}) %collective-permute-start.6) | collective-permute-done | bytes 393248 | tf_op jit(solution)/shard_map/ppermute | solution.py:31
  44.9 0.8 copy-done.4
  45.6 0.8 collective-permute-start.9
  47.1 0.8 slice_bitcast_fusion.phi_ref
  48.5 6.0 %shard_map.103 = (bf16[256,2048]{1,0:T(8,128)(2,1)}, bf16[256,2048]{1,0:T(8,128)(2,1)}, bf16[256,768]{1,0:T(8,128)(2,1)}, f32[256,768]{1,0:T(8,128)}, f32[256,1]...) custom-call(bf16[256,768]{1,0:T(8,128)(2,1)} %slice_bitcast_fusion.phi_ref, f32[1,2048]{1,0:T(1,128)} %bitcast.66, ...), custom_call_target="tpu_custom_call" | custom-call | flops 1000 | bytes 1000 | tf_op jit(solution)/shard_map/pallas_call | solution.py:82
  54.5 17.9 %all_to_all.25 = bf16[32,8,768]{2,1,0:T(8,128)(2,1)} all-to-all(bf16[32,8,768]{2,1,0:T(8,128)(2,1)} %bitcast.63), channel_id=1, replica_groups=mesh['x'=4,'y'=4,'z'=4,'core'=2] {'y','z','core'}, dimensions={0} | all-to-all | bytes 786432 | tf_op jit(solution)/shard_map/all_to_all | solution.py:43
  72.4 8.6 %shard_map.104 = (bf16[256,3072]{1,0:T(8,128)(2,1)}, bf16[256,3072]{1,0:T(8,128)(2,1)}, bf16[256,768]{1,0:T(8,128)(2,1)}) custom-call(bf16[256,768]{1,0:T(8,128)(2,1)} %bitcast.57, bf16[768,3072]{1,0:T(8,128)(2,1)} %bitcast.37, bf16[3072,768]{1,0:T(8,128)(2,1)} %bitcast.39), custom_call_target="tpu_custom_call" | custom-call | flops 1000 | bytes 1000 | tf_op jit(solution)/shard_map/pallas_call | solution.py:82
  81.1 2.6 %collective-permute-done.10.refs_3_ = bf16[512,768]{1,0:T(8,128)(2,1)S(1)} collective-permute-done((bf16[512,768]{1,0:T(8,128)(2,1)}, bf16[512,768]{1,0:T(8,128)(2,1)S(1)}, u32[]{:S(2)}, u32[]{:S(2)}) %collective-permute-start.10) | collective-permute-done | bytes 786464 | tf_op jit(solution)/shard_map/ppermute | solution.py:31
  83.7 0.9 copy-done.10
  84.5 4.1 %shard_map.107 = bf16[256,1536]{1,0:T(8,128)(2,1)} custom-call(bf16[256,2048]{1,0:T(8,128)(2,1)} %get-tuple-element.33.combine_ref, bf16[256,768]{1,0:T(8,128)(2,1)} %get-tuple-element.32._.output_ref, bf16[512,768]{1,0:T(8,128)(2,1)} %shard_map.106.refs_0_.grad_ref, bf16[512,768]{1,0:T(8,128)(2,1)} %copy-done.8, bf16[512,768]{1,0:T(8,128)(2,1)} %copy-done.9, ...), custom_call_target="tpu_custom_call" | custom-call | flops 1000 | bytes 1000 | tf_op jit(solution)/shard_map/pallas_call | solution.py:82
  88.7 5.9 %all-to-all-start.2 = ((bf16[32,8,1536]{2,1,0:T(8,128)(2,1)}), bf16[32,8,1536]{2,1,0:T(8,128)(2,1)S(1)}, u32[]{:S(2)}, u32[]{:S(2)}) async-start(bf16[32,8,1536]{2,1,0:T(8,128)(2,1)} %bitcast.59), calls=%async_computation.2 | async-start | bytes 1572864 | tf_op jit(solution)/shard_map/all_to_all | solution.py:43
  94.6 0.8 broadcast_in_dim.38.live_ref
  95.5 4.3 %shard_map.105._.combine_ref = bf16[512,1024]{1,0:T(8,128)(2,1)} custom-call(f32[512,128]{1,0:T(8,128)} %broadcast_in_dim.38.live_ref, bf16[512,768]{1,0:T(8,128)(2,1)} %bitcast.50, bf16[1024,768]{1,0:T(8,128)(2,1)} %bitcast.45, bf16[256,768]{1,0:T(8,128)(2,1)} %get-tuple-element.32._.output_ref), custom_call_target="tpu_custom_call" | custom-call | flops 1000 | bytes 1000 | tf_op jit(solution)/shard_map/pallas_call | solution.py:82
  99.8 9.0 %all-to-all-done.2 = bf16[32,8,1536]{2,1,0:T(8,128)(2,1)S(1)} async-done(((bf16[32,8,1536]{2,1,0:T(8,128)(2,1)}), bf16[32,8,1536]{2,1,0:T(8,128)(2,1)S(1)}, u32[]{:S(2)}, u32[]{:S(2)}) %all-to-all-start.2) | async-done | bytes 786464 | tf_op jit(solution)/shard_map/all_to_all | solution.py:43
  108.9 0.9 copy-done
  109.7 4.9 %shard_map.108 = (f32[256,2048]{1,0:T(8,128)}, bf16[272,768]{1,0:T(8,128)(2,1)}) custom-call(bf16[256,1536]{1,0:T(8,128)(2,1)} %bitcast.41, bf16[512,1024]{1,0:T(8,128)(2,1)} %shard_map.105._.combine_ref, bf16[256,2048]{1,0:T(8,128)(2,1)} %get-tuple-element.33.combine_ref, f32[256,1]{1,0:T(8,128)} %get-tuple-element.34.top_ref, ...), custom_call_target="tpu_custom_call" | custom-call | flops 1000 | bytes 1000 | tf_op jit(solution)/shard_map/pallas_call | solution.py:82
  114.6 1.2 collective-permute-start.11
  116.5 8.3 %shard_map.110 = (bf16[256,3072]{1,0:T(8,128)(2,1)}, bf16[256,768]{1,0:T(8,128)(2,1)}) custom-call(bf16[256,1536]{1,0:T(8,128)(2,1)} %bitcast.42, bf16[256,3072]{1,0:T(8,128)(2,1)} %get-tuple-element.39.slope_ref, bf16[768,3072]{1,0:T(8,128)(2,1)} %bitcast.38, bf16[3072,768]{1,0:T(8,128)(2,1)} %bitcast.40, bf16[272,768]{1,0:T(8,128)(2,1)} %get-tuple-element.36.refs_0_._), custom_call_target="tpu_custom_call" | custom-call | flops 1000 | bytes 1000 | tf_op jit(solution)/shard_map/pallas_call | solution.py:82
  124.9 4.7 %all-to-all-start.3 = ((bf16[32,8,768]{2,1,0:T(8,128)(2,1)}), bf16[32,8,768]{2,1,0:T(8,128)(2,1)S(1)}, u32[]{:S(2)}, u32[]{:S(2)}) async-start(bf16[32,8,768]{2,1,0:T(8,128)(2,1)} %bitcast.62), calls=%async_computation.3 | async-start | bytes 786432 | tf_op jit(solution)/shard_map/all_to_all | solution.py:43
  129.6 7.1 %shard_map.111 = (bf16[768,3072]{1,0:T(8,128)(2,1)}, bf16[3072,768]{1,0:T(8,128)(2,1)}) custom-call(bf16[256,768]{1,0:T(8,128)(2,1)} %bitcast.58, bf16[256,1536]{1,0:T(8,128)(2,1)} %bitcast.43, bf16[256,3072]{1,0:T(8,128)(2,1)} %get-tuple-element.43.hidden_ref, bf16[256,3072]{1,0:T(8,128)(2,1)} %get-tuple-element.44.pre_ref), custom_call_target="tpu_custom_call" | custom-call | flops 1000 | bytes 1000 | tf_op jit(solution)/shard_map/pallas_call | solution.py:82
  136.7 3.2 %all-to-all-done.3 = bf16[32,8,768]{2,1,0:T(8,128)(2,1)S(1)} async-done(((bf16[32,8,768]{2,1,0:T(8,128)(2,1)}), bf16[32,8,768]{2,1,0:T(8,128)(2,1)S(1)}, u32[]{:S(2)}, u32[]{:S(2)}) %all-to-all-start.3) | async-done | bytes 393248 | tf_op jit(solution)/shard_map/all_to_all | solution.py:43
  139.9 0.7 copy-done.12
  140.6 2.6 %shard_map.112 = (bf16[272,768]{1,0:T(8,128)(2,1)}, f32[256,1]{1,0:T(8,128)}) custom-call(bf16[256,768]{1,0:T(8,128)(2,1)} %bitcast.61, f32[256,768]{1,0:T(8,128)} %get-tuple-element.41.normed_ref, f32[256,1]{1,0:T(8,128)} %get-tuple-element.42.factor_ref, bf16[3072,768]{1,0:T(8,128)(2,1)} %get-tuple-element.45._down, bf16[768,3072]{1,0:T(8,128)(2,1)} %get-tuple-element.46._up), custom_call_target="tpu_custom_call" | custom-call | flops 1000 | bytes 1000 | tf_op jit(solution)/shard_map/pallas_call | solution.py:82
  143.2 2.1 %collective-permute-start.14 = (bf16[272,768]{1,0:T(8,128)(2,1)}, bf16[272,768]{1,0:T(8,128)(2,1)S(1)}, u32[]{:S(2)}, u32[]{:S(2)}) collective-permute-start(bf16[272,768]{1,0:T(8,128)(2,1)} %get-tuple-element.47.refs_4_.grad_ref), channel_id=1, source_target_pairs={{0,96},{32,0},{64,32},{96,64},{1,97},{33,1},{65,33},{97,65},{2,98}... | collective-permute-start | bytes 1253384 | tf_op jit(solution)/shard_map/ppermute | solution.py:31
  145.3 1.5 collective-permute-start.15
  147.9 0.8 copy-done.16
  148.7 1.4 shard_map.114.row_ref
  150.1 6.3 %shard_map.115 = bf16[256,768]{1,0:T(8,128)(2,1)} custom-call(bf16[272,768]{1,0:T(8,128)(2,1)} %get-tuple-element.47.refs_4_.grad_ref, bf16[256,2048]{1,0:T(8,128)(2,1)} %get-tuple-element.33.combine_ref, f32[256,2048]{1,0:T(8,128)} %get-tuple-element.49.combine_grad_ref, f32[1,2048]{1,0:T(1,128)} %shard_map.114.row_ref, ...), custom_call_target="tpu_custom_call" | custom-call | flops 1000 | bytes 1000 | tf_op jit(solution)/shard_map/pallas_call | solution.py:82
  156.5 5.0 %all-to-all-start.4 = ((bf16[32,8,768]{2,1,0:T(8,128)(2,1)}), bf16[32,8,768]{2,1,0:T(8,128)(2,1)S(1)}, u32[]{:S(2)}, u32[]{:S(2)}) async-start(bf16[32,8,768]{2,1,0:T(8,128)(2,1)} %bitcast.60), calls=%async_computation.4 | async-start | bytes 786432 | tf_op jit(solution)/shard_map/all_to_all | solution.py:43
  161.5 4.7 %shard_map.109 = (bf16[512,768]{1,0:T(8,128)(2,1)}, bf16[512,1024]{1,0:T(8,128)(2,1)}) custom-call(bf16[512,1024]{1,0:T(8,128)(2,1)} %shard_map.105._.combine_ref, bf16[512,768]{1,0:T(8,128)(2,1)} %shard_map.106.refs_0_.grad_ref, bf16[272,768]{1,0:T(8,128)(2,1)} %get-tuple-element.36.refs_0_._, bf16[272,768]{1,0:T(8,128)(2,1)} %copy-done.14, ...), custom_call_target="tpu_custom_call" | custom-call | flops 1000 | bytes 1000 | tf_op jit(solution)/shard_map/pallas_call | solution.py:82
  166.3 1.3 collective-permute-done.16.refs_7_
  168.3 7.4 %shard_map.113 = (bf16[512,768]{1,0:T(8,128)(2,1)}, f32[8,128]{1,0:T(8,128)}) custom-call(f32[512,128]{1,0:T(8,128)} %broadcast_in_dim.38.live_ref, bf16[512,1024]{1,0:T(8,128)(2,1)} %get-tuple-element.38.logit_ref, bf16[512,768]{1,0:T(8,128)(2,1)} %bitcast.52, bf16[1024,768]{1,0:T(8,128)(2,1)} %bitcast.46, bf16[272,768]{1,0:T(8,128)(2,1)} %get-tuple-element.36.refs_0_._, ...), custom_call_target="tpu_custom_call" | custom-call | flops 5000000000 | bytes 1000 | tf_op jit(solution)/shard_map/pallas_call | solution.py:82
  175.8 0.7 copy-done.11
  176.5 1.7 shard_map.116
  (77 shorter events, 6.7 us)
Async XLA Ops:
  0.6 12.9 %copy-start.19 = (s32[1,512]{1,0:T(1,128)S(1)}, s32[1,512]{1,0:T(1,128)}, u32[]{:S(2)}) copy-start(s32[1,512]{1,0:T(1,128)} %param.7) | copy-start | bytes 6148
  0.6 13.0 %copy-start.13 = (bf16[1,512,768]{2,1,0:T(8,128)(2,1)S(1)}, bf16[1,512,768]{2,1,0:T(8,128)(2,1)}, u32[]{:S(2)}) copy-start(bf16[1,512,768]{2,1,0:T(8,128)(2,1)} %param.11) | copy-start | bytes 2359300
  0.7 19.9 %collective-permute-start = (bf16[512,768]{1,0:T(8,128)(2,1)}, bf16[512,768]{1,0:T(8,128)(2,1)S(1)}, u32[]{:S(2)}, u32[]{:S(2)}) collective-permute-start(bf16[512,768]{1,0:T(8,128)(2,1)} %bitcast.47), channel_id=1, source_target_pairs={{0,96},{32,0},{64,32},{96,64},{1,97},{33,1},{65,33},{97,65},{2,98}... | collective-permute-start | bytes 2359304 | tf_op jit(solution)/shard_map/ppermute | solution.py:31
  4.0 19.5 %collective-permute-start.1 = (bf16[512,768]{1,0:T(8,128)(2,1)}, bf16[512,768]{1,0:T(8,128)(2,1)S(1)}, u32[]{:S(2)}, u32[]{:S(2)}) collective-permute-start(bf16[512,768]{1,0:T(8,128)(2,1)} %bitcast.48), channel_id=1, source_target_pairs={{0,32},{32,64},{64,96},{96,0},{1,33},{33,65},{65,97},{97,1},{2,34}... | collective-permute-start | bytes 2359304 | tf_op jit(solution)/shard_map/ppermute | solution.py:31
  5.8 20.7 %all-to-all-start = ((bf16[16,32,768]{2,1,0:T(8,128)(2,1)}), bf16[16,32,768]{2,1,0:T(8,128)(2,1)S(1)}, u32[]{:S(2)}, u32[]{:S(2)}) async-start(bf16[16,32,768]{2,1,0:T(8,128)(2,1)} %broadcast_in_dim.39), calls=%async_computation | async-start | bytes 1572864 | tf_op jit(solution)/shard_map/all_to_all | solution.py:43
  20.6 3.0 %copy-start.6 = (bf16[512,768]{1,0:T(8,128)(2,1)}, bf16[512,768]{1,0:T(8,128)(2,1)S(1)}, u32[]{:S(2)}) copy-start(bf16[512,768]{1,0:T(8,128)(2,1)S(1)} %collective-permute-done.ahead_ref.refs_1_) | copy-start | bytes 2359300
  23.5 0.9 copy-start.7
  26.4 3.3 %copy-start.17 = (bf16[256,768]{1,0:T(8,128)(2,1)S(1)}, bf16[256,768]{1,0:T(8,128)(2,1)}, u32[]{:S(2)}) copy-start(bf16[256,768]{1,0:T(8,128)(2,1)} %get-tuple-element.29.refs_1_) | copy-start | bytes 1179652
  26.4 5.9 %copy-start.23 = (bf16[256,768]{1,0:T(8,128)(2,1)S(1)}, bf16[256,768]{1,0:T(8,128)(2,1)}, u32[]{:S(2)}) copy-start(bf16[256,768]{1,0:T(8,128)(2,1)} %get-tuple-element.30) | copy-start | bytes 1179652
  26.5 0.9 copy-start.3
  27.3 5.0 %collective-permute-start.2 = (bf16[16,32,768]{2,1,0:T(8,128)(2,1)}, bf16[16,32,768]{2,1,0:T(8,128)(2,1)S(1)}, u32[]{:S(2)}, u32[]{:S(2)}) collective-permute-start(bf16[16,32,768]{2,1,0:T(8,128)(2,1)} %shard_map.102), channel_id=1, source_target_pairs={{0,1},{1,0},{2,3},{3,2},{4,5},{5,4},{6,7},{7,6},{8,9},{9,8},{10,11... | collective-permute-start | bytes 2359304 | tf_op jit(solution)/shard_map/ppermute | solution.py:26
  29.7 14.4 %collective-permute-start.7 = (bf16[256,768]{1,0:T(8,128)(2,1)S(1)}, bf16[256,768]{1,0:T(8,128)(2,1)S(1)}, u32[]{:S(2)}, u32[]{:S(2)}) collective-permute-start(bf16[256,768]{1,0:T(8,128)(2,1)S(1)} %copy-done.17), channel_id=1, source_target_pairs={{0,96},{32,0},{64,32},{96,64},{1,97},{33,1},{65,33},{97,65},{2,98}... | collective-permute-start | bytes 1179656 | tf_op jit(solution)/shard_map/ppermute | solution.py:31
  32.4 11.7 %collective-permute-start.6 = (bf16[256,768]{1,0:T(8,128)(2,1)S(1)}, bf16[256,768]{1,0:T(8,128)(2,1)S(1)}, u32[]{:S(2)}, u32[]{:S(2)}) collective-permute-start(bf16[256,768]{1,0:T(8,128)(2,1)S(1)} %copy-done.23), channel_id=1, source_target_pairs={{0,32},{32,64},{64,96},{96,0},{1,33},{33,65},{65,97},{97,1},{2,34}... | collective-permute-start | bytes 1179656 | tf_op jit(solution)/shard_map/ppermute | solution.py:31
  34.1 1.1 copy-start.2
  34.7 12.4 %copy-start.1 = (bf16[4,256,768]{2,1,0:T(8,128)(2,1)}, bf16[4,256,768]{2,1,0:T(8,128)(2,1)S(1)}, u32[]{:S(2)}) copy-start(bf16[4,256,768]{2,1,0:T(8,128)(2,1)S(1)} %fusion) | copy-start | bytes 4718596
  36.7 7.4 %copy-start.18 = (f32[2,4,128]{2,1,0:T(4,128)}, f32[2,4,128]{2,1,0:T(4,128)S(1)}, u32[]{:S(2)}) copy-start(f32[2,4,128]{2,1,0:T(4,128)S(1)} %pad_maximum_fusion.2.refs_3_) | copy-start | bytes 12292
  36.7 9.7 %collective-permute-start.5 = (f32[2,4,128]{2,1,0:T(4,128)S(1)}, f32[2,4,128]{2,1,0:T(4,128)S(1)}, u32[]{:S(2)}, u32[]{:S(2)}) collective-permute-start(f32[2,4,128]{2,1,0:T(4,128)S(1)} %pad_maximum_fusion.2.refs_3_), channel_id=1, source_target_pairs={{0,32},{32,64},{64,96},{96,0},{1,33},{33,65},{65,97},{97,1},{2,34}... | collective-permute-start | bytes 12296 | tf_op jit(solution)/shard_map/ppermute | solution.py:31
  36.8 11.1 %collective-permute-start.4 = (f32[2,4,128]{2,1,0:T(4,128)S(1)}, f32[2,4,128]{2,1,0:T(4,128)S(1)}, u32[]{:S(2)}, u32[]{:S(2)}) collective-permute-start(f32[2,4,128]{2,1,0:T(4,128)S(1)} %pad_maximum_fusion.2.refs_3_), channel_id=1, source_target_pairs={{0,64},{32,96},{64,0},{96,32},{1,65},{33,97},{65,1},{97,33},{2,66}... | collective-permute-start | bytes 12296 | tf_op jit(solution)/shard_map/ppermute | solution.py:31
  40.6 7.3 %collective-permute-start.3 = (f32[2,4,128]{2,1,0:T(4,128)S(1)}, f32[2,4,128]{2,1,0:T(4,128)S(1)}, u32[]{:S(2)}, u32[]{:S(2)}) collective-permute-start(f32[2,4,128]{2,1,0:T(4,128)S(1)} %pad_maximum_fusion.2.refs_3_), channel_id=1, source_target_pairs={{0,96},{32,0},{64,32},{96,64},{1,97},{33,1},{65,33},{97,65},{2,98}... | collective-permute-start | bytes 12296 | tf_op jit(solution)/shard_map/ppermute | solution.py:31
  44.1 0.7 copy-start.5
  44.9 0.8 copy-start.4
  45.6 35.4 %collective-permute-start.8 = (bf16[512,768]{1,0:T(8,128)(2,1)}, bf16[512,768]{1,0:T(8,128)(2,1)S(1)}, u32[]{:S(2)}, u32[]{:S(2)}) collective-permute-start(bf16[512,768]{1,0:T(8,128)(2,1)} %shard_map.106.refs_0_.grad_ref), channel_id=1, source_target_pairs={{0,96},{32,0},{64,32},{96,64},{1,97},{33,1},{65,33},{97,65},{2,98}... | collective-permute-start | bytes 2359304 | tf_op jit(solution)/shard_map/ppermute | solution.py:31
  45.6 35.4 %collective-permute-start.9 = (bf16[512,768]{1,0:T(8,128)(2,1)}, bf16[512,768]{1,0:T(8,128)(2,1)S(1)}, u32[]{:S(2)}, u32[]{:S(2)}) collective-permute-start(bf16[512,768]{1,0:T(8,128)(2,1)} %shard_map.106.refs_0_.grad_ref), channel_id=1, source_target_pairs={{0,64},{32,96},{64,0},{96,32},{1,65},{33,97},{65,1},{97,33},{2,66}... | collective-permute-start | bytes 2359304 | tf_op jit(solution)/shard_map/ppermute | solution.py:31
  46.4 37.2 %collective-permute-start.10 = (bf16[512,768]{1,0:T(8,128)(2,1)}, bf16[512,768]{1,0:T(8,128)(2,1)S(1)}, u32[]{:S(2)}, u32[]{:S(2)}) collective-permute-start(bf16[512,768]{1,0:T(8,128)(2,1)} %shard_map.106.refs_0_.grad_ref), channel_id=1, source_target_pairs={{0,32},{32,64},{64,96},{96,0},{1,33},{33,65},{65,97},{97,1},{2,34}... | collective-permute-start | bytes 2359304 | tf_op jit(solution)/shard_map/ppermute | solution.py:31
  81.0 2.6 %copy-start.8 = (bf16[512,768]{1,0:T(8,128)(2,1)}, bf16[512,768]{1,0:T(8,128)(2,1)S(1)}, u32[]{:S(2)}) copy-start(bf16[512,768]{1,0:T(8,128)(2,1)S(1)} %collective-permute-done.8.refs_1_) | copy-start | bytes 2359300
  81.0 2.6 %copy-start.9 = (bf16[512,768]{1,0:T(8,128)(2,1)}, bf16[512,768]{1,0:T(8,128)(2,1)S(1)}, u32[]{:S(2)}) copy-start(bf16[512,768]{1,0:T(8,128)(2,1)S(1)} %collective-permute-done.9.refs_2_) | copy-start | bytes 2359300
  83.6 0.9 copy-start.10
  88.7 20.2 %all-to-all-start.2 = ((bf16[32,8,1536]{2,1,0:T(8,128)(2,1)}), bf16[32,8,1536]{2,1,0:T(8,128)(2,1)S(1)}, u32[]{:S(2)}, u32[]{:S(2)}) async-start(bf16[32,8,1536]{2,1,0:T(8,128)(2,1)} %bitcast.59), calls=%async_computation.2 | async-start | bytes 1572864 | tf_op jit(solution)/shard_map/all_to_all | solution.py:43
  108.8 0.9 copy-start
  114.6 32.3 %collective-permute-start.11 = (bf16[272,768]{1,0:T(8,128)(2,1)}, bf16[272,768]{1,0:T(8,128)(2,1)S(1)}, u32[]{:S(2)}, u32[]{:S(2)}) collective-permute-start(bf16[272,768]{1,0:T(8,128)(2,1)} %get-tuple-element.36.refs_0_._), channel_id=1, source_target_pairs={{0,96},{32,0},{64,32},{96,64},{1,97},{33,1},{65,33},{97,65},{2,98}... | collective-permute-start | bytes 1253384 | tf_op jit(solution)/shard_map/ppermute | solution.py:31
  115.8 31.4 %collective-permute-start.12 = (bf16[272,768]{1,0:T(8,128)(2,1)}, bf16[272,768]{1,0:T(8,128)(2,1)S(1)}, u32[]{:S(2)}, u32[]{:S(2)}) collective-permute-start(bf16[272,768]{1,0:T(8,128)(2,1)} %get-tuple-element.36.refs_0_._), channel_id=1, source_target_pairs={{0,64},{32,96},{64,0},{96,32},{1,65},{33,97},{65,1},{97,33},{2,66}... | collective-permute-start | bytes 1253384 | tf_op jit(solution)/shard_map/ppermute | solution.py:31
  116.0 31.2 %collective-permute-start.13 = (bf16[272,768]{1,0:T(8,128)(2,1)}, bf16[272,768]{1,0:T(8,128)(2,1)S(1)}, u32[]{:S(2)}, u32[]{:S(2)}) collective-permute-start(bf16[272,768]{1,0:T(8,128)(2,1)} %get-tuple-element.36.refs_0_._), channel_id=1, source_target_pairs={{0,32},{32,64},{64,96},{96,0},{1,33},{33,65},{65,97},{97,1},{2,34}... | collective-permute-start | bytes 1253384 | tf_op jit(solution)/shard_map/ppermute | solution.py:31
  124.9 15.0 %all-to-all-start.3 = ((bf16[32,8,768]{2,1,0:T(8,128)(2,1)}), bf16[32,8,768]{2,1,0:T(8,128)(2,1)S(1)}, u32[]{:S(2)}, u32[]{:S(2)}) async-start(bf16[32,8,768]{2,1,0:T(8,128)(2,1)} %bitcast.62), calls=%async_computation.3 | async-start | bytes 786432 | tf_op jit(solution)/shard_map/all_to_all | solution.py:43
  139.9 0.7 copy-start.12
  143.2 23.1 %collective-permute-start.14 = (bf16[272,768]{1,0:T(8,128)(2,1)}, bf16[272,768]{1,0:T(8,128)(2,1)S(1)}, u32[]{:S(2)}, u32[]{:S(2)}) collective-permute-start(bf16[272,768]{1,0:T(8,128)(2,1)} %get-tuple-element.47.refs_4_.grad_ref), channel_id=1, source_target_pairs={{0,96},{32,0},{64,32},{96,64},{1,97},{33,1},{65,33},{97,65},{2,98}... | collective-permute-start | bytes 1253384 | tf_op jit(solution)/shard_map/ppermute | solution.py:31
  145.3 20.9 %collective-permute-start.15 = (bf16[272,768]{1,0:T(8,128)(2,1)}, bf16[272,768]{1,0:T(8,128)(2,1)S(1)}, u32[]{:S(2)}, u32[]{:S(2)}) collective-permute-start(bf16[272,768]{1,0:T(8,128)(2,1)} %get-tuple-element.47.refs_4_.grad_ref), channel_id=1, source_target_pairs={{0,64},{32,96},{64,0},{96,32},{1,65},{33,97},{65,1},{97,33},{2,66}... | collective-permute-start | bytes 1253384 | tf_op jit(solution)/shard_map/ppermute | solution.py:31
  146.9 0.8 copy-start.14
  146.9 20.7 %collective-permute-start.16 = (bf16[272,768]{1,0:T(8,128)(2,1)}, bf16[272,768]{1,0:T(8,128)(2,1)S(1)}, u32[]{:S(2)}, u32[]{:S(2)}) collective-permute-start(bf16[272,768]{1,0:T(8,128)(2,1)} %get-tuple-element.47.refs_4_.grad_ref), channel_id=1, source_target_pairs={{0,32},{32,64},{64,96},{96,0},{1,33},{33,65},{65,97},{97,1},{2,34}... | collective-permute-start | bytes 1253384 | tf_op jit(solution)/shard_map/ppermute | solution.py:31
  147.2 0.7 copy-start.15
  147.9 0.8 copy-start.16
  156.5 19.3 %all-to-all-start.4 = ((bf16[32,8,768]{2,1,0:T(8,128)(2,1)}), bf16[32,8,768]{2,1,0:T(8,128)(2,1)S(1)}, u32[]{:S(2)}, u32[]{:S(2)}) async-start(bf16[32,8,768]{2,1,0:T(8,128)(2,1)} %bitcast.60), calls=%async_computation.4 | async-start | bytes 786432 | tf_op jit(solution)/shard_map/all_to_all | solution.py:43
  166.2 1.3 copy-start.20
  166.3 1.3 copy-start.21
  167.6 0.7 copy-start.22
  175.8 0.8 copy-start.11
